TPU v7x, 32 devices: a whole 2x2x4 slice. The times are simulated.
32 devices in a mesh: prow: 8 (over z, x), pcol: 4 (over y, core).
Axes of the slice: x: 2, y: 2, z: 4, core: 2. Of those that a mesh axis runs over, the one named last changes fastest.
Arguments:
- kernel_tiles: float32 [4, 8, 256, 8, 4, 256], P(None, 'prow', None, None, 'pcol'), may hold values from 0 to 11, as said below
Outputs:
- factored: float32 [4, 8, 256, 8, 4, 256], P(None, 'prow', None, None, 'pcol')
Inputs may be any that keep to these rules, and one draw needn't show every extreme that they name: kernel_tiles is a symmetric positive definite matrix in the stated layout: a product of two exponential covariances of locations and times, scaled per point, plus a diagonal term of at least 0.5.
All inputs are finite; a program needn't handle non-finite values.
Results may differ from a plain program's by a relative error of at most 0.000061.
Values sent between devices are 32-bit elements; how exact they have to be, the bound alone decides.
No kernel may reach another device: no remote copies, remote signals or barrier semaphores. Data moves between devices by JAX's collectives and lax.ppermute only.
A program may use at most 128 MiB of HBM per device.

v0:
```python
import functools

import jax
import jax.numpy as jnp
from jax import lax
from jax.experimental import pallas as pl
from jax.experimental.pallas import tpu as pltpu
from jax.sharding import PartitionSpec as P

HI = lax.Precision.HIGHEST
F32 = jnp.float32
BF16 = jnp.bfloat16
LANES = 128
VMEM_BYTES = 56 * 1024 * 1024


def splat(x, shape):
    return jnp.broadcast_to(x, shape)


def reciprocal(x):
    r = pl.reciprocal(x, approx=True)
    for _ in range(2):
        r = r * (2.0 - x * r)
    return r


def inverse_factor_128(block):
    size = 128
    step = 8
    count = size // step
    lane = lax.broadcasted_iota(jnp.int32, (step, size), 1)
    sub = lax.broadcasted_iota(jnp.int32, (step, size), 0)
    rows = [block[step * i : step * (i + 1), :] for i in range(count)]
    shape = (step, size)
    for j in range(count):
        base = step * j
        cols = [splat(rows[j][:, base + t : base + t + 1], shape) for t in range(step)]
        a = {}
        for t in range(step):
            for s in range(t, step):
                a[s, t] = splat(cols[t][s : s + 1, :], shape)
        in_block = (lane >= base) & (lane < base + step)
        unit = jnp.where(lane - base == sub, F32(1.0), F32(0.0))
        own = jnp.where(in_block, unit, rows[j])
        if j + 1 < count:
            below = [splat(rows[j + 1][:, base + t : base + t + 1], shape) for t in range(step)]
            near = jnp.where(in_block, F32(0.0), rows[j + 1])
        m = {}
        u = []
        w = []
        done = jnp.zeros(shape, F32)
        for t in range(0, step, 2):
            p, b, c = a[t, t], a[t + 1, t], a[t + 1, t + 1]
            det = p * c - b * b
            inv = reciprocal(det)
            for s in range(t + 2, step):
                m[s, t] = (c * a[s, t] - b * a[s, t + 1]) * inv
                m[s, t + 1] = (p * a[s, t + 1] - b * a[s, t]) * inv
            for v in range(t + 2, step):
                for s in range(v, step):
                    a[s, v] = a[s, v] - (m[s, t] * a[v, t] + m[s, t + 1] * a[v, t + 1])
            for k in (t, t + 1):
                row = splat(own[k : k + 1, :], shape)
                for s in range(t):
                    row = row - m[k, s] * u[s]
                u.append(row)
            w.append((c * u[t] - b * u[t + 1]) * inv)
            w.append((p * u[t + 1] - b * u[t]) * inv)
            root = lax.rsqrt(p)
            over = root * root
            done = jnp.where(sub == t, u[t] * root, done)
            done = jnp.where(sub == t + 1, (u[t + 1] - (b * over) * u[t]) * lax.rsqrt(det * over), done)
            if j + 1 < count:
                for k in (t, t + 1):
                    for s in range(t):
                        below[k] = below[k] - m[k, s] * below[s]
                near = near - (below[t] * w[t] + below[t + 1] * w[t + 1])
        if j + 1 < count:
            rows[j + 1] = near
        g = [None] * step
        for t in reversed(range(0, step, 2)):
            for k in (t + 1, t):
                row = w[k]
                for s in reversed(range(t + 2, step)):
                    row = row - m[s, k] * g[s]
                g[k] = row
        for i in range(j + 2, count):
            acc = jnp.where(in_block, F32(0.0), rows[i])
            for t in reversed(range(step)):
                acc = acc - splat(rows[i][:, base + t : base + t + 1], shape) * g[t]
            rows[i] = acc
        rows[j] = jnp.where(lane < base + step, done, F32(0.0))
    return jnp.concatenate(rows, axis=0)


def eliminate(state, first, last):
    rows = state.shape[0]
    for o in range(first, last):
        lo, hi = o * LANES, (o + 1) * LANES
        diag = inverse_factor_128(state[lo:hi, lo:hi])
        upper = jnp.dot(diag, state[lo:hi, :], precision=HI, preferred_element_type=F32)
        parts = ([upper[:, :lo]] if lo else []) + [diag] + ([upper[:, hi:]] if hi < rows else [])
        wide = jnp.concatenate(parts, axis=1)
        if hi < rows:
            state[hi:, lo:hi] = jnp.zeros((rows - hi, LANES), F32)
            state[hi:, :] -= lax.dot_general(
                upper[:, hi:], wide, (((0,), (0,)), ((), ())), precision=HI, preferred_element_type=F32
            )
            state[lo:hi, hi:] = jnp.zeros((LANES, rows - hi), F32)
        state[lo:hi, :hi] = wide[:, :hi]


def corner_start_kernel(place_ref, mine_ref, other_ref, state):
    core, side, across = place_ref[0], place_ref[1], place_ref[2]
    rows = state.shape[0]
    tile = rows // 2
    half = tile // 2
    per = tile // LANES
    for which, ref in ((core, mine_ref), (1 - core, other_ref)):
        for target in range(2):

            @pl.when(which == target)
            def _(ref=ref, target=target):
                for part in range(4):
                    at_side = side if part % 2 == 0 else 1 - side
                    at_half = across if part < 2 else 1 - across
                    at = pl.multiple_of(at_side * tile + at_half * half, half)
                    for h in range(per):
                        start = target * tile + h * LANES
                        state[pl.ds(at, half), start : start + LANES] = ref[
                            pl.ds(part * half * per + h, half, stride=per), :
                        ]

    eliminate(state, 0, tile // LANES)


def corner_end_kernel(state_ref, inverse_ref):
    rows = state_ref.shape[0]
    inverse_ref[...] = state_ref[...]
    eliminate(inverse_ref, rows // 2 // LANES, rows // LANES)


CORNER_COST = pl.CostEstimate(flops=1000, bytes_accessed=1000, transcendentals=0)


def corner_start(place, mine, other):
    width = mine.shape[0] // 2
    vmem = pl.BlockSpec(memory_space=pltpu.VMEM)
    return pl.pallas_call(
        corner_start_kernel,
        out_shape=jax.ShapeDtypeStruct((width, width), F32),
        in_specs=[pl.BlockSpec(memory_space=pltpu.SMEM), vmem, vmem],
        out_specs=vmem,
        compiler_params=pltpu.CompilerParams(vmem_limit_bytes=16 * 1024 * 1024),
        cost_estimate=CORNER_COST,
        name="corner_start",
    )(place, mine, other)


def corner_end(state):
    vmem = pl.BlockSpec(memory_space=pltpu.VMEM)
    return pl.pallas_call(
        corner_end_kernel,
        out_shape=jax.ShapeDtypeStruct(state.shape, F32),
        in_specs=[vmem],
        out_specs=vmem,
        compiler_params=pltpu.CompilerParams(vmem_limit_bytes=16 * 1024 * 1024),
        cost_estimate=CORNER_COST,
        name="corner_end",
    )(state)


def gather_kernel(row_tiles, col_tiles, tile, block_ref, across_ref, even_ref, odd_ref):
    step = pl.program_id(0)
    per = tile // LANES
    stride = col_tiles * per
    keep = row_tiles * per
    first = jnp.concatenate([block_ref[pl.ds(h, tile, stride=stride), :] for h in range(per)], axis=1).T
    for h in range(per):
        across_ref[pl.ds(step * per + h, tile, stride=keep), :] = first[:, h * LANES : (h + 1) * LANES]

    @pl.when(step == 0)
    def _():
        keep = col_tiles // 2 * per
        for parity, ref in enumerate((even_ref, odd_ref)):
            for i in range(col_tiles // 2):
                for h in range(per):
                    ref[pl.ds(i * per + h, tile, stride=keep), :] = block_ref[
                        pl.ds((2 * i + parity) * per + h, tile, stride=stride), :
                    ]


def gather_pieces(block, row_tiles, col_tiles, tile):
    per = tile // LANES
    shapes = [tile * row_tiles * per] + [tile * (col_tiles // 2) * per] * 2
    return pl.pallas_call(
        functools.partial(gather_kernel, row_tiles, col_tiles, tile),
        grid=(row_tiles,),
        out_shape=[jax.ShapeDtypeStruct((s, LANES), F32) for s in shapes],
        in_specs=[pl.BlockSpec((tile * col_tiles * per, LANES), lambda a: (a, 0))],
        out_specs=[pl.BlockSpec((s, LANES), lambda a: (0, 0)) for s in shapes],
        compiler_params=pltpu.CompilerParams(vmem_limit_bytes=VMEM_BYTES),
        cost_estimate=pl.CostEstimate(flops=1000, bytes_accessed=1000, transcendentals=0),
        name="gather_pieces",
    )(block)


def halves(x):
    high = x.astype(BF16)
    return high, (x - high.astype(F32)).astype(BF16)


def product(a, b, dims):
    (a_high, a_low), (b_high, b_low) = a, b
    dot = functools.partial(lax.dot_general, dimension_numbers=(dims, ((), ())), preferred_element_type=F32)
    return dot(a_high, b_high) + (dot(a_low, b_high) + dot(a_high, b_low))


def load_columns(place_ref, pieces, raw, col_high, col_low, sems, tile, count):
    per = tile // LANES
    for panel in range(2):
        for which, ref in enumerate(pieces):

            @pl.when(place_ref[3 + panel] == which)
            def _(panel=panel, ref=ref):
                pltpu.make_async_copy(ref, raw.at[panel], sems.at[panel]).start()

    for panel in range(2):
        pltpu.make_async_copy(pieces[0], raw.at[panel], sems.at[panel]).wait()
        for i in range(count):
            for h in range(per):
                high, low = halves(raw[panel, pl.ds(i * per + h, tile, stride=count * per), :])
                at = (i * per + h) * LANES
                col_high[panel * tile : (panel + 1) * tile, at : at + LANES] = high
                col_low[panel * tile : (panel + 1) * tile, at : at + LANES] = low


def subtract(place_ref, block_ref, out_ref, weights, col_high, col_low, tile, count):
    per = tile // LANES
    parity = place_ref[2]
    for i in range(count):
        at = i * tile
        update = product(weights, (col_high[:, at : at + tile], col_low[:, at : at + tile]), ((1,), (0,)))
        for h in range(per):
            where = pl.ds((2 * i + parity) * per + h, tile, stride=2 * count * per)
            out_ref[where, :] = block_ref[where, :] - update[:, h * LANES : (h + 1) * LANES]


def first_kernel(tile, row_tiles, count, place_ref, block_ref, rows_mine, rows_other, inverse_ref,
                 piece_a, piece_b, piece_c, out_ref, high_ref, low_ref, solved_ref, raw, col_high, col_low, sems,
                 inverse_high, inverse_low):
    step = pl.program_id(0)
    row, col, core = place_ref[0], place_ref[1], place_ref[5]
    per = tile // LANES

    @pl.when(step == 0)
    def _():
        inverse_high[...], inverse_low[...] = halves(inverse_ref[...])
        load_columns(place_ref, (piece_a, piece_b, piece_c), raw, col_high, col_low, sems, tile, count)

    out_ref[...] = block_ref[...]
    mine, other = [
        jnp.concatenate([r[pl.ds(step * per + h, tile, stride=row_tiles * per), :] for h in range(per)], axis=1)
        for r in (rows_mine, rows_other)
    ]
    lead = jnp.concatenate([jnp.where(core == 0, mine, other), jnp.where(core == 0, other, mine)], axis=0)
    inverse = (inverse_high[...], inverse_low[...])
    solved = product(halves(lead.T), inverse, ((1,), (1,)))
    weights = halves(product(halves(solved), inverse, ((1,), (0,))))
    high_ref[...], low_ref[...] = weights
    subtract(place_ref, block_ref, out_ref, weights, col_high, col_low, tile, count)

    @pl.when(col < 2)
    def _():
        mine = jnp.where(col == 0, solved[:, :tile], solved[:, tile:])
        r = lax.broadcasted_iota(jnp.int32, (tile, tile), 0)
        s = lax.broadcasted_iota(jnp.int32, (tile, tile), 1)
        top = (step == 0) & (row < 2)
        on_diag = top & (row == col)
        above = top & (row < col)
        keep = jnp.where(on_diag, s - r, jnp.where(above, 1, 0)) <= 0
        solved_ref[...] = jnp.where(keep, mine, F32(0.0))


def second_kernel(tile, row_tiles, count, place_ref, block_ref, high_ref, low_ref, solved_ref, piece_a, piece_b,
                  piece_c, out_ref, raw, col_high, col_low, sems):
    step = pl.program_id(0)
    row, col = place_ref[0], place_ref[1]
    per = tile // LANES
    top = (step == 0) & (row < 2)

    @pl.when(step == 0)
    def _():
        load_columns(place_ref, (piece_a, piece_b, piece_c), raw, col_high, col_low, sems, tile, count)

    @pl.when(top)
    def _():
        out_ref[...] = jnp.zeros_like(out_ref)

    @pl.when(jnp.logical_not(top))
    def _():
        out_ref[...] = block_ref[...]
        subtract(place_ref, block_ref, out_ref, (high_ref[...], low_ref[...]), col_high, col_low, tile, count)

    @pl.when(col < 2)
    def _():
        for h in range(per):
            out_ref[pl.ds(h, tile, stride=2 * count * per), :] = solved_ref[:, h * LANES : (h + 1) * LANES]


def trailing(places, block, rows_mine, rows_other, inverse, pieces, row_tiles, col_tiles, tile):
    per = tile // LANES
    depth = inverse.shape[0]
    count = col_tiles // 2
    smem = pl.BlockSpec(memory_space=pltpu.SMEM)
    whole = pl.BlockSpec((depth, depth), lambda a: (0, 0))
    rows_spec = pl.BlockSpec(rows_mine.shape, lambda a: (0, 0))
    block_spec = pl.BlockSpec((tile * col_tiles * per, LANES), lambda a: (a, 0))
    weight_spec = pl.BlockSpec((tile, depth), lambda a: (a, 0))
    solved_spec = pl.BlockSpec((tile, tile), lambda a: (a, 0))
    anywhere = [pl.BlockSpec(memory_space=pl.ANY)] * 3
    scratch = [
        pltpu.VMEM((2, tile * count * per, LANES), F32),
        pltpu.VMEM((depth, count * tile), BF16),
        pltpu.VMEM((depth, count * tile), BF16),
        pltpu.SemaphoreType.DMA((2,)),
    ]
    total = row_tiles * tile
    params = pltpu.CompilerParams(vmem_limit_bytes=40 * 1024 * 1024)
    cost = pl.CostEstimate(flops=1000, bytes_accessed=1000, transcendentals=0)
    block, high, low, solved = pl.pallas_call(
        functools.partial(first_kernel, tile, row_tiles, count),
        grid=(row_tiles,),
        out_shape=[
            jax.ShapeDtypeStruct(block.shape, F32),
            jax.ShapeDtypeStruct((total, depth), BF16),
            jax.ShapeDtypeStruct((total, depth), BF16),
            jax.ShapeDtypeStruct((total, tile), F32),
        ],
        in_specs=[smem, block_spec, rows_spec, rows_spec, whole] + anywhere,
        out_specs=[block_spec, weight_spec, weight_spec, solved_spec],
        scratch_shapes=scratch + [pltpu.VMEM((depth, depth), BF16)] * 2,
        compiler_params=params,
        cost_estimate=cost,
        name="trailing_first",
    )(places[0], block, rows_mine, rows_other, inverse, *pieces[0])
    return pl.pallas_call(
        functools.partial(second_kernel, tile, row_tiles, count),
        grid=(row_tiles,),
        out_shape=jax.ShapeDtypeStruct(block.shape, F32),
        in_specs=[smem, block_spec, weight_spec, weight_spec, solved_spec] + anywhere,
        out_specs=block_spec,
        scratch_shapes=scratch,
        compiler_params=params,
        cost_estimate=cost,
        input_output_aliases={1: 0},
        name="trailing_second",
    )(places[1], block, high, low, solved, *pieces[1])


AXES = ("prow", "pcol")


def send(value, route):
    pairs = []
    for device in range(32):
        to = route(device // 8, device // 4 % 2, device // 2 % 2, device % 2)
        if to is not None:
            pairs.append((device, ((to[0] * 2 + to[1]) * 2 + to[2]) * 2 + to[3]))
    return lax.ppermute(value, AXES, pairs)


def far_stage(z, x, y, k):
    to = {(0, 0): 3, (2, 0): 1, (0, 1): 2}.get((z, y))
    return None if to is None else (to, x, y, k)


def near_stage(z, x, y, k):
    to = {(0, 0): 1, (2, 0): 3, (3, 0): 2, (0, 1): 1, (1, 1): 3, (3, 1): 2}.get((z, y))
    return None if to is None else (to, x, y, k)


def by_rows(stage, z, y):
    return z == 0 or (y == 1 and z == (2 if stage == 0 else 1))


def same_core(stage):
    def route(z, x, y, k):
        if by_rows(stage, z, y) or k == x:
            return (z, 1 - x, y, k)
        return (z, x, y, x)

    return route


def cross_core(stage):
    def route(z, x, y, k):
        if by_rows(stage, z, y) or k == x:
            return None
        return (z, 1 - x, y, x)

    return route


def shards(kernel_tiles):
    row_tiles, _, tile, col_tiles, _, _ = kernel_tiles.shape
    row = lax.axis_index("prow")
    col = lax.axis_index("pcol")
    z, x, y, core = row // 2, row % 2, col // 2, col % 2
    per = tile // LANES
    block = kernel_tiles.reshape(row_tiles * tile * col_tiles * per, LANES)

    lead = kernel_tiles[0, 0, :, 0, 0, :].reshape(tile * per, LANES)
    middle = tile * per // 2
    half = send(lead[middle:], lambda z, x, y, k: (z, x, 1, k) if z == 0 and y == 0 else None)
    across, even, odd = gather_pieces(block, row_tiles, col_tiles, tile)
    to_far = jnp.where(y == 0, across, even)
    half, across, to_far = lax.optimization_barrier((half, across, to_far))
    over = send(across, lambda z, x, y, k: (z, x, 1, k) if y == 0 else None)
    half = jnp.where(y == 0, lead[:middle], half)
    half = jnp.where(z == 2, send(half, lambda z, x, y, k: (2, x, y, k) if z == 0 else None), half)
    half, to_far = lax.optimization_barrier((half, to_far))
    half = jnp.where(z % 2 == 1, send(half, lambda z, x, y, k: (z + 1, x, y, k) if z % 2 == 0 else None), half)
    far = send(to_far, far_stage)
    beside = send(half, lambda z, x, y, k: (z, 1 - x, y, k))
    above = send(half, lambda z, x, y, k: (z, x, 1 - y, k))
    corner = send(half, lambda z, x, y, k: (z, 1 - x, 1 - y, k))
    mine = jnp.concatenate([half, beside, above, corner], axis=0)
    other = send(mine, lambda z, x, y, k: (z, x, y, 1 - k))
    state = corner_start(jnp.stack([core, x, y]).astype(jnp.int32), mine, other)

    state, far, over = lax.optimization_barrier((state, far, over))
    rows_mine = jnp.where(y == 0, across, over)
    first_held = jnp.where(z == 0, even, jnp.where(y == 0, jnp.where(z == 2, across, far), jnp.where(z == 2, far, over)))
    to_near = jnp.where(y == 0, jnp.where(z == 3, far, across), jnp.where(z == 0, odd, over))
    near = send(to_near, near_stage)
    first = [first_held, send(first_held, same_core(0)), send(first_held, cross_core(0))]
    rows_other = send(rows_mine, lambda z, x, y, k: (z, x, y, 1 - k))
    state, first_held, to_near = lax.optimization_barrier((state, first_held, to_near))
    inverse = corner_end(state)

    inverse, near = lax.optimization_barrier((inverse, near))
    last_held = jnp.where(z == 0, odd, near)
    inverse, last_held = lax.optimization_barrier((inverse, last_held))
    last = [last_held, send(last_held, same_core(1)), send(last_held, cross_core(1))]
    pieces = [first, last]

    places = []
    for stage in range(2):
        first_odd = jnp.where(y == 0, (z == 1) | (z == 2), z == 3).astype(jnp.int32)
        parity = jnp.where(z == 0, stage, first_odd if stage == 0 else 1 - first_odd)
        rowwise = (z == 0) | ((y == 1) & (z == 2 - stage))
        own = core == x
        zero = jnp.where(rowwise, jnp.where(x == 0, 0, 1), jnp.where(own, jnp.where(core == 0, 0, 1), jnp.where(core == 0, 1, 2)))
        one = jnp.where(rowwise, jnp.where(x == 0, 1, 0), jnp.where(own, jnp.where(core == 0, 1, 0), jnp.where(core == 0, 2, 1)))
        places.append(jnp.stack([row, col, parity, zero, one, core]).astype(jnp.int32))
    result = trailing(places, block, rows_mine, rows_other, inverse, pieces, row_tiles, col_tiles, tile)
    return result.reshape(kernel_tiles.shape)


def from_root(value, axis, root):
    mine = lax.axis_index(axis) == root
    return lax.psum(jnp.where(mine, value, jnp.zeros_like(value)), axis)


def shards_any(kernel_tiles):
    row_tiles, _, tile, col_tiles, _, _ = kernel_tiles.shape
    row = lax.axis_index("prow")
    col = lax.axis_index("pcol")
    per = tile // LANES
    block = kernel_tiles.reshape(row_tiles * tile * col_tiles * per, LANES)
    across, even, odd = gather_pieces(block, row_tiles, col_tiles, tile)
    rows = [from_root(across, "pcol", panel) for panel in range(2)]
    lead = kernel_tiles[0, 0, :, 0, 0, :].reshape(tile * per, LANES)
    middle = tile * per // 2
    columns = []
    for panel in range(2):
        tops = [from_root(from_root(lead, "pcol", panel), "prow", p) for p in range(2)]
        columns.append(jnp.concatenate([t[s : s + middle] for s in (0, middle) for t in tops], axis=0))
    inverse = corner_end(corner_start(jnp.zeros((3,), jnp.int32), columns[0], columns[1]))
    pieces = []
    places = []
    zero = jnp.zeros((), jnp.int32)
    for stage, part in enumerate((even, odd)):
        panels = [from_root(part, "prow", p) for p in range(2)]
        pieces.append(panels + [panels[0]])
        places.append(jnp.stack([row, col, zero + stage, zero, zero + 1, zero]).astype(jnp.int32))
    result = trailing(places, block, rows[0], rows[1], inverse, pieces, row_tiles, col_tiles, tile)
    return result.reshape(kernel_tiles.shape)


def solution(mesh):
    in_specs = (P(None, "prow", None, None, "pcol", None),)
    out_specs = P(None, "prow", None, None, "pcol", None)
    body = shards if (mesh.shape["prow"], mesh.shape["pcol"]) == (8, 4) else shards_any
    return jax.shard_map(body, mesh=mesh, in_specs=in_specs, out_specs=out_specs, check_vma=False)
```

profile of v0, /device:TPU:16, one launch (start us, length us, event | category | flops | bytes accessed | tf_op | source)
XLA Modules:
  0.0 133.9 jit_solution(8177994875102515856)
XLA Ops:
  0.0 1.2 fusion
  1.2 0.7 collective-permute-start
  1.9 6.8 %gather_pieces.1 = (f32[2048,128]{1,0:T(8,128)}, f32[2048,128]{1,0:T(8,128)}, f32[2048,128]{1,0:T(8,128)}) custom-call(f32[16384,128]{1,0:T(8,128)} %bitcast.15), custom_call_target="tpu_custom_call" | custom-call | flops 1000 | bytes 1000 | tf_op jit(solution)/shard_map/gather_pieces/pallas_call | solution.py:197
  8.6 2.3 %broadcast_select_fusion.2 = f32[2048,128]{1,0:T(8,128)} fusion(f32[2048,128]{1,0:T(8,128)} %get-tuple-element.27, f32[2048,128]{1,0:T(8,128)} %get-tuple-element.26, pred[]{:T(512)S(6)} %eq.25), kind=kLoop, calls=%fused_computation.5 | loop fusion | flops 262144 | bytes 3145729 | tf_op jit(solution)/shard_map/jit(_where)/select_n | solution.py:418
  11.0 0.0 collective-permute-done
  11.0 1.3 collective-permute-start.1
  12.3 6.7 %collective-permute-done.1 = f32[256,128]{1,0:T(8,128)S(1)} collective-permute-done((f32[256,128]{1,0:T(8,128)S(1)}, f32[256,128]{1,0:T(8,128)S(1)}, u32[]{:S(2)}, u32[]{:S(2)}) %collective-permute-start.1) | collective-permute-done | bytes 131104 | tf_op jit(solution)/shard_map/ppermute | solution.py:371
  19.0 1.3 collective-permute-start.2
  20.3 3.5 %collective-permute-start.8 = (f32[2048,128]{1,0:T(8,128)}, f32[2048,128]{1,0:T(8,128)S(1)}, u32[]{:S(2)}, u32[]{:S(2)}) collective-permute-start(f32[2048,128]{1,0:T(8,128)} %get-tuple-element.27), channel_id=1, source_target_pairs={{0,2},{1,3},{4,6},{5,7},{8,10},{9,11},{12,14},{13,15},{16,18},{17,... | collective-permute-start | bytes 3145736 | tf_op jit(solution)/shard_map/ppermute | solution.py:371
  23.8 2.3 %collective-permute-start.7 = (f32[2048,128]{1,0:T(8,128)}, f32[2048,128]{1,0:T(8,128)}, u32[]{:S(2)}, u32[]{:S(2)}) collective-permute-start(f32[2048,128]{1,0:T(8,128)} %broadcast_select_fusion.2), channel_id=1, source_target_pairs={{0,24},{1,25},{2,18},{3,19},{4,28},{5,29},{6,22},{7,23},{16,8},{17... | collective-permute-start | bytes 3145736 | tf_op jit(solution)/shard_map/ppermute | solution.py:371
  26.1 0.0 collective-permute-done.2
  26.1 0.1 collective-permute-start.5
  26.2 2.9 %collective-permute-start.4 = (f32[256,128]{1,0:T(8,128)S(1)}, f32[256,128]{1,0:T(8,128)S(1)}, u32[]{:S(2)}, u32[]{:S(2)}) collective-permute-start(f32[256,128]{1,0:T(8,128)S(1)} %broadcast_select_fusion.5), channel_id=1, source_target_pairs={{0,2},{1,3},{2,0},{3,1},{4,6},{5,7},{6,4},{7,5},{8,10},{9,11},{10,... | collective-permute-start | bytes 393224 | tf_op jit(solution)/shard_map/ppermute | solution.py:371
  29.2 0.5 collective-permute-start.3
  29.7 3.0 %collective-permute-done.5 = f32[256,128]{1,0:T(8,128)S(1)} collective-permute-done((f32[256,128]{1,0:T(8,128)S(1)}, f32[256,128]{1,0:T(8,128)S(1)}, u32[]{:S(2)}, u32[]{:S(2)}) %collective-permute-start.5) | collective-permute-done | bytes 131104 | tf_op jit(solution)/shard_map/ppermute | solution.py:371
  32.7 18.4 %collective-permute-done.4 = f32[256,128]{1,0:T(8,128)S(1)} collective-permute-done((f32[256,128]{1,0:T(8,128)S(1)}, f32[256,128]{1,0:T(8,128)S(1)}, u32[]{:S(2)}, u32[]{:S(2)}) %collective-permute-start.4) | collective-permute-done | bytes 131104 | tf_op jit(solution)/shard_map/ppermute | solution.py:371
  51.1 0.0 collective-permute-done.3
  51.2 0.1 collective-permute-start.6
  51.3 0.1 pad_add_fusion.place_ref
  51.4 1.8 %collective-permute-done.6.other_ref = f32[1024,128]{1,0:T(8,128)S(1)} collective-permute-done((f32[1024,128]{1,0:T(8,128)S(1)}, f32[1024,128]{1,0:T(8,128)S(1)}, u32[]{:S(2)}, u32[]{:S(2)}) %collective-permute-start.6) | collective-permute-done | bytes 524320 | tf_op jit(solution)/shard_map/ppermute | solution.py:371
  53.1 11.4 %corner_start.1.state_ref = f32[512,512]{1,0:T(8,128)S(1)} custom-call(s32[3]{0:T(128)S(1)} %pad_add_fusion.place_ref, f32[1024,128]{1,0:T(8,128)S(1)} %pad_maximum_fusion.mine_ref, f32[1024,128]{1,0:T(8,128)S(1)} %collective-permute-done.6.other_ref), custom_call_target="tpu_custom_call" | custom-call | flops 1000 | bytes 1000 | tf_op jit(solution)/shard_map/corner_start/pallas_call | solution.py:150
  64.6 0.0 collective-permute-done.8
  64.6 0.0 collective-permute-done.7
  64.6 1.9 %select_select_fusion = (f32[2048,128]{1,0:T(8,128)S(1)}, f32[2048,128]{1,0:T(8,128)S(1)}, f32[2048,128]{1,0:T(8,128)S(1)}) fusion(f32[2048,128]{1,0:T(8,128)} %get-tuple-element.35, f32[2048,128]{1,0:T(8,128)S(1)} %collective-permute-done.8, f32[2048,128]{1,0:T(8,128)} %collective-permute-done.7, f32[2048,128]{1,0:T(8,128)} %get-tuple-element.27, pred[]{:T(512)S(6)} %eq.28, ...), kind=kLoop, calls=%fused_computation | loop fusion | flops 2097152 | bytes 8388612 | tf_op jit(solution)/shard_map/jit(_where)/select_n | solution.py:436
  66.5 1.9 %collective-permute-start.10 = (f32[2048,128]{1,0:T(8,128)S(1)}, f32[2048,128]{1,0:T(8,128)S(1)}, u32[]{:S(2)}, u32[]{:S(2)}) collective-permute-start(f32[2048,128]{1,0:T(8,128)S(1)} %get-tuple-element.47), channel_id=1, source_target_pairs={{0,8},{1,9},{2,10},{3,11},{4,12},{5,13},{6,14},{7,15},{10,26},{11,... | collective-permute-start | bytes 3145736 | tf_op jit(solution)/shard_map/ppermute | solution.py:371
  68.4 1.6 %collective-permute-start.12 = (f32[2048,128]{1,0:T(8,128)S(1)}, f32[2048,128]{1,0:T(8,128)}, u32[]{:S(2)}, u32[]{:S(2)}) collective-permute-start(f32[2048,128]{1,0:T(8,128)S(1)} %get-tuple-element.48.piece_a), channel_id=1, source_target_pairs={{9,12},{11,14},{12,9},{14,11},{17,20},{20,17},{25,28},{27,30},{28,... | collective-permute-start | bytes 3145736 | tf_op jit(solution)/shard_map/ppermute | solution.py:371
  70.0 2.3 %collective-permute-start.11 = (f32[2048,128]{1,0:T(8,128)S(1)}, f32[2048,128]{1,0:T(8,128)}, u32[]{:S(2)}, u32[]{:S(2)}) collective-permute-start(f32[2048,128]{1,0:T(8,128)S(1)} %get-tuple-element.48.piece_a), channel_id=1, source_target_pairs={{0,4},{1,5},{2,6},{3,7},{4,0},{5,1},{6,2},{7,3},{8,12},{9,8},{10,1... | collective-permute-start | bytes 3145736 | tf_op jit(solution)/shard_map/ppermute | solution.py:371
  72.3 10.3 %corner_end.1.inverse_ref = f32[512,512]{1,0:T(8,128)S(1)} custom-call(f32[512,512]{1,0:T(8,128)S(1)} %corner_start.1.state_ref), custom_call_target="tpu_custom_call" | custom-call | flops 1000 | bytes 1000 | tf_op jit(solution)/shard_map/corner_end/pallas_call | solution.py:163
  82.6 0.1 collective-permute-start.9
  82.7 10.9 %collective-permute-done.10 = f32[2048,128]{1,0:T(8,128)S(1)} collective-permute-done((f32[2048,128]{1,0:T(8,128)S(1)}, f32[2048,128]{1,0:T(8,128)S(1)}, u32[]{:S(2)}, u32[]{:S(2)}) %collective-permute-start.10) | collective-permute-done | bytes 1048608 | tf_op jit(solution)/shard_map/ppermute | solution.py:371
  93.6 1.1 broadcast_select_fusion.piece_a
  94.7 1.7 %collective-permute-start.14 = (f32[2048,128]{1,0:T(8,128)}, f32[2048,128]{1,0:T(8,128)}, u32[]{:S(2)}, u32[]{:S(2)}) collective-permute-start(f32[2048,128]{1,0:T(8,128)} %broadcast_select_fusion.piece_a), channel_id=1, source_target_pairs={{9,12},{12,9},{17,20},{19,22},{20,17},{22,19},{25,28},{27,30},{28,... | collective-permute-start | bytes 3145736 | tf_op jit(solution)/shard_map/ppermute | solution.py:371
  96.3 2.0 %collective-permute-start.13 = (f32[2048,128]{1,0:T(8,128)}, f32[2048,128]{1,0:T(8,128)}, u32[]{:S(2)}, u32[]{:S(2)}) collective-permute-start(f32[2048,128]{1,0:T(8,128)} %broadcast_select_fusion.piece_a), channel_id=1, source_target_pairs={{0,4},{1,5},{2,6},{3,7},{4,0},{5,1},{6,2},{7,3},{8,12},{9,8},{10,1... | collective-permute-start | bytes 3145736 | tf_op jit(solution)/shard_map/ppermute | solution.py:371
  98.4 0.1 stack.56.place_ref
  98.4 0.1 stack.52.place_ref
  98.5 0.0 collective-permute-done.9.rows_other
  98.5 0.0 collective-permute-done.12.piece_c
  98.5 0.0 collective-permute-done.11.piece_b
  98.6 15.8 %trailing_first.1 = (f32[16384,128]{1,0:T(8,128)}, bf16[1024,512]{1,0:T(8,128)(2,1)S(1)}, bf16[1024,512]{1,0:T(8,128)(2,1)S(1)}, f32[1024,256]{1,0:T(8,128)S(1)}) custom-call(s32[6]{0:T(128)S(1)} %stack.56.place_ref, f32[16384,128]{1,0:T(8,128)} %bitcast.16, f32[2048,128]{1,0:T(8,128)S(1)} %get-tuple-element.49.rows_mine, ...), custom_call_target="tpu_custom_call" | custom-call | flops 1000 | bytes 1000 | tf_op jit(solution)/shard_map/trailing_first/pallas_call | solution.py:332
  114.4 0.0 collective-permute-done.14.piece_c
  114.4 6.9 %collective-permute-done.13.piece_b = f32[2048,128]{1,0:T(8,128)} collective-permute-done((f32[2048,128]{1,0:T(8,128)}, f32[2048,128]{1,0:T(8,128)}, u32[]{:S(2)}, u32[]{:S(2)}) %collective-permute-start.13) | collective-permute-done | bytes 1048608 | tf_op jit(solution)/shard_map/ppermute | solution.py:371
  121.3 12.4 %trailing_second.1 = f32[16384,128]{1,0:T(8,128)} custom-call(s32[6]{0:T(128)S(1)} %stack.52.place_ref, f32[16384,128]{1,0:T(8,128)} %get-tuple-element.40.block_ref, bf16[1024,512]{1,0:T(8,128)(2,1)S(1)} %get-tuple-element.41.high_ref, bf16[1024,512]{1,0:T(8,128)(2,1)S(1)} %get-tuple-element.42.low_ref, ...), custom_call_target="tpu_custom_call", output_to_operand_aliasing={{}: (1, {})} | custom-call | flops 1000 | bytes 1000 | tf_op jit(solution)/shard_map/trailing_second/pallas_call | solution.py:348
  (4 shorter events, 0.1 us)
Async XLA Ops:
  1.2 9.8 %collective-permute-start = (f32[256,128]{1,0:T(8,128)S(1)}, f32[256,128]{1,0:T(8,128)S(1)}, u32[]{:S(2)}, u32[]{:S(2)}) collective-permute-start(f32[256,128]{1,0:T(8,128)S(1)} %bitcast.18), channel_id=1, source_target_pairs={{0,2},{1,3},{4,6},{5,7}} | collective-permute-start | bytes 393224 | tf_op jit(solution)/shard_map/ppermute | solution.py:371
  11.0 8.0 %collective-permute-start.1 = (f32[256,128]{1,0:T(8,128)S(1)}, f32[256,128]{1,0:T(8,128)S(1)}, u32[]{:S(2)}, u32[]{:S(2)}) collective-permute-start(f32[256,128]{1,0:T(8,128)S(1)} %broadcast_select_fusion.3), channel_id=1, source_target_pairs={{0,16},{1,17},{2,18},{3,19},{4,20},{5,21},{6,22},{7,23}} | collective-permute-start | bytes 393224 | tf_op jit(solution)/shard_map/ppermute | solution.py:371
  19.0 7.1 %collective-permute-start.2 = (f32[256,128]{1,0:T(8,128)S(1)}, f32[256,128]{1,0:T(8,128)S(1)}, u32[]{:S(2)}, u32[]{:S(2)}) collective-permute-start(f32[256,128]{1,0:T(8,128)S(1)} %broadcast_select_fusion.4), channel_id=1, source_target_pairs={{0,8},{1,9},{2,10},{3,11},{4,12},{5,13},{6,14},{7,15},{16,24},{17,... | collective-permute-start | bytes 393224 | tf_op jit(solution)/shard_map/ppermute | solution.py:371
  20.3 44.2 %collective-permute-start.8 = (f32[2048,128]{1,0:T(8,128)}, f32[2048,128]{1,0:T(8,128)S(1)}, u32[]{:S(2)}, u32[]{:S(2)}) collective-permute-start(f32[2048,128]{1,0:T(8,128)} %get-tuple-element.27), channel_id=1, source_target_pairs={{0,2},{1,3},{4,6},{5,7},{8,10},{9,11},{12,14},{13,15},{16,18},{17,... | collective-permute-start | bytes 3145736 | tf_op jit(solution)/shard_map/ppermute | solution.py:371
  23.8 40.8 %collective-permute-start.7 = (f32[2048,128]{1,0:T(8,128)}, f32[2048,128]{1,0:T(8,128)}, u32[]{:S(2)}, u32[]{:S(2)}) collective-permute-start(f32[2048,128]{1,0:T(8,128)} %broadcast_select_fusion.2), channel_id=1, source_target_pairs={{0,24},{1,25},{2,18},{3,19},{4,28},{5,29},{6,22},{7,23},{16,8},{17... | collective-permute-start | bytes 3145736 | tf_op jit(solution)/shard_map/ppermute | solution.py:371
  26.1 6.6 %collective-permute-start.5 = (f32[256,128]{1,0:T(8,128)S(1)}, f32[256,128]{1,0:T(8,128)S(1)}, u32[]{:S(2)}, u32[]{:S(2)}) collective-permute-start(f32[256,128]{1,0:T(8,128)S(1)} %broadcast_select_fusion.5), channel_id=1, source_target_pairs={{0,6},{1,7},{2,4},{3,5},{4,2},{5,3},{6,0},{7,1},{8,14},{9,15},{10,... | collective-permute-start | bytes 393224 | tf_op jit(solution)/shard_map/ppermute | solution.py:371
  26.2 24.9 %collective-permute-start.4 = (f32[256,128]{1,0:T(8,128)S(1)}, f32[256,128]{1,0:T(8,128)S(1)}, u32[]{:S(2)}, u32[]{:S(2)}) collective-permute-start(f32[256,128]{1,0:T(8,128)S(1)} %broadcast_select_fusion.5), channel_id=1, source_target_pairs={{0,2},{1,3},{2,0},{3,1},{4,6},{5,7},{6,4},{7,5},{8,10},{9,11},{10,... | collective-permute-start | bytes 393224 | tf_op jit(solution)/shard_map/ppermute | solution.py:371
  29.2 22.0 %collective-permute-start.3 = (f32[256,128]{1,0:T(8,128)S(1)}, f32[256,128]{1,0:T(8,128)S(1)}, u32[]{:S(2)}, u32[]{:S(2)}) collective-permute-start(f32[256,128]{1,0:T(8,128)S(1)} %broadcast_select_fusion.5), channel_id=1, source_target_pairs={{0,4},{1,5},{2,6},{3,7},{4,0},{5,1},{6,2},{7,3},{8,12},{9,13},{10,... | collective-permute-start | bytes 393224 | tf_op jit(solution)/shard_map/ppermute | solution.py:371
  51.2 2.0 %collective-permute-start.6 = (f32[1024,128]{1,0:T(8,128)S(1)}, f32[1024,128]{1,0:T(8,128)S(1)}, u32[]{:S(2)}, u32[]{:S(2)}) collective-permute-start(f32[1024,128]{1,0:T(8,128)S(1)} %pad_maximum_fusion.mine_ref), channel_id=1, source_target_pairs={{0,1},{1,0},{2,3},{3,2},{4,5},{5,4},{6,7},{7,6},{8,9},{9,8},{10,11... | collective-permute-start | bytes 1572872 | tf_op jit(solution)/shard_map/ppermute | solution.py:371
  66.5 27.1 %collective-permute-start.10 = (f32[2048,128]{1,0:T(8,128)S(1)}, f32[2048,128]{1,0:T(8,128)S(1)}, u32[]{:S(2)}, u32[]{:S(2)}) collective-permute-start(f32[2048,128]{1,0:T(8,128)S(1)} %get-tuple-element.47), channel_id=1, source_target_pairs={{0,8},{1,9},{2,10},{3,11},{4,12},{5,13},{6,14},{7,15},{10,26},{11,... | collective-permute-start | bytes 3145736 | tf_op jit(solution)/shard_map/ppermute | solution.py:371
  68.4 30.1 %collective-permute-start.12 = (f32[2048,128]{1,0:T(8,128)S(1)}, f32[2048,128]{1,0:T(8,128)}, u32[]{:S(2)}, u32[]{:S(2)}) collective-permute-start(f32[2048,128]{1,0:T(8,128)S(1)} %get-tuple-element.48.piece_a), channel_id=1, source_target_pairs={{9,12},{11,14},{12,9},{14,11},{17,20},{20,17},{25,28},{27,30},{28,... | collective-permute-start | bytes 3145736 | tf_op jit(solution)/shard_map/ppermute | solution.py:371
  70.0 28.5 %collective-permute-start.11 = (f32[2048,128]{1,0:T(8,128)S(1)}, f32[2048,128]{1,0:T(8,128)}, u32[]{:S(2)}, u32[]{:S(2)}) collective-permute-start(f32[2048,128]{1,0:T(8,128)S(1)} %get-tuple-element.48.piece_a), channel_id=1, source_target_pairs={{0,4},{1,5},{2,6},{3,7},{4,0},{5,1},{6,2},{7,3},{8,12},{9,8},{10,1... | collective-permute-start | bytes 3145736 | tf_op jit(solution)/shard_map/ppermute | solution.py:371
  82.6 16.0 %collective-permute-start.9 = (f32[2048,128]{1,0:T(8,128)S(1)}, f32[2048,128]{1,0:T(8,128)}, u32[]{:S(2)}, u32[]{:S(2)}) collective-permute-start(f32[2048,128]{1,0:T(8,128)S(1)} %get-tuple-element.49.rows_mine), channel_id=1, source_target_pairs={{0,1},{1,0},{2,3},{3,2},{4,5},{5,4},{6,7},{7,6},{8,9},{9,8},{10,11... | collective-permute-start | bytes 3145736 | tf_op jit(solution)/shard_map/ppermute | solution.py:371
  94.7 19.7 %collective-permute-start.14 = (f32[2048,128]{1,0:T(8,128)}, f32[2048,128]{1,0:T(8,128)}, u32[]{:S(2)}, u32[]{:S(2)}) collective-permute-start(f32[2048,128]{1,0:T(8,128)} %broadcast_select_fusion.piece_a), channel_id=1, source_target_pairs={{9,12},{12,9},{17,20},{19,22},{20,17},{22,19},{25,28},{27,30},{28,... | collective-permute-start | bytes 3145736 | tf_op jit(solution)/shard_map/ppermute | solution.py:371
  96.3 25.0 %collective-permute-start.13 = (f32[2048,128]{1,0:T(8,128)}, f32[2048,128]{1,0:T(8,128)}, u32[]{:S(2)}, u32[]{:S(2)}) collective-permute-start(f32[2048,128]{1,0:T(8,128)} %broadcast_select_fusion.piece_a), channel_id=1, source_target_pairs={{0,4},{1,5},{2,6},{3,7},{4,0},{5,1},{6,2},{7,3},{8,12},{9,8},{10,1... | collective-permute-start | bytes 3145736 | tf_op jit(solution)/shard_map/ppermute | solution.py:371
where the time goes:
time: 136 us; the launch traced here: 134 us
  Pallas kernels  56.7 us (42%)
  waiting for transfers between devices  47.8 us (35%)
  starting transfers between devices  22.2 us (16%)
  other arithmetic  5.47 us (4%)
    ppermute x15, waiting for transfers between devices, send(): return lax.ppermute(value, AXES, pairs)  47.8 us
    ppermute x15, starting transfers between devices, send(): return lax.ppermute(value, AXES, pairs)  22.2 us
    pallas_call x1, Pallas kernels, trailing(): pl.pallas_call(functools.partial(first_kernel, tile, row_tiles, count), g...  15.8 us
    pallas_call x1, Pallas kernels, trailing(): pl.pallas_call(functools.partial(second_kernel, tile, row_tiles, count),...  12.4 us
    pallas_call x1, Pallas kernels, corner_start(): pl.pallas_call(corner_start_kernel, out_shape=jax.ShapeDtypeStruct((width...  11.4 us
    pallas_call x1, Pallas kernels, corner_end(): pl.pallas_call(corner_end_kernel, out_shape=jax.ShapeDtypeStruct(state.sh...  10.3 us
    pallas_call x1, Pallas kernels, gather_pieces(): pl.pallas_call(functools.partial(gather_kernel, row_tiles, col_tiles, til...  6.77 us
  transfers between devices with their start and end apart: 15, of which 6 were waited for; matrix products, arithmetic and copies ran while one was open for 3% of the time, Pallas kernels for 33%

commit v1 on v0

v1 whole, which is shorter than its diff:
```python
import functools

import jax
import jax.numpy as jnp
from jax import lax
from jax.experimental import pallas as pl
from jax.experimental.pallas import tpu as pltpu
from jax.sharding import PartitionSpec as P

HI = lax.Precision.HIGHEST
F32 = jnp.float32
BF16 = jnp.bfloat16
LANES = 128
VMEM_BYTES = 56 * 1024 * 1024


def splat(x, shape):
    return jnp.broadcast_to(x, shape)


def reciprocal(x):
    r = pl.reciprocal(x, approx=True)
    for _ in range(2):
        r = r * (2.0 - x * r)
    return r


def inverse_factor_128(block):
    size = 128
    step = 8
    count = size // step
    lane = lax.broadcasted_iota(jnp.int32, (step, size), 1)
    sub = lax.broadcasted_iota(jnp.int32, (step, size), 0)
    rows = [block[step * i : step * (i + 1), :] for i in range(count)]
    shape = (step, size)
    for j in range(count):
        base = step * j
        cols = [splat(rows[j][:, base + t : base + t + 1], shape) for t in range(step)]
        a = {}
        for t in range(step):
            for s in range(t, step):
                a[s, t] = splat(cols[t][s : s + 1, :], shape)
        in_block = (lane >= base) & (lane < base + step)
        unit = jnp.where(lane - base == sub, F32(1.0), F32(0.0))
        own = jnp.where(in_block, unit, rows[j])
        if j + 1 < count:
            below = [splat(rows[j + 1][:, base + t : base + t + 1], shape) for t in range(step)]
            near = jnp.where(in_block, F32(0.0), rows[j + 1])
        m = {}
        u = []
        w = []
        done = jnp.zeros(shape, F32)
        for t in range(0, step, 2):
            p, b, c = a[t, t], a[t + 1, t], a[t + 1, t + 1]
            det = p * c - b * b
            inv = reciprocal(det)
            for s in range(t + 2, step):
                m[s, t] = (c * a[s, t] - b * a[s, t + 1]) * inv
                m[s, t + 1] = (p * a[s, t + 1] - b * a[s, t]) * inv
            for v in range(t + 2, step):
                for s in range(v, step):
                    a[s, v] = a[s, v] - (m[s, t] * a[v, t] + m[s, t + 1] * a[v, t + 1])
            for k in (t, t + 1):
                row = splat(own[k : k + 1, :], shape)
                for s in range(t):
                    row = row - m[k, s] * u[s]
                u.append(row)
            w.append((c * u[t] - b * u[t + 1]) * inv)
            w.append((p * u[t + 1] - b * u[t]) * inv)
            root = lax.rsqrt(p)
            over = root * root
            done = jnp.where(sub == t, u[t] * root, done)
            done = jnp.where(sub == t + 1, (u[t + 1] - (b * over) * u[t]) * lax.rsqrt(det * over), done)
            if j + 1 < count:
                for k in (t, t + 1):
                    for s in range(t):
                        below[k] = below[k] - m[k, s] * below[s]
                near = near - (below[t] * w[t] + below[t + 1] * w[t + 1])
        if j + 1 < count:
            rows[j + 1] = near
        g = [None] * step
        for t in reversed(range(0, step, 2)):
            for k in (t + 1, t):
                row = w[k]
                for s in reversed(range(t + 2, step)):
                    row = row - m[s, k] * g[s]
                g[k] = row
        for i in range(j + 2, count):
            acc = jnp.where(in_block, F32(0.0), rows[i])
            for t in reversed(range(step)):
                acc = acc - splat(rows[i][:, base + t : base + t + 1], shape) * g[t]
            rows[i] = acc
        rows[j] = jnp.where(lane < base + step, done, F32(0.0))
    return jnp.concatenate(rows, axis=0)


def eliminate(state, first, last):
    rows = state.shape[0]
    for o in range(first, last):
        lo, hi = o * LANES, (o + 1) * LANES
        diag = inverse_factor_128(state[lo:hi, lo:hi])
        upper = jnp.dot(diag, state[lo:hi, :], precision=HI, preferred_element_type=F32)
        parts = ([upper[:, :lo]] if lo else []) + [diag] + ([upper[:, hi:]] if hi < rows else [])
        wide = jnp.concatenate(parts, axis=1)
        if hi < rows:
            state[hi:, lo:hi] = jnp.zeros((rows - hi, LANES), F32)
            state[hi:, :] -= lax.dot_general(
                upper[:, hi:], wide, (((0,), (0,)), ((), ())), precision=HI, preferred_element_type=F32
            )
            state[lo:hi, hi:] = jnp.zeros((LANES, rows - hi), F32)
        state[lo:hi, :hi] = wide[:, :hi]


def corner_start_kernel(place_ref, mine_ref, other_ref, state):
    core, side, across = place_ref[0], place_ref[1], place_ref[2]
    rows = state.shape[0]
    tile = rows // 2
    half = tile // 2
    per = tile // LANES
    for which, ref in ((core, mine_ref), (1 - core, other_ref)):
        for part in range(4):
            at_side = side if part % 2 == 0 else 1 - side
            at_half = across if part < 2 else 1 - across
            at = pl.multiple_of(which * tile + at_half * half, half)
            for target in range(2):

                @pl.when(at_side == target)
                def _(ref=ref, part=part, at=at, target=target):
                    for h in range(per):
                        start = target * tile + h * LANES
                        state[pl.ds(at, half), start : start + LANES] = ref[
                            pl.ds(part * half * per + h, half, stride=per), :
                        ]

    eliminate(state, 0, tile // LANES)


def corner_end_kernel(state_ref, inverse_ref):
    rows = state_ref.shape[0]
    inverse_ref[...] = state_ref[...]
    eliminate(inverse_ref, rows // 2 // LANES, rows // LANES)


COST = pl.CostEstimate(flops=1000, bytes_accessed=1000, transcendentals=0)


def corner_start(place, mine, other):
    width = mine.shape[0] // 2
    vmem = pl.BlockSpec(memory_space=pltpu.VMEM)
    return pl.pallas_call(
        corner_start_kernel,
        out_shape=jax.ShapeDtypeStruct((width, width), F32),
        in_specs=[pl.BlockSpec(memory_space=pltpu.SMEM), vmem, vmem],
        out_specs=vmem,
        compiler_params=pltpu.CompilerParams(vmem_limit_bytes=16 * 1024 * 1024),
        cost_estimate=COST,
        name="corner_start",
    )(place, mine, other)


def corner_end(state):
    vmem = pl.BlockSpec(memory_space=pltpu.VMEM)
    return pl.pallas_call(
        corner_end_kernel,
        out_shape=jax.ShapeDtypeStruct(state.shape, F32),
        in_specs=[vmem],
        out_specs=vmem,
        compiler_params=pltpu.CompilerParams(vmem_limit_bytes=16 * 1024 * 1024),
        cost_estimate=COST,
        name="corner_end",
    )(state)


def transposed_tile(block_ref, tile, stride):
    per = tile // LANES
    return jnp.concatenate([block_ref[pl.ds(h, tile, stride=stride), :] for h in range(per)], axis=1).T


def store_tile(ref, start, value, tile):
    per = tile // LANES
    for h in range(per):
        ref[pl.ds(start + h, tile, stride=per), :] = value[:, h * LANES : (h + 1) * LANES]


def lead_kernel(tile, block_ref, out_ref):
    store_tile(out_ref, 0, transposed_tile(block_ref.reshape(tile * GROUP, LANES), tile, GROUP), tile)


def gather_kernel(tile, col_tiles, row_tiles, place_ref, lead_ref, block_ref, top_ref, rest_ref, far_ref, even_ref,
                  odd_ref):
    step = pl.program_id(0)
    per = tile // LANES
    size = tile * per
    value = transposed_tile(block_ref.reshape(tile * GROUP, LANES), tile, GROUP)
    store_tile(rest_ref, 0, value, tile)

    @pl.when(place_ref[0] == 0)
    def _():
        store_tile(far_ref, pl.multiple_of((step + 1) * size, size), value, tile)

    @pl.when(step == 0)
    def _():
        for parity, ref in enumerate((even_ref, odd_ref)):
            for i in range(col_tiles // 2):
                for h in range(per):
                    ref[pl.ds(i * size + h, tile, stride=per), :] = top_ref[
                        pl.ds((2 * i + parity) * per + h, tile, stride=col_tiles * per), :
                    ]

        @pl.when(place_ref[0] == 0)
        def _():
            far_ref[:size, :] = lead_ref[...]

        @pl.when(place_ref[0] != 0)
        def _():
            far_ref[...] = even_ref[...]


GROUP = 8


def grouped(block, row_tiles, col_tiles, tile):
    return block.reshape(row_tiles * tile, col_tiles * tile // LANES // GROUP, GROUP, LANES)


def gather_lead(block, row_tiles, col_tiles, tile):
    return pl.pallas_call(
        functools.partial(lead_kernel, tile),
        grid=(1,),
        out_shape=jax.ShapeDtypeStruct((tile * tile // LANES, LANES), F32),
        in_specs=[pl.BlockSpec((tile, None, GROUP, LANES), lambda a: (0, 0, 0, 0))],
        out_specs=pl.BlockSpec((tile * tile // LANES, LANES), lambda a: (0, 0)),
        compiler_params=pltpu.CompilerParams(vmem_limit_bytes=VMEM_BYTES),
        cost_estimate=COST,
        name="gather_lead",
    )(grouped(block, row_tiles, col_tiles, tile))


def gather_pieces(place, lead, block, row_tiles, col_tiles, tile):
    per = tile // LANES
    size = tile * per
    top = (tile * col_tiles * per, LANES)
    whole = [size * row_tiles] + [size * (col_tiles // 2)] * 2
    return pl.pallas_call(
        functools.partial(gather_kernel, tile, col_tiles, row_tiles),
        grid=(row_tiles - 1,),
        out_shape=[jax.ShapeDtypeStruct((s, LANES), F32) for s in [size * (row_tiles - 1)] + whole],
        in_specs=[
            pl.BlockSpec(memory_space=pltpu.SMEM),
            pl.BlockSpec((size, LANES), lambda a: (0, 0)),
            pl.BlockSpec((tile, None, GROUP, LANES), lambda a: (a + 1, 0, 0, 0)),
            pl.BlockSpec(top, lambda a: (0, 0)),
        ],
        out_specs=[pl.BlockSpec((size, LANES), lambda a: (a, 0))]
        + [pl.BlockSpec((s, LANES), lambda a: (0, 0)) for s in whole],
        compiler_params=pltpu.CompilerParams(vmem_limit_bytes=VMEM_BYTES),
        cost_estimate=COST,
        name="gather_pieces",
    )(place, lead, grouped(block, row_tiles, col_tiles, tile), block)


def halves(x):
    high = x.astype(BF16)
    return high, (x - high.astype(F32)).astype(BF16)


def product(a, b, dims):
    (a_high, a_low), (b_high, b_low) = a, b
    dot = functools.partial(lax.dot_general, dimension_numbers=(dims, ((), ())), preferred_element_type=F32)
    return dot(a_high, b_high) + (dot(a_low, b_high) + dot(a_high, b_low))


def weights_kernel(tile, place_ref, rows_mine, rows_other, inverse_ref, high_ref, low_ref, solved_ref, inverse_high,
                   inverse_low):
    step = pl.program_id(0)
    row, col, core = place_ref[0], place_ref[1], place_ref[2]
    per = tile // LANES

    @pl.when(step == 0)
    def _():
        inverse_high[...], inverse_low[...] = halves(inverse_ref[...])

    mine, other = [
        jnp.concatenate([r[pl.ds(h, tile, stride=per), :] for h in range(per)], axis=1)
        for r in (rows_mine, rows_other)
    ]
    lead = jnp.concatenate([jnp.where(core == 0, mine, other).T, jnp.where(core == 0, other, mine).T], axis=1)
    inverse = (inverse_high[...], inverse_low[...])
    solved = product(halves(lead), inverse, ((1,), (1,)))
    high_ref[...], low_ref[...] = halves(product(halves(solved), inverse, ((1,), (0,))))

    @pl.when(col < 2)
    def _():
        mine = jnp.where(col == 0, solved[:, :tile], solved[:, tile:])
        r = lax.broadcasted_iota(jnp.int32, (tile, tile), 0)
        s = lax.broadcasted_iota(jnp.int32, (tile, tile), 1)
        top = (step == 0) & (row < 2)
        on_diag = top & (row == col)
        above = top & (row < col)
        keep = jnp.where(on_diag, s - r, jnp.where(above, 1, 0)) <= 0
        solved_ref[...] = jnp.where(keep, mine, F32(0.0))


def row_weights(place, rows_mine, rows_other, inverse, row_tiles, tile):
    depth = inverse.shape[0]
    rows_spec = pl.BlockSpec((tile * tile // LANES, LANES), lambda a: (a, 0))
    total = row_tiles * tile
    return pl.pallas_call(
        functools.partial(weights_kernel, tile),
        grid=(row_tiles,),
        out_shape=[jax.ShapeDtypeStruct((total, depth), BF16)] * 2 + [jax.ShapeDtypeStruct((total, tile), F32)],
        in_specs=[
            pl.BlockSpec(memory_space=pltpu.SMEM),
            rows_spec,
            rows_spec,
            pl.BlockSpec((depth, depth), lambda a: (0, 0)),
        ],
        out_specs=[pl.BlockSpec((tile, depth), lambda a: (a, 0))] * 2 + [pl.BlockSpec((tile, tile), lambda a: (a, 0))],
        scratch_shapes=[pltpu.VMEM((depth, depth), BF16)] * 2,
        compiler_params=pltpu.CompilerParams(vmem_limit_bytes=32 * 1024 * 1024),
        cost_estimate=COST,
        name="row_weights",
    )(place, rows_mine, rows_other, inverse)


def load_columns(place_ref, pieces, offsets, raw, col_high, col_low, sems, tile, count):
    per = tile // LANES
    size = count * tile * per
    for stage in range(2):
        for panel in range(2):
            for which, ref in enumerate(pieces[stage]):

                @pl.when(place_ref[3 + 2 * stage + panel] == which)
                def _(stage=stage, panel=panel, ref=ref):
                    pltpu.make_async_copy(
                        ref.at[pl.ds(offsets[stage], size), :], raw.at[stage, panel], sems.at[stage, panel]
                    ).start()

    for stage in range(2):
        for panel in range(2):
            pltpu.make_async_copy(
                pieces[stage][0].at[pl.ds(offsets[stage], size), :], raw.at[stage, panel], sems.at[stage, panel]
            ).wait()
            for i in range(count):
                for h in range(per):
                    high, low = halves(raw[stage, panel, pl.ds(i * tile * per + h, tile, stride=per), :])
                    at = ((stage * count + i) * per + h) * LANES
                    col_high[panel * tile : (panel + 1) * tile, at : at + LANES] = high
                    col_low[panel * tile : (panel + 1) * tile, at : at + LANES] = low


def trailing_kernel(tile, group, count, offsets, place_ref, block_ref, high_ref, low_ref, *rest):
    solved_ref = rest[0] if group == 0 else None
    pieces = (rest[1:4], rest[4:7])
    block_out, raw, col_high, col_low, sems = rest[-5:]
    step = pl.program_id(0)
    row, col = place_ref[0], place_ref[1]
    per = tile // LANES
    top = (step == 0) & (row < 2)
    block = block_ref.reshape(tile * GROUP, LANES)
    out = block_out.reshape(tile * GROUP, LANES)

    @pl.when(step == 0)
    def _():
        load_columns(place_ref, pieces, offsets, raw, col_high, col_low, sems, tile, count)

    @pl.when(top)
    def _():
        block_out[...] = jnp.zeros_like(block_out)

    @pl.when(jnp.logical_not(top))
    def _():
        weights = (high_ref[...], low_ref[...])
        for stage in range(2):
            parity = place_ref[2] if stage == 0 else 1 - place_ref[2]
            for i in range(count):
                at = (stage * count + i) * tile
                update = product(weights, (col_high[:, at : at + tile], col_low[:, at : at + tile]), ((1,), (0,)))
                for h in range(per):
                    where = pl.ds((2 * i + parity) * per + h, tile, stride=GROUP)
                    out[where, :] = block[where, :] - update[:, h * LANES : (h + 1) * LANES]

    if group == 0:

        @pl.when(col < 2)
        def _():
            for h in range(per):
                out[pl.ds(h, tile, stride=GROUP), :] = solved_ref[:, h * LANES : (h + 1) * LANES]


def trailing(group, place, block, weights, extra, pieces, offsets, row_tiles, col_tiles, tile):
    per = tile // LANES
    high, low = weights
    depth = high.shape[1]
    count = GROUP // per // 2
    view = grouped(block, row_tiles, col_tiles, tile)
    block_spec = pl.BlockSpec((tile, None, GROUP, LANES), lambda a: (a, group, 0, 0))
    weight_spec = pl.BlockSpec((tile, depth), lambda a: (a, 0))
    anywhere = pl.BlockSpec(memory_space=pl.ANY)
    return pl.pallas_call(
        functools.partial(trailing_kernel, tile, group, count, offsets),
        grid=(row_tiles,),
        out_shape=jax.ShapeDtypeStruct(view.shape, F32),
        in_specs=[pl.BlockSpec(memory_space=pltpu.SMEM), block_spec, weight_spec, weight_spec]
        + [pl.BlockSpec((tile, tile), lambda a: (a, 0)) if group == 0 else anywhere]
        + [anywhere] * 6,
        out_specs=block_spec,
        scratch_shapes=[
            pltpu.VMEM((2, 2, count * tile * per, LANES), F32),
            pltpu.VMEM((depth, 2 * count * tile), BF16),
            pltpu.VMEM((depth, 2 * count * tile), BF16),
            pltpu.SemaphoreType.DMA((2, 2)),
        ],
        input_output_aliases={} if group == 0 else {4: 0},
        compiler_params=pltpu.CompilerParams(vmem_limit_bytes=40 * 1024 * 1024),
        cost_estimate=COST,
        name="trailing_%d" % group,
    )(place, view, high, low, extra, *pieces[0], *pieces[1])


AXES = ("prow", "pcol")


def send(value, route):
    pairs = []
    for device in range(32):
        to = route(device // 8, device // 4 % 2, device // 2 % 2, device % 2)
        if to is not None:
            pairs.append((device, ((to[0] * 2 + to[1]) * 2 + to[2]) * 2 + to[3]))
    return lax.ppermute(value, AXES, pairs)


def far_stage(z, x, y, k):
    to = {(0, 0): 3, (2, 0): 1, (0, 1): 2}.get((z, y))
    return None if to is None else (to, x, y, k)


def near_stage(z, x, y, k):
    to = {(0, 0): 1, (2, 0): 3, (3, 0): 2, (0, 1): 1, (1, 1): 3, (3, 1): 2}.get((z, y))
    return None if to is None else (to, x, y, k)


def by_rows(stage, z, y):
    return z == 0 or (y == 1 and z == (2 if stage == 0 else 1))


def same_core(stage):
    def route(z, x, y, k):
        if by_rows(stage, z, y) or k == x:
            return (z, 1 - x, y, k)
        return (z, x, y, x)

    return route


def cross_core(stage):
    def route(z, x, y, k):
        if by_rows(stage, z, y) or k == x:
            return None
        return (z, 1 - x, y, x)

    return route


def shards(kernel_tiles):
    row_tiles, _, tile, col_tiles, _, _ = kernel_tiles.shape
    row = lax.axis_index("prow")
    col = lax.axis_index("pcol")
    z, x, y, core = row // 2, row % 2, col // 2, col % 2
    per = tile // LANES
    block = kernel_tiles.reshape(row_tiles * tile * col_tiles * per, LANES)

    lead = gather_lead(block, row_tiles, col_tiles, tile)
    middle = tile * per // 2
    over_first = send(lead, lambda z, x, y, k: (z, x, 1, k) if y == 0 else None)
    rest, to_far, even, odd = gather_pieces(y.reshape(1), lead, block, row_tiles, col_tiles, tile)
    over_first, rest, to_far = lax.optimization_barrier((over_first, rest, to_far))
    half = jnp.where(y == 0, lead[:middle], over_first[middle:])
    half = jnp.where(z == 2, send(half, lambda z, x, y, k: (2, x, y, k) if z == 0 else None), half)
    half, to_far = lax.optimization_barrier((half, to_far))
    half = jnp.where(z % 2 == 1, send(half, lambda z, x, y, k: (z + 1, x, y, k) if z % 2 == 0 else None), half)
    far = send(to_far, far_stage)
    beside = send(half, lambda z, x, y, k: (z, 1 - x, y, k))
    above = send(half, lambda z, x, y, k: (z, x, 1 - y, k))
    corner = send(half, lambda z, x, y, k: (z, 1 - x, 1 - y, k))
    mine = jnp.concatenate([half, beside, above, corner], axis=0)
    mine, rest = lax.optimization_barrier((mine, rest))
    over_rest = send(rest, lambda z, x, y, k: (z, x, 1, k) if y == 0 else None)
    other = send(mine, lambda z, x, y, k: (z, x, y, 1 - k))
    state = corner_start(jnp.stack([core, x, y]).astype(jnp.int32), mine, other)

    state, far, over_rest = lax.optimization_barrier((state, far, over_rest))
    over = jnp.concatenate([over_first, over_rest], axis=0)
    rows_mine = jnp.where(y == 0, to_far, over)
    first = jnp.where(z == 0, even, jnp.where(y == 0, jnp.where(z == 2, to_far, far), jnp.where(z == 2, far, over)))
    to_near = jnp.where(y == 0, jnp.where(z == 3, far, to_far), jnp.where(z == 0, odd, over))
    split = to_near.shape[0] // 2
    to_near = [to_near[:split], to_near[split:]]
    state, first, to_near = lax.optimization_barrier((state, first, to_near))
    near = [send(to_near[0], near_stage), send(to_near[1], near_stage)]
    first = [first, send(first, same_core(0)), send(first, cross_core(0))]
    rows_other = send(rows_mine, lambda z, x, y, k: (z, x, y, 1 - k))
    inverse = corner_end(state)

    last = []
    for part in range(2):
        inverse, near[part] = lax.optimization_barrier((inverse, near[part]))
        held = jnp.where(z == 0, odd[part * split : (part + 1) * split], near[part])
        inverse, held = lax.optimization_barrier((inverse, held))
        last.append([held, send(held, same_core(1)), send(held, cross_core(1))])
        if part == 0:
            place = jnp.stack([row, col, core]).astype(jnp.int32)
            high, low, solved = row_weights(place, rows_mine, rows_other, inverse, row_tiles, tile)

    first_odd = jnp.where(y == 0, (z == 1) | (z == 2), z == 3).astype(jnp.int32)
    chosen = []
    for stage in range(2):
        rowwise = (z == 0) | ((y == 1) & (z == 2 - stage))
        own = core == x
        for panel in range(2):
            by_row = jnp.where(x == panel, 0, 1)
            by_col = jnp.where(own, jnp.where(core == panel, 0, 1), jnp.where(core == panel, 1, 2))
            chosen.append(jnp.where(rowwise, by_row, by_col))
    place = jnp.stack([row, col, jnp.where(z == 0, 0, first_odd)] + chosen).astype(jnp.int32)
    result = solved
    for part in range(2):
        result = trailing(
            part, place, block, (high, low), result, (first, last[part]), (part * split, 0), row_tiles, col_tiles, tile
        )
    return result.reshape(kernel_tiles.shape)


def from_root(value, axis, root):
    mine = lax.axis_index(axis) == root
    return lax.psum(jnp.where(mine, value, jnp.zeros_like(value)), axis)


def shards_any(kernel_tiles):
    row_tiles, _, tile, col_tiles, _, _ = kernel_tiles.shape
    row = lax.axis_index("prow")
    col = lax.axis_index("pcol")
    per = tile // LANES
    block = kernel_tiles.reshape(row_tiles * tile * col_tiles * per, LANES)
    zero = jnp.zeros((), jnp.int32)
    lead = gather_lead(block, row_tiles, col_tiles, tile)
    _, across, even, odd = gather_pieces(zero.reshape(1), lead, block, row_tiles, col_tiles, tile)
    rows = [from_root(across, "pcol", panel) for panel in range(2)]
    middle = tile * per // 2
    tile_rows = []
    for panel in range(2):
        tiles = [from_root(from_root(lead, "pcol", panel), "prow", p) for p in range(2)]
        tile_rows.append(jnp.concatenate([t[s : s + middle] for s in (0, middle) for t in tiles], axis=0))
    inverse = corner_end(corner_start(jnp.zeros((3,), jnp.int32), tile_rows[0], tile_rows[1]))
    pieces = []
    for part in (even, odd):
        panels = [from_root(part, "prow", p) for p in range(2)]
        pieces.append(panels + [panels[0]])
    place = jnp.stack([row, col, zero, zero, zero + 1, zero, zero + 1]).astype(jnp.int32)
    high, low, result = row_weights(place, rows[0], rows[1], inverse, row_tiles, tile)
    split = even.shape[0] // 2
    for part in range(2):
        result = trailing(
            part, place, block, (high, low), result, pieces, (part * split,) * 2, row_tiles, col_tiles, tile
        )
    return result.reshape(kernel_tiles.shape)


def solution(mesh):
    in_specs = (P(None, "prow", None, None, "pcol", None),)
    out_specs = P(None, "prow", None, None, "pcol", None)
    body = shards if (mesh.shape["prow"], mesh.shape["pcol"]) == (8, 4) else shards_any
    return jax.shard_map(body, mesh=mesh, in_specs=in_specs, out_specs=out_specs, check_vma=False)
```

time: 136 us -> 138 us (1.015)
  starting transfers between devices: 22.2 us -> 28.7 us
  waiting for transfers between devices: 47.8 us -> 44.1 us
  local copies, waits for them, and re-layouts: 1.32 us -> 4.62 us
  Pallas kernels: 56.7 us -> 54.4 us
  other arithmetic: 5.47 us -> 3.48 us
    ppermute x15 -> x18, starting transfers between devices: 22.2 us -> 28.7 us  [send(): return lax.ppermute(value, AXES, pairs)]
    unnamed x0 -> x15, local copies, waits for them, and re-layouts: none -> 4.41 us
    ppermute x15 -> x18, waiting for transfers between devices: 47.8 us -> 44.1 us  [send(): return lax.ppermute(value, AXES, pairs)]
    pallas_call x3 -> x5, Pallas kernels: 35 us -> 32.7 us  [the longest x2 18.9 us: trailing(): pl.pallas_call(functools.partial(trailing_kernel, tile, group, count, off...]
    select_n x4, other arithmetic: 5.33 us -> 3.27 us  [the longest x2 1.7 us: shards(): held = jnp.where(z == 0, odd[part * split:(part + 1) * split], near[part])]
  transfers between devices with their start and end apart: 15 -> 18, of which waited for: 6 -> 8; matrix products, arithmetic and copies ran while one was open for 3% -> 1% of each run, Pallas kernels for 33% -> 32%
where the time goes in v1:
time: 138 us; the launch traced here: 136 us
  Pallas kernels  54.4 us (39%)
  waiting for transfers between devices  44.1 us (32%)
  starting transfers between devices  28.7 us (21%)
  local copies, waits for them, and re-layouts  4.62 us (3%)
  other arithmetic  3.48 us (3%)
    ppermute x18, waiting for transfers between devices, send(): return lax.ppermute(value, AXES, pairs)  44.1 us
    ppermute x18, starting transfers between devices, send(): return lax.ppermute(value, AXES, pairs)  28.7 us
    pallas_call x2, Pallas kernels, trailing(): pl.pallas_call(functools.partial(trailing_kernel, tile, group, count, off...  18.9 us
    pallas_call x1, Pallas kernels, corner_start(): pl.pallas_call(corner_start_kernel, out_shape=jax.ShapeDtypeStruct((width...  11.4 us
    pallas_call x1, Pallas kernels, corner_end(): pl.pallas_call(corner_end_kernel, out_shape=jax.ShapeDtypeStruct(state.sh...  10.3 us
    pallas_call x1, Pallas kernels, gather_pieces(): pl.pallas_call(functools.partial(gather_kernel, tile, col_tiles, row_tile...  6.42 us
    pallas_call x1, Pallas kernels, row_weights(): pl.pallas_call(functools.partial(weights_kernel, tile), grid=(row_tiles,)...  5.39 us
    unnamed x15, local copies, waits for them, and re-layouts  4.41 us
  transfers between devices with their start and end apart: 18, of which 8 were waited for; matrix products, arithmetic and copies ran while one was open for 1% of the time, Pallas kernels for 32%

profile of v1, /device:TPU:16, one launch (start us, length us, event | category | flops | bytes accessed | tf_op | source)
XLA Modules:
  0.0 135.8 jit_solution(17849319197815749179)
XLA Ops:
  0.0 2.1 %gather_lead.1.lead_ref = f32[512,128]{1,0:T(8,128)} custom-call(f32[1024,2,8,128]{3,2,1,0:T(8,128)} %bitcast.13), custom_call_target="tpu_custom_call" | custom-call | flops 1000 | bytes 1000 | tf_op jit(solution)/shard_map/gather_lead/pallas_call | solution.py:227
  2.1 3.4 %collective-permute-start = (f32[512,128]{1,0:T(8,128)}, f32[512,128]{1,0:T(8,128)S(1)}, u32[]{:S(2)}, u32[]{:S(2)}) collective-permute-start(f32[512,128]{1,0:T(8,128)} %gather_lead.1.lead_ref), channel_id=1, source_target_pairs={{0,2},{1,3},{4,6},{5,7},{8,10},{9,11},{12,14},{13,15},{16,18},{17,... | collective-permute-start | bytes 786440 | tf_op jit(solution)/shard_map/ppermute | solution.py:430
  5.5 6.4 %gather_pieces.1 = (f32[1536,128]{1,0:T(8,128)}, f32[2048,128]{1,0:T(8,128)}, f32[2048,128]{1,0:T(8,128)}, f32[2048,128]{1,0:T(8,128)}) custom-call(s32[1]{0:T(128)} %bitcast.9.place_ref, f32[512,128]{1,0:T(8,128)} %gather_lead.1.lead_ref, f32[1024,2,8,128]{3,2,1,0:T(8,128)} %bitcast.14, f32[16384,128]{1,0:T(8,128)} %bitcast.15), custom_call_target="tpu_custom_call" | custom-call | flops 1000 | bytes 1000 | tf_op jit(solution)/shard_map/gather_pieces/pallas_call | solution.py:244
  11.9 0.0 collective-permute-done
  12.0 1.3 collective-permute-start.1
  13.3 6.4 %collective-permute-done.1 = f32[256,128]{1,0:T(8,128)S(1)} collective-permute-done((f32[256,128]{1,0:T(8,128)S(1)}, f32[256,128]{1,0:T(8,128)S(1)}, u32[]{:S(2)}, u32[]{:S(2)}) %collective-permute-start.1) | collective-permute-done | bytes 131104 | tf_op jit(solution)/shard_map/ppermute | solution.py:430
  19.8 1.3 collective-permute-start.2
  21.1 1.4 collective-permute-start.7
  22.5 22.7 %collective-permute-done.2 = f32[256,128]{1,0:T(8,128)S(1)} collective-permute-done((f32[256,128]{1,0:T(8,128)S(1)}, f32[256,128]{1,0:T(8,128)S(1)}, u32[]{:S(2)}, u32[]{:S(2)}) %collective-permute-start.2) | collective-permute-done | bytes 131104 | tf_op jit(solution)/shard_map/ppermute | solution.py:430
  45.2 0.1 collective-permute-start.5
  45.3 2.9 %collective-permute-start.4 = (f32[256,128]{1,0:T(8,128)S(1)}, f32[256,128]{1,0:T(8,128)S(1)}, u32[]{:S(2)}, u32[]{:S(2)}) collective-permute-start(f32[256,128]{1,0:T(8,128)S(1)} %broadcast_select_fusion.1), channel_id=1, source_target_pairs={{0,2},{1,3},{2,0},{3,1},{4,6},{5,7},{6,4},{7,5},{8,10},{9,11},{10,... | collective-permute-start | bytes 393224 | tf_op jit(solution)/shard_map/ppermute | solution.py:430
  48.2 0.5 collective-permute-start.3
  48.7 2.5 %collective-permute-done.5 = f32[256,128]{1,0:T(8,128)S(1)} collective-permute-done((f32[256,128]{1,0:T(8,128)S(1)}, f32[256,128]{1,0:T(8,128)S(1)}, u32[]{:S(2)}, u32[]{:S(2)}) %collective-permute-start.5) | collective-permute-done | bytes 131104 | tf_op jit(solution)/shard_map/ppermute | solution.py:430
  51.2 1.3 collective-permute-done.4
  52.5 0.7 collective-permute-done.3
  53.2 2.0 %collective-permute-start.8 = (f32[1536,128]{1,0:T(8,128)}, f32[1536,128]{1,0:T(8,128)S(1)}, u32[]{:S(2)}, u32[]{:S(2)}) collective-permute-start(f32[1536,128]{1,0:T(8,128)} %get-tuple-element.39), channel_id=1, source_target_pairs={{0,2},{1,3},{4,6},{5,7},{8,10},{9,11},{12,14},{13,15},{16,18},{17,... | collective-permute-start | bytes 2359304 | tf_op jit(solution)/shard_map/ppermute | solution.py:430
  55.2 0.1 collective-permute-start.6
  55.3 0.1 pad_add_fusion.1.place_ref
  55.4 1.8 %collective-permute-done.6.other_ref = f32[1024,128]{1,0:T(8,128)S(1)} collective-permute-done((f32[1024,128]{1,0:T(8,128)S(1)}, f32[1024,128]{1,0:T(8,128)S(1)}, u32[]{:S(2)}, u32[]{:S(2)}) %collective-permute-start.6) | collective-permute-done | bytes 524320 | tf_op jit(solution)/shard_map/ppermute | solution.py:430
  57.1 11.4 %corner_start.1.state_ref = f32[512,512]{1,0:T(8,128)S(1)} custom-call(s32[3]{0:T(128)S(1)} %pad_add_fusion.1.place_ref, f32[1024,128]{1,0:T(8,128)S(1)} %pad_maximum_fusion.mine_ref, f32[1024,128]{1,0:T(8,128)S(1)} %collective-permute-done.6.other_ref), custom_call_target="tpu_custom_call" | custom-call | flops 1000 | bytes 1000 | tf_op jit(solution)/shard_map/corner_start/pallas_call | solution.py:150
  68.6 0.0 collective-permute-done.8
  68.6 0.1 constant_dynamic-update-slice_fusion
  68.7 1.5 %select_select_fusion = (f32[2048,128]{1,0:T(8,128)S(1)}, f32[2048,128]{1,0:T(8,128)S(1)}, f32[2048,128]{1,0:T(8,128)S(1)}) fusion(f32[2048,128]{1,0:T(8,128)} %get-tuple-element.44, f32[2048,128]{1,0:T(8,128)S(1)} %constant_dynamic-update-slice_fusion, f32[2048,128]{1,0:T(8,128)S(1)} %collective-permute-done.7, f32[2048,128]{1,0:T(8,128)} %get-tuple-element.35, ...), kind=kLoop, calls=%fused_computation | loop fusion | flops 2097152 | bytes 8388612 | tf_op jit(solution)/shard_map/jit(_where)/select_n | solution.py:496
  70.2 0.1 fusion
  70.3 4.4 %collective-permute-start.10 = (f32[1024,128]{1,0:T(8,128)S(1)}, f32[1024,128]{1,0:T(8,128)S(1)}, u32[]{:S(2)}, u32[]{:S(2)}) collective-permute-start(f32[1024,128]{1,0:T(8,128)S(1)} %get-tuple-element.46), channel_id=1, source_target_pairs={{0,8},{1,9},{2,10},{3,11},{4,12},{5,13},{6,14},{7,15},{10,26},{11,... | collective-permute-start | bytes 1572872 | tf_op jit(solution)/shard_map/ppermute | solution.py:430
  74.7 0.7 collective-permute-start.12
  75.4 2.8 %collective-permute-start.9 = (f32[2048,128]{1,0:T(8,128)S(1)}, f32[2048,128]{1,0:T(8,128)S(1)}, u32[]{:S(2)}, u32[]{:S(2)}) collective-permute-start(f32[2048,128]{1,0:T(8,128)S(1)} %get-tuple-element.59.rows_mine), channel_id=1, source_target_pairs={{0,1},{1,0},{2,3},{3,2},{4,5},{5,4},{6,7},{7,6},{8,9},{9,8},{10,11... | collective-permute-start | bytes 3145736 | tf_op jit(solution)/shard_map/ppermute | solution.py:430
  78.2 1.9 %collective-permute-start.15 = (f32[1024,128]{1,0:T(8,128)S(1)}, f32[1024,128]{1,0:T(8,128)S(1)}, u32[]{:S(2)}, u32[]{:S(2)}) collective-permute-start(f32[1024,128]{1,0:T(8,128)S(1)} %get-tuple-element.55), channel_id=1, source_target_pairs={{0,8},{1,9},{2,10},{3,11},{4,12},{5,13},{6,14},{7,15},{10,26},{11,... | collective-permute-start | bytes 1572872 | tf_op jit(solution)/shard_map/ppermute | solution.py:430
  80.1 0.5 collective-permute-start.11
  80.6 10.3 %corner_end.1.inverse_ref = f32[512,512]{1,0:T(8,128)S(1)} custom-call(f32[512,512]{1,0:T(8,128)S(1)} %corner_start.1.state_ref), custom_call_target="tpu_custom_call" | custom-call | flops 1000 | bytes 1000 | tf_op jit(solution)/shard_map/corner_end/pallas_call | solution.py:163
  90.9 0.8 slice_select_fusion.1.rest_4_
  91.7 1.5 %collective-permute-start.14 = (f32[1024,128]{1,0:T(8,128)}, f32[1024,128]{1,0:T(8,128)}, u32[]{:S(2)}, u32[]{:S(2)}) collective-permute-start(f32[1024,128]{1,0:T(8,128)} %slice_select_fusion.1.rest_4_), channel_id=1, source_target_pairs={{9,12},{12,9},{17,20},{19,22},{20,17},{22,19},{25,28},{27,30},{28,... | collective-permute-start | bytes 1572872 | tf_op jit(solution)/shard_map/ppermute | solution.py:430
  93.2 4.9 %collective-permute-done.15 = f32[1024,128]{1,0:T(8,128)S(1)} collective-permute-done((f32[1024,128]{1,0:T(8,128)S(1)}, f32[1024,128]{1,0:T(8,128)S(1)}, u32[]{:S(2)}, u32[]{:S(2)}) %collective-permute-start.15) | collective-permute-done | bytes 524320 | tf_op jit(solution)/shard_map/ppermute | solution.py:430
  98.1 1.5 %collective-permute-start.13 = (f32[1024,128]{1,0:T(8,128)}, f32[1024,128]{1,0:T(8,128)}, u32[]{:S(2)}, u32[]{:S(2)}) collective-permute-start(f32[1024,128]{1,0:T(8,128)} %slice_select_fusion.1.rest_4_), channel_id=1, source_target_pairs={{0,4},{1,5},{2,6},{3,7},{4,0},{5,1},{6,2},{7,3},{8,12},{9,8},{10,1... | collective-permute-start | bytes 1572872 | tf_op jit(solution)/shard_map/ppermute | solution.py:430
  99.5 0.9 slice_select_fusion.rest_4_
  100.4 1.0 copy-done
  101.4 1.5 %collective-permute-start.17 = (f32[1024,128]{1,0:T(8,128)}, f32[1024,128]{1,0:T(8,128)}, u32[]{:S(2)}, u32[]{:S(2)}) collective-permute-start(f32[1024,128]{1,0:T(8,128)} %slice_select_fusion.rest_4_), channel_id=1, source_target_pairs={{9,12},{12,9},{17,20},{19,22},{20,17},{22,19},{25,28},{27,30},{28,... | collective-permute-start | bytes 1572872 | tf_op jit(solution)/shard_map/ppermute | solution.py:430
  102.8 1.0 copy-done.3
  103.8 1.1 collective-permute-start.16
  105.0 0.1 pad_add_fusion.place_ref
  105.0 0.1 stack.47.place_ref
  105.1 1.2 copy-done.4
  106.3 5.4 %row_weights.1 = (bf16[1024,512]{1,0:T(8,128)(2,1)S(1)}, bf16[1024,512]{1,0:T(8,128)(2,1)S(1)}, f32[1024,256]{1,0:T(8,128)S(1)}) custom-call(s32[3]{0:T(128)S(1)} %pad_add_fusion.place_ref, f32[2048,128]{1,0:T(8,128)S(1)} %get-tuple-element.59.rows_mine, f32[2048,128]{1,0:T(8,128)S(1)} %copy-done.4, f32[512,512]{1,0:T(8,128)S(1)} %corner_end.1.inverse_ref), custom_call_target="tpu_custom_call" | custom-call | flops 1000 | bytes 1000 | tf_op jit(solution)/shard_map/row_weights/pallas_call | solution.py:308
  111.7 0.0 collective-permute-done.11.rest_2_
  111.8 3.8 %collective-permute-done.13.rest_5_ = f32[1024,128]{1,0:T(8,128)} collective-permute-done((f32[1024,128]{1,0:T(8,128)}, f32[1024,128]{1,0:T(8,128)}, u32[]{:S(2)}, u32[]{:S(2)}) %collective-permute-start.13) | collective-permute-done | bytes 524320 | tf_op jit(solution)/shard_map/ppermute | solution.py:430
  115.5 1.2 copy-done.1
  116.8 9.6 %trailing_0.1.rest_0_ = f32[1024,2,8,128]{3,2,1,0:T(8,128)} custom-call(s32[7]{0:T(128)S(1)} %stack.47.place_ref, f32[1024,2,8,128]{3,2,1,0:T(8,128)} %bitcast.16, bf16[1024,512]{1,0:T(8,128)(2,1)S(1)} %get-tuple-element.50.high_ref, bf16[1024,512]{1,0:T(8,128)(2,1)S(1)} %get-tuple-element.51.low_ref, f32[1024,256]{1,0:T(8,128)S(1)} %get-tuple-element.52.rest_0_, ...), custom_call_target="tpu_custom_call" | custom-call | flops 1000 | bytes 1000 | tf_op jit(solution)/shard_map/trailing_0/pallas_call | solution.py:400
  126.4 9.3 %trailing_1.1 = f32[1024,2,8,128]{3,2,1,0:T(8,128)} custom-call(s32[7]{0:T(128)S(1)} %stack.47.place_ref, f32[1024,2,8,128]{3,2,1,0:T(8,128)} %bitcast.17, bf16[1024,512]{1,0:T(8,128)(2,1)S(1)} %get-tuple-element.50.high_ref, bf16[1024,512]{1,0:T(8,128)(2,1)S(1)} %get-tuple-element.51.low_ref, ...), custom_call_target="tpu_custom_call", output_to_operand_aliasing={{}: (4, {})} | custom-call | flops 1000 | bytes 1000 | tf_op jit(solution)/shard_map/trailing_1/pallas_call | solution.py:400
  (22 shorter events, 0.1 us)
Async XLA Ops:
  2.1 9.9 %collective-permute-start = (f32[512,128]{1,0:T(8,128)}, f32[512,128]{1,0:T(8,128)S(1)}, u32[]{:S(2)}, u32[]{:S(2)}) collective-permute-start(f32[512,128]{1,0:T(8,128)} %gather_lead.1.lead_ref), channel_id=1, source_target_pairs={{0,2},{1,3},{4,6},{5,7},{8,10},{9,11},{12,14},{13,15},{16,18},{17,... | collective-permute-start | bytes 786440 | tf_op jit(solution)/shard_map/ppermute | solution.py:430
  5.5 6.4 %copy-start.6 = (f32[512,128]{1,0:T(8,128)S(1)}, f32[512,128]{1,0:T(8,128)}, u32[]{:S(2)}) copy-start(f32[512,128]{1,0:T(8,128)} %gather_lead.1.lead_ref) | copy-start | bytes 786436
  12.0 7.8 %collective-permute-start.1 = (f32[256,128]{1,0:T(8,128)S(1)}, f32[256,128]{1,0:T(8,128)S(1)}, u32[]{:S(2)}, u32[]{:S(2)}) collective-permute-start(f32[256,128]{1,0:T(8,128)S(1)} %slice_select_fusion.2), channel_id=1, source_target_pairs={{0,16},{1,17},{2,18},{3,19},{4,20},{5,21},{6,22},{7,23}} | collective-permute-start | bytes 393224 | tf_op jit(solution)/shard_map/ppermute | solution.py:430
  19.8 25.4 %collective-permute-start.2 = (f32[256,128]{1,0:T(8,128)S(1)}, f32[256,128]{1,0:T(8,128)S(1)}, u32[]{:S(2)}, u32[]{:S(2)}) collective-permute-start(f32[256,128]{1,0:T(8,128)S(1)} %broadcast_select_fusion.2), channel_id=1, source_target_pairs={{0,8},{1,9},{2,10},{3,11},{4,12},{5,13},{6,14},{7,15},{16,24},{17,... | collective-permute-start | bytes 393224 | tf_op jit(solution)/shard_map/ppermute | solution.py:430
  21.1 47.5 %collective-permute-start.7 = (f32[2048,128]{1,0:T(8,128)}, f32[2048,128]{1,0:T(8,128)S(1)}, u32[]{:S(2)}, u32[]{:S(2)}) collective-permute-start(f32[2048,128]{1,0:T(8,128)} %get-tuple-element.35), channel_id=1, source_target_pairs={{0,24},{1,25},{2,18},{3,19},{4,28},{5,29},{6,22},{7,23},{16,8},{17... | collective-permute-start | bytes 3145736 | tf_op jit(solution)/shard_map/ppermute | solution.py:430
  45.2 6.0 %collective-permute-start.5 = (f32[256,128]{1,0:T(8,128)S(1)}, f32[256,128]{1,0:T(8,128)S(1)}, u32[]{:S(2)}, u32[]{:S(2)}) collective-permute-start(f32[256,128]{1,0:T(8,128)S(1)} %broadcast_select_fusion.1), channel_id=1, source_target_pairs={{0,6},{1,7},{2,4},{3,5},{4,2},{5,3},{6,0},{7,1},{8,14},{9,15},{10,... | collective-permute-start | bytes 393224 | tf_op jit(solution)/shard_map/ppermute | solution.py:430
  45.3 7.3 %collective-permute-start.4 = (f32[256,128]{1,0:T(8,128)S(1)}, f32[256,128]{1,0:T(8,128)S(1)}, u32[]{:S(2)}, u32[]{:S(2)}) collective-permute-start(f32[256,128]{1,0:T(8,128)S(1)} %broadcast_select_fusion.1), channel_id=1, source_target_pairs={{0,2},{1,3},{2,0},{3,1},{4,6},{5,7},{6,4},{7,5},{8,10},{9,11},{10,... | collective-permute-start | bytes 393224 | tf_op jit(solution)/shard_map/ppermute | solution.py:430
  48.2 5.0 %collective-permute-start.3 = (f32[256,128]{1,0:T(8,128)S(1)}, f32[256,128]{1,0:T(8,128)S(1)}, u32[]{:S(2)}, u32[]{:S(2)}) collective-permute-start(f32[256,128]{1,0:T(8,128)S(1)} %broadcast_select_fusion.1), channel_id=1, source_target_pairs={{0,4},{1,5},{2,6},{3,7},{4,0},{5,1},{6,2},{7,3},{8,12},{9,13},{10,... | collective-permute-start | bytes 393224 | tf_op jit(solution)/shard_map/ppermute | solution.py:430
  53.2 15.4 %collective-permute-start.8 = (f32[1536,128]{1,0:T(8,128)}, f32[1536,128]{1,0:T(8,128)S(1)}, u32[]{:S(2)}, u32[]{:S(2)}) collective-permute-start(f32[1536,128]{1,0:T(8,128)} %get-tuple-element.39), channel_id=1, source_target_pairs={{0,2},{1,3},{4,6},{5,7},{8,10},{9,11},{12,14},{13,15},{16,18},{17,... | collective-permute-start | bytes 2359304 | tf_op jit(solution)/shard_map/ppermute | solution.py:430
  55.2 2.0 %collective-permute-start.6 = (f32[1024,128]{1,0:T(8,128)S(1)}, f32[1024,128]{1,0:T(8,128)S(1)}, u32[]{:S(2)}, u32[]{:S(2)}) collective-permute-start(f32[1024,128]{1,0:T(8,128)S(1)} %pad_maximum_fusion.mine_ref), channel_id=1, source_target_pairs={{0,1},{1,0},{2,3},{3,2},{4,5},{5,4},{6,7},{7,6},{8,9},{9,8},{10,11... | collective-permute-start | bytes 1572872 | tf_op jit(solution)/shard_map/ppermute | solution.py:430
  55.4 35.5 %copy-start.5 = (f32[2048,128]{1,0:T(8,128)S(1)}, f32[2048,128]{1,0:T(8,128)}, u32[]{:S(2)}) copy-start(f32[2048,128]{1,0:T(8,128)} %get-tuple-element.44) | copy-start | bytes 3145732
  70.3 20.6 %collective-permute-start.10 = (f32[1024,128]{1,0:T(8,128)S(1)}, f32[1024,128]{1,0:T(8,128)S(1)}, u32[]{:S(2)}, u32[]{:S(2)}) collective-permute-start(f32[1024,128]{1,0:T(8,128)S(1)} %get-tuple-element.46), channel_id=1, source_target_pairs={{0,8},{1,9},{2,10},{3,11},{4,12},{5,13},{6,14},{7,15},{10,26},{11,... | collective-permute-start | bytes 1572872 | tf_op jit(solution)/shard_map/ppermute | solution.py:430
  74.7 25.8 %collective-permute-start.12 = (f32[2048,128]{1,0:T(8,128)S(1)}, f32[2048,128]{1,0:T(8,128)S(1)}, u32[]{:S(2)}, u32[]{:S(2)}) collective-permute-start(f32[2048,128]{1,0:T(8,128)S(1)} %get-tuple-element.53.rest_1_), channel_id=1, source_target_pairs={{9,12},{11,14},{12,9},{14,11},{17,20},{20,17},{25,28},{27,30},{28,... | collective-permute-start | bytes 3145736 | tf_op jit(solution)/shard_map/ppermute | solution.py:430
  75.4 27.4 %collective-permute-start.9 = (f32[2048,128]{1,0:T(8,128)S(1)}, f32[2048,128]{1,0:T(8,128)S(1)}, u32[]{:S(2)}, u32[]{:S(2)}) collective-permute-start(f32[2048,128]{1,0:T(8,128)S(1)} %get-tuple-element.59.rows_mine), channel_id=1, source_target_pairs={{0,1},{1,0},{2,3},{3,2},{4,5},{5,4},{6,7},{7,6},{8,9},{9,8},{10,11... | collective-permute-start | bytes 3145736 | tf_op jit(solution)/shard_map/ppermute | solution.py:430
  78.2 19.9 %collective-permute-start.15 = (f32[1024,128]{1,0:T(8,128)S(1)}, f32[1024,128]{1,0:T(8,128)S(1)}, u32[]{:S(2)}, u32[]{:S(2)}) collective-permute-start(f32[1024,128]{1,0:T(8,128)S(1)} %get-tuple-element.55), channel_id=1, source_target_pairs={{0,8},{1,9},{2,10},{3,11},{4,12},{5,13},{6,14},{7,15},{10,26},{11,... | collective-permute-start | bytes 1572872 | tf_op jit(solution)/shard_map/ppermute | solution.py:430
  80.1 31.6 %collective-permute-start.11 = (f32[2048,128]{1,0:T(8,128)S(1)}, f32[2048,128]{1,0:T(8,128)}, u32[]{:S(2)}, u32[]{:S(2)}) collective-permute-start(f32[2048,128]{1,0:T(8,128)S(1)} %get-tuple-element.53.rest_1_), channel_id=1, source_target_pairs={{0,4},{1,5},{2,6},{3,7},{4,0},{5,1},{6,2},{7,3},{8,12},{9,8},{10,1... | collective-permute-start | bytes 3145736 | tf_op jit(solution)/shard_map/ppermute | solution.py:430
  91.7 20.0 %collective-permute-start.14 = (f32[1024,128]{1,0:T(8,128)}, f32[1024,128]{1,0:T(8,128)}, u32[]{:S(2)}, u32[]{:S(2)}) collective-permute-start(f32[1024,128]{1,0:T(8,128)} %slice_select_fusion.1.rest_4_), channel_id=1, source_target_pairs={{9,12},{12,9},{17,20},{19,22},{20,17},{22,19},{25,28},{27,30},{28,... | collective-permute-start | bytes 1572872 | tf_op jit(solution)/shard_map/ppermute | solution.py:430
  98.1 17.4 %collective-permute-start.13 = (f32[1024,128]{1,0:T(8,128)}, f32[1024,128]{1,0:T(8,128)}, u32[]{:S(2)}, u32[]{:S(2)}) collective-permute-start(f32[1024,128]{1,0:T(8,128)} %slice_select_fusion.1.rest_4_), channel_id=1, source_target_pairs={{0,4},{1,5},{2,6},{3,7},{4,0},{5,1},{6,2},{7,3},{8,12},{9,8},{10,1... | collective-permute-start | bytes 1572872 | tf_op jit(solution)/shard_map/ppermute | solution.py:430
  100.4 1.0 copy-start
  101.4 25.0 %collective-permute-start.17 = (f32[1024,128]{1,0:T(8,128)}, f32[1024,128]{1,0:T(8,128)}, u32[]{:S(2)}, u32[]{:S(2)}) collective-permute-start(f32[1024,128]{1,0:T(8,128)} %slice_select_fusion.rest_4_), channel_id=1, source_target_pairs={{9,12},{12,9},{17,20},{19,22},{20,17},{22,19},{25,28},{27,30},{28,... | collective-permute-start | bytes 1572872 | tf_op jit(solution)/shard_map/ppermute | solution.py:430
  102.8 1.0 copy-start.3
  103.8 22.5 %collective-permute-start.16 = (f32[1024,128]{1,0:T(8,128)}, f32[1024,128]{1,0:T(8,128)}, u32[]{:S(2)}, u32[]{:S(2)}) collective-permute-start(f32[1024,128]{1,0:T(8,128)} %slice_select_fusion.rest_4_), channel_id=1, source_target_pairs={{0,4},{1,5},{2,6},{3,7},{4,0},{5,1},{6,2},{7,3},{8,12},{9,8},{10,1... | collective-permute-start | bytes 1572872 | tf_op jit(solution)/shard_map/ppermute | solution.py:430
  105.1 1.2 copy-start.4
  115.5 1.2 copy-start.1
  116.8 9.6 %copy-start.2 = (f32[2048,128]{1,0:T(8,128)S(1)}, f32[2048,128]{1,0:T(8,128)}, u32[]{:S(2)}) copy-start(f32[2048,128]{1,0:T(8,128)} %copy-done) | copy-start | bytes 3145732

commit v2 on v1

--- a/solution.py
+++ b/solution.py
@@ -264,30 +264,37 @@
     return high, (x - high.astype(F32)).astype(BF16)
 
 
+def left_factor(x):
+    high, low = halves(x)
+    return jnp.concatenate([high, low, high], axis=1)
+
+
+def right_factor(x, axis):
+    high, low = halves(x)
+    return jnp.concatenate([high, high, low], axis=axis)
+
+
 def product(a, b, dims):
-    (a_high, a_low), (b_high, b_low) = a, b
-    dot = functools.partial(lax.dot_general, dimension_numbers=(dims, ((), ())), preferred_element_type=F32)
-    return dot(a_high, b_high) + (dot(a_low, b_high) + dot(a_high, b_low))
-
-
-def weights_kernel(tile, place_ref, rows_mine, rows_other, inverse_ref, high_ref, low_ref, solved_ref, inverse_high,
-                   inverse_low):
+    return lax.dot_general(a, b, (dims, ((), ())), preferred_element_type=F32)
+
+
+def weights_kernel(tile, place_ref, rows_mine, rows_other, inverse_ref, weights_ref, solved_ref, across, along):
     step = pl.program_id(0)
     row, col, core = place_ref[0], place_ref[1], place_ref[2]
     per = tile // LANES
 
     @pl.when(step == 0)
     def _():
-        inverse_high[...], inverse_low[...] = halves(inverse_ref[...])
+        across[...] = right_factor(inverse_ref[...], 1)
+        along[...] = right_factor(inverse_ref[...], 0)
 
     mine, other = [
         jnp.concatenate([r[pl.ds(h, tile, stride=per), :] for h in range(per)], axis=1)
         for r in (rows_mine, rows_other)
     ]
     lead = jnp.concatenate([jnp.where(core == 0, mine, other).T, jnp.where(core == 0, other, mine).T], axis=1)
-    inverse = (inverse_high[...], inverse_low[...])
-    solved = product(halves(lead), inverse, ((1,), (1,)))
-    high_ref[...], low_ref[...] = halves(product(halves(solved), inverse, ((1,), (0,))))
+    solved = product(left_factor(lead), across[...], ((1,), (1,)))
+    weights_ref[...] = left_factor(product(left_factor(solved), along[...], ((1,), (0,))))
 
     @pl.when(col < 2)
     def _():
@@ -308,51 +315,44 @@
     return pl.pallas_call(
         functools.partial(weights_kernel, tile),
         grid=(row_tiles,),
-        out_shape=[jax.ShapeDtypeStruct((total, depth), BF16)] * 2 + [jax.ShapeDtypeStruct((total, tile), F32)],
+        out_shape=[jax.ShapeDtypeStruct((total, 3 * depth), BF16), jax.ShapeDtypeStruct((total, tile), F32)],
         in_specs=[
             pl.BlockSpec(memory_space=pltpu.SMEM),
             rows_spec,
             rows_spec,
             pl.BlockSpec((depth, depth), lambda a: (0, 0)),
         ],
-        out_specs=[pl.BlockSpec((tile, depth), lambda a: (a, 0))] * 2 + [pl.BlockSpec((tile, tile), lambda a: (a, 0))],
-        scratch_shapes=[pltpu.VMEM((depth, depth), BF16)] * 2,
+        out_specs=[pl.BlockSpec((tile, 3 * depth), lambda a: (a, 0)), pl.BlockSpec((tile, tile), lambda a: (a, 0))],
+        scratch_shapes=[pltpu.VMEM((depth, 3 * depth), BF16), pltpu.VMEM((3 * depth, depth), BF16)],
         compiler_params=pltpu.CompilerParams(vmem_limit_bytes=32 * 1024 * 1024),
         cost_estimate=COST,
         name="row_weights",
     )(place, rows_mine, rows_other, inverse)
 
 
-def load_columns(place_ref, pieces, offsets, raw, col_high, col_low, sems, tile, count):
-    per = tile // LANES
-    size = count * tile * per
+def load_columns(place_ref, pieces, offsets, columns, tile, count):
+    per = tile // LANES
+    depth = 2 * tile
     for stage in range(2):
         for panel in range(2):
             for which, ref in enumerate(pieces[stage]):
 
                 @pl.when(place_ref[3 + 2 * stage + panel] == which)
                 def _(stage=stage, panel=panel, ref=ref):
-                    pltpu.make_async_copy(
-                        ref.at[pl.ds(offsets[stage], size), :], raw.at[stage, panel], sems.at[stage, panel]
-                    ).start()
-
-    for stage in range(2):
-        for panel in range(2):
-            pltpu.make_async_copy(
-                pieces[stage][0].at[pl.ds(offsets[stage], size), :], raw.at[stage, panel], sems.at[stage, panel]
-            ).wait()
-            for i in range(count):
-                for h in range(per):
-                    high, low = halves(raw[stage, panel, pl.ds(i * tile * per + h, tile, stride=per), :])
-                    at = ((stage * count + i) * per + h) * LANES
-                    col_high[panel * tile : (panel + 1) * tile, at : at + LANES] = high
-                    col_low[panel * tile : (panel + 1) * tile, at : at + LANES] = low
-
-
-def trailing_kernel(tile, group, count, offsets, place_ref, block_ref, high_ref, low_ref, *rest):
+                    for i in range(count):
+                        for h in range(per):
+                            start = offsets[stage] + i * tile * per + h
+                            high, low = halves(ref[pl.ds(start, tile, stride=per), :])
+                            at = ((stage * count + i) * per + h) * LANES
+                            for copy, value in enumerate((high, high, low)):
+                                row = copy * depth + panel * tile
+                                columns[row : row + tile, at : at + LANES] = value
+
+
+def trailing_kernel(tile, group, count, offsets, place_ref, block_ref, weights_ref, *rest):
     solved_ref = rest[0] if group == 0 else None
     pieces = (rest[1:4], rest[4:7])
-    block_out, raw, col_high, col_low, sems = rest[-5:]
+    block_out, columns = rest[-2:]
     step = pl.program_id(0)
     row, col = place_ref[0], place_ref[1]
     per = tile // LANES
@@ -362,7 +362,7 @@
 
     @pl.when(step == 0)
     def _():
-        load_columns(place_ref, pieces, offsets, raw, col_high, col_low, sems, tile, count)
+        load_columns(place_ref, pieces, offsets, columns, tile, count)
 
     @pl.when(top)
     def _():
@@ -370,12 +370,11 @@
 
     @pl.when(jnp.logical_not(top))
     def _():
-        weights = (high_ref[...], low_ref[...])
         for stage in range(2):
             parity = place_ref[2] if stage == 0 else 1 - place_ref[2]
             for i in range(count):
                 at = (stage * count + i) * tile
-                update = product(weights, (col_high[:, at : at + tile], col_low[:, at : at + tile]), ((1,), (0,)))
+                update = product(weights_ref[...], columns[:, at : at + tile], ((1,), (0,)))
                 for h in range(per):
                     where = pl.ds((2 * i + parity) * per + h, tile, stride=GROUP)
                     out[where, :] = block[where, :] - update[:, h * LANES : (h + 1) * LANES]
@@ -390,32 +389,25 @@
 
 def trailing(group, place, block, weights, extra, pieces, offsets, row_tiles, col_tiles, tile):
     per = tile // LANES
-    high, low = weights
-    depth = high.shape[1]
+    depth = weights.shape[1]
     count = GROUP // per // 2
     view = grouped(block, row_tiles, col_tiles, tile)
     block_spec = pl.BlockSpec((tile, None, GROUP, LANES), lambda a: (a, group, 0, 0))
     weight_spec = pl.BlockSpec((tile, depth), lambda a: (a, 0))
-    anywhere = pl.BlockSpec(memory_space=pl.ANY)
     return pl.pallas_call(
         functools.partial(trailing_kernel, tile, group, count, offsets),
         grid=(row_tiles,),
         out_shape=jax.ShapeDtypeStruct(view.shape, F32),
-        in_specs=[pl.BlockSpec(memory_space=pltpu.SMEM), block_spec, weight_spec, weight_spec]
-        + [pl.BlockSpec((tile, tile), lambda a: (a, 0)) if group == 0 else anywhere]
-        + [anywhere] * 6,
+        in_specs=[pl.BlockSpec(memory_space=pltpu.SMEM), block_spec, weight_spec]
+        + [pl.BlockSpec((tile, tile), lambda a: (a, 0)) if group == 0 else pl.BlockSpec(memory_space=pl.ANY)]
+        + [pl.BlockSpec(memory_space=pltpu.VMEM)] * 6,
         out_specs=block_spec,
-        scratch_shapes=[
-            pltpu.VMEM((2, 2, count * tile * per, LANES), F32),
-            pltpu.VMEM((depth, 2 * count * tile), BF16),
-            pltpu.VMEM((depth, 2 * count * tile), BF16),
-            pltpu.SemaphoreType.DMA((2, 2)),
-        ],
-        input_output_aliases={} if group == 0 else {4: 0},
-        compiler_params=pltpu.CompilerParams(vmem_limit_bytes=40 * 1024 * 1024),
+        scratch_shapes=[pltpu.VMEM((depth, 2 * count * tile), BF16)],
+        input_output_aliases={} if group == 0 else {3: 0},
+        compiler_params=pltpu.CompilerParams(vmem_limit_bytes=32 * 1024 * 1024),
         cost_estimate=COST,
         name="trailing_%d" % group,
-    )(place, view, high, low, extra, *pieces[0], *pieces[1])
+    )(place, view, weights, extra, *pieces[0], *pieces[1])
 
 
 AXES = ("prow", "pcol")
@@ -477,14 +469,14 @@
     over_first, rest, to_far = lax.optimization_barrier((over_first, rest, to_far))
     half = jnp.where(y == 0, lead[:middle], over_first[middle:])
     half = jnp.where(z == 2, send(half, lambda z, x, y, k: (2, x, y, k) if z == 0 else None), half)
+    half = jnp.where(z % 2 == 1, send(half, lambda z, x, y, k: (z + 1, x, y, k) if z % 2 == 0 else None), half)
     half, to_far = lax.optimization_barrier((half, to_far))
-    half = jnp.where(z % 2 == 1, send(half, lambda z, x, y, k: (z + 1, x, y, k) if z % 2 == 0 else None), half)
     far = send(to_far, far_stage)
     beside = send(half, lambda z, x, y, k: (z, 1 - x, y, k))
     above = send(half, lambda z, x, y, k: (z, x, 1 - y, k))
     corner = send(half, lambda z, x, y, k: (z, 1 - x, 1 - y, k))
+    corner, rest = lax.optimization_barrier((corner, rest))
     mine = jnp.concatenate([half, beside, above, corner], axis=0)
-    mine, rest = lax.optimization_barrier((mine, rest))
     over_rest = send(rest, lambda z, x, y, k: (z, x, 1, k) if y == 0 else None)
     other = send(mine, lambda z, x, y, k: (z, x, y, 1 - k))
     state = corner_start(jnp.stack([core, x, y]).astype(jnp.int32), mine, other)
@@ -504,13 +496,14 @@
 
     last = []
     for part in range(2):
-        inverse, near[part] = lax.optimization_barrier((inverse, near[part]))
         held = jnp.where(z == 0, odd[part * split : (part + 1) * split], near[part])
-        inverse, held = lax.optimization_barrier((inverse, held))
+        if part == 0:
+            inverse, held = lax.optimization_barrier((inverse, held))
         last.append([held, send(held, same_core(1)), send(held, cross_core(1))])
         if part == 0:
             place = jnp.stack([row, col, core]).astype(jnp.int32)
-            high, low, solved = row_weights(place, rows_mine, rows_other, inverse, row_tiles, tile)
+            weights, solved = row_weights(place, rows_mine, rows_other, inverse, row_tiles, tile)
+            weights, near[1] = lax.optimization_barrier((weights, near[1]))
 
     first_odd = jnp.where(y == 0, (z == 1) | (z == 2), z == 3).astype(jnp.int32)
     chosen = []
@@ -525,7 +518,7 @@
     result = solved
     for part in range(2):
         result = trailing(
-            part, place, block, (high, low), result, (first, last[part]), (part * split, 0), row_tiles, col_tiles, tile
+            part, place, block, weights, result, (first, last[part]), (part * split, 0), row_tiles, col_tiles, tile
         )
     return result.reshape(kernel_tiles.shape)
 
@@ -556,11 +549,11 @@
         panels = [from_root(part, "prow", p) for p in range(2)]
         pieces.append(panels + [panels[0]])
     place = jnp.stack([row, col, zero, zero, zero + 1, zero, zero + 1]).astype(jnp.int32)
-    high, low, result = row_weights(place, rows[0], rows[1], inverse, row_tiles, tile)
+    weights, result = row_weights(place, rows[0], rows[1], inverse, row_tiles, tile)
     split = even.shape[0] // 2
     for part in range(2):
         result = trailing(
-            part, place, block, (high, low), result, pieces, (part * split,) * 2, row_tiles, col_tiles, tile
+            part, place, block, weights, result, pieces, (part * split,) * 2, row_tiles, col_tiles, tile
         )
     return result.reshape(kernel_tiles.shape)
 

time: 138 us -> 123 us (0.89)
  waiting for transfers between devices: 44.1 us -> 14.1 us
  starting transfers between devices: 28.7 us -> 40.8 us
  local copies, waits for them, and re-layouts: 4.62 us -> 7.7 us
    ppermute x18, waiting for transfers between devices: 44.1 us -> 14.1 us  [send(): return lax.ppermute(value, AXES, pairs)]
    ppermute x18, starting transfers between devices: 28.7 us -> 40.8 us  [send(): return lax.ppermute(value, AXES, pairs)]
    unnamed x15 -> x18, local copies, waits for them, and re-layouts: 4.41 us -> 7.48 us
  transfers between devices with their start and end apart: 18 -> 18, of which waited for: 8 -> 5; matrix products, arithmetic and copies ran while one was open for 1% -> 2% of each run, Pallas kernels for 32% -> 35%
where the time goes in v2:
time: 123 us; the launch traced here: 122 us
  Pallas kernels  54.7 us (44%)
  starting transfers between devices  40.8 us (33%)
  waiting for transfers between devices  14.1 us (11%)
  local copies, waits for them, and re-layouts  7.7 us (6%)
  other arithmetic  4.48 us (4%)
    ppermute x18, starting transfers between devices, send(): return lax.ppermute(value, AXES, pairs)  40.8 us
    pallas_call x2, Pallas kernels, trailing(): pl.pallas_call(functools.partial(trailing_kernel, tile, group, count, off...  19 us
    ppermute x18, waiting for transfers between devices, send(): return lax.ppermute(value, AXES, pairs)  14.1 us
    pallas_call x1, Pallas kernels, corner_start(): pl.pallas_call(corner_start_kernel, out_shape=jax.ShapeDtypeStruct((width...  11.4 us
    pallas_call x1, Pallas kernels, corner_end(): pl.pallas_call(corner_end_kernel, out_shape=jax.ShapeDtypeStruct(state.sh...  10.3 us
    unnamed x18, local copies, waits for them, and re-layouts  7.48 us
    pallas_call x1, Pallas kernels, gather_pieces(): pl.pallas_call(functools.partial(gather_kernel, tile, col_tiles, row_tile...  6.42 us
    pallas_call x1, Pallas kernels, row_weights(): pl.pallas_call(functools.partial(weights_kernel, tile), grid=(row_tiles,)...  5.55 us
  transfers between devices with their start and end apart: 18, of which 5 were waited for; matrix products, arithmetic and copies ran while one was open for 2% of the time, Pallas kernels for 35%

profile of v2, /device:TPU:16, one launch (start us, length us, event | category | flops | bytes accessed | tf_op | source)
XLA Modules:
  0.0 122.1 jit_solution(12027405732360080686)
XLA Ops:
  0.0 2.1 %gather_lead.1.lead_ref = f32[512,128]{1,0:T(8,128)} custom-call(f32[1024,2,8,128]{3,2,1,0:T(8,128)} %bitcast.13), custom_call_target="tpu_custom_call" | custom-call | flops 1000 | bytes 1000 | tf_op jit(solution)/shard_map/gather_lead/pallas_call | solution.py:227
  2.1 3.4 %collective-permute-start = (f32[512,128]{1,0:T(8,128)}, f32[512,128]{1,0:T(8,128)S(1)}, u32[]{:S(2)}, u32[]{:S(2)}) collective-permute-start(f32[512,128]{1,0:T(8,128)} %gather_lead.1.lead_ref), channel_id=1, source_target_pairs={{0,2},{1,3},{4,6},{5,7},{8,10},{9,11},{12,14},{13,15},{16,18},{17,... | collective-permute-start | bytes 786440 | tf_op jit(solution)/shard_map/ppermute | solution.py:422
  5.5 6.4 %gather_pieces.1 = (f32[1536,128]{1,0:T(8,128)}, f32[2048,128]{1,0:T(8,128)}, f32[2048,128]{1,0:T(8,128)}, f32[2048,128]{1,0:T(8,128)}) custom-call(s32[1]{0:T(128)} %bitcast.9.place_ref, f32[512,128]{1,0:T(8,128)} %gather_lead.1.lead_ref, f32[1024,2,8,128]{3,2,1,0:T(8,128)} %bitcast.14, f32[16384,128]{1,0:T(8,128)} %bitcast.15), custom_call_target="tpu_custom_call" | custom-call | flops 1000 | bytes 1000 | tf_op jit(solution)/shard_map/gather_pieces/pallas_call | solution.py:244
  12.0 0.0 collective-permute-done
  12.0 1.3 %collective-permute-start.1 = (f32[256,128]{1,0:T(8,128)S(1)}, f32[256,128]{1,0:T(8,128)S(1)}, u32[]{:S(2)}, u32[]{:S(2)}) collective-permute-start(f32[256,128]{1,0:T(8,128)S(1)} %slice_select_fusion.2), channel_id=1, source_target_pairs={{0,16},{1,17},{2,18},{3,19},{4,20},{5,21},{6,22},{7,23}} | collective-permute-start | bytes 393224 | tf_op jit(solution)/shard_map/ppermute | solution.py:422
  13.3 6.4 %collective-permute-done.1 = f32[256,128]{1,0:T(8,128)S(1)} collective-permute-done((f32[256,128]{1,0:T(8,128)S(1)}, f32[256,128]{1,0:T(8,128)S(1)}, u32[]{:S(2)}, u32[]{:S(2)}) %collective-permute-start.1) | collective-permute-done | bytes 131104 | tf_op jit(solution)/shard_map/ppermute | solution.py:422
  19.8 1.3 %collective-permute-start.2 = (f32[256,128]{1,0:T(8,128)S(1)}, f32[256,128]{1,0:T(8,128)S(1)}, u32[]{:S(2)}, u32[]{:S(2)}) collective-permute-start(f32[256,128]{1,0:T(8,128)S(1)} %broadcast_select_fusion.1), channel_id=1, source_target_pairs={{0,8},{1,9},{2,10},{3,11},{4,12},{5,13},{6,14},{7,15},{16,24},{17,... | collective-permute-start | bytes 393224 | tf_op jit(solution)/shard_map/ppermute | solution.py:422
  21.1 2.5 %collective-permute-done.2 = f32[256,128]{1,0:T(8,128)S(1)} collective-permute-done((f32[256,128]{1,0:T(8,128)S(1)}, f32[256,128]{1,0:T(8,128)S(1)}, u32[]{:S(2)}, u32[]{:S(2)}) %collective-permute-start.2) | collective-permute-done | bytes 131104 | tf_op jit(solution)/shard_map/ppermute | solution.py:422
  23.6 2.5 %collective-permute-start.7 = (f32[2048,128]{1,0:T(8,128)}, f32[2048,128]{1,0:T(8,128)S(1)}, u32[]{:S(2)}, u32[]{:S(2)}) collective-permute-start(f32[2048,128]{1,0:T(8,128)} %get-tuple-element.33), channel_id=1, source_target_pairs={{0,24},{1,25},{2,18},{3,19},{4,28},{5,29},{6,22},{7,23},{16,8},{17... | collective-permute-start | bytes 3145736 | tf_op jit(solution)/shard_map/ppermute | solution.py:422
  26.1 1.6 %collective-permute-start.5 = (f32[256,128]{1,0:T(8,128)S(1)}, f32[256,128]{1,0:T(8,128)S(1)}, u32[]{:S(2)}, u32[]{:S(2)}) collective-permute-start(f32[256,128]{1,0:T(8,128)S(1)} %broadcast_select_fusion.2), channel_id=1, source_target_pairs={{0,6},{1,7},{2,4},{3,5},{4,2},{5,3},{6,0},{7,1},{8,14},{9,15},{10,... | collective-permute-start | bytes 393224 | tf_op jit(solution)/shard_map/ppermute | solution.py:422
  27.8 0.5 collective-permute-start.3
  28.3 1.4 %collective-permute-start.4 = (f32[256,128]{1,0:T(8,128)S(1)}, f32[256,128]{1,0:T(8,128)S(1)}, u32[]{:S(2)}, u32[]{:S(2)}) collective-permute-start(f32[256,128]{1,0:T(8,128)S(1)} %broadcast_select_fusion.2), channel_id=1, source_target_pairs={{0,2},{1,3},{2,0},{3,1},{4,6},{5,7},{6,4},{7,5},{8,10},{9,11},{10,... | collective-permute-start | bytes 393224 | tf_op jit(solution)/shard_map/ppermute | solution.py:422
  29.7 2.4 %collective-permute-done.5 = f32[256,128]{1,0:T(8,128)S(1)} collective-permute-done((f32[256,128]{1,0:T(8,128)S(1)}, f32[256,128]{1,0:T(8,128)S(1)}, u32[]{:S(2)}, u32[]{:S(2)}) %collective-permute-start.5) | collective-permute-done | bytes 131104 | tf_op jit(solution)/shard_map/ppermute | solution.py:422
  32.1 2.6 %collective-permute-start.8 = (f32[1536,128]{1,0:T(8,128)}, f32[1536,128]{1,0:T(8,128)S(1)}, u32[]{:S(2)}, u32[]{:S(2)}) collective-permute-start(f32[1536,128]{1,0:T(8,128)} %get-tuple-element.37), channel_id=1, source_target_pairs={{0,2},{1,3},{4,6},{5,7},{8,10},{9,11},{12,14},{13,15},{16,18},{17,... | collective-permute-start | bytes 2359304 | tf_op jit(solution)/shard_map/ppermute | solution.py:422
  34.7 0.0 collective-permute-done.3
  34.7 0.0 collective-permute-done.4
  34.7 0.1 collective-permute-start.6
  34.9 0.1 pad_add_fusion.1.place_ref
  35.0 1.8 %collective-permute-done.6.other_ref = f32[1024,128]{1,0:T(8,128)S(1)} collective-permute-done((f32[1024,128]{1,0:T(8,128)S(1)}, f32[1024,128]{1,0:T(8,128)S(1)}, u32[]{:S(2)}, u32[]{:S(2)}) %collective-permute-start.6) | collective-permute-done | bytes 524320 | tf_op jit(solution)/shard_map/ppermute | solution.py:422
  36.7 11.4 %corner_start.1.state_ref = f32[512,512]{1,0:T(8,128)S(1)} custom-call(s32[3]{0:T(128)S(1)} %pad_add_fusion.1.place_ref, f32[1024,128]{1,0:T(8,128)S(1)} %constant_dynamic-update-slice_fusion.mine_ref, f32[1024,128]{1,0:T(8,128)S(1)} %collective-permute-done.6.other_ref), custom_call_target="tpu_custom_call" | custom-call | flops 1000 | bytes 1000 | tf_op jit(solution)/shard_map/corner_start/pallas_call | solution.py:150
  48.2 1.0 collective-permute-done.8
  49.1 0.1 constant_dynamic-update-slice_fusion.4
  49.2 2.6 %select_select_fusion = (f32[2048,128]{1,0:T(8,128)S(1)}, f32[2048,128]{1,0:T(8,128)}, f32[2048,128]{1,0:T(8,128)S(1)}) fusion(f32[2048,128]{1,0:T(8,128)} %get-tuple-element.42, f32[2048,128]{1,0:T(8,128)S(1)} %constant_dynamic-update-slice_fusion.4, f32[2048,128]{1,0:T(8,128)S(1)} %collective-permute-done.7, f32[2048,128]{1,0:T(8,128)} %get-tuple-element.33, ...), kind=kLoop, calls=%fused_computation | loop fusion | flops 2097152 | bytes 8388612 | tf_op jit(solution)/shard_map/jit(_where)/select_n | solution.py:488
  51.8 0.1 fusion
  51.8 0.1 collective-permute-start.9
  51.9 5.3 %collective-permute-start.10 = (f32[1024,128]{1,0:T(8,128)S(1)}, f32[1024,128]{1,0:T(8,128)S(1)}, u32[]{:S(2)}, u32[]{:S(2)}) collective-permute-start(f32[1024,128]{1,0:T(8,128)S(1)} %get-tuple-element.44), channel_id=1, source_target_pairs={{0,8},{1,9},{2,10},{3,11},{4,12},{5,13},{6,14},{7,15},{10,26},{11,... | collective-permute-start | bytes 1572872 | tf_op jit(solution)/shard_map/ppermute | solution.py:422
  57.2 1.7 %collective-permute-start.13 = (f32[2048,128]{1,0:T(8,128)}, f32[2048,128]{1,0:T(8,128)}, u32[]{:S(2)}, u32[]{:S(2)}) collective-permute-start(f32[2048,128]{1,0:T(8,128)} %get-tuple-element.50.rest_1_), channel_id=1, source_target_pairs={{9,12},{11,14},{12,9},{14,11},{17,20},{20,17},{25,28},{27,30},{28,... | collective-permute-start | bytes 3145736 | tf_op jit(solution)/shard_map/ppermute | solution.py:422
  58.9 2.2 %collective-permute-start.12 = (f32[2048,128]{1,0:T(8,128)}, f32[2048,128]{1,0:T(8,128)}, u32[]{:S(2)}, u32[]{:S(2)}) collective-permute-start(f32[2048,128]{1,0:T(8,128)} %get-tuple-element.50.rest_1_), channel_id=1, source_target_pairs={{0,4},{1,5},{2,6},{3,7},{4,0},{5,1},{6,2},{7,3},{8,12},{9,8},{10,1... | collective-permute-start | bytes 3145736 | tf_op jit(solution)/shard_map/ppermute | solution.py:422
  61.0 2.4 %collective-permute-start.11 = (f32[1024,128]{1,0:T(8,128)S(1)}, f32[1024,128]{1,0:T(8,128)S(1)}, u32[]{:S(2)}, u32[]{:S(2)}) collective-permute-start(f32[1024,128]{1,0:T(8,128)S(1)} %get-tuple-element.47), channel_id=1, source_target_pairs={{0,8},{1,9},{2,10},{3,11},{4,12},{5,13},{6,14},{7,15},{10,26},{11,... | collective-permute-start | bytes 1572872 | tf_op jit(solution)/shard_map/ppermute | solution.py:422
  63.4 10.3 %corner_end.1.inverse_ref = f32[512,512]{1,0:T(8,128)S(1)} custom-call(f32[512,512]{1,0:T(8,128)S(1)} %corner_start.1.state_ref), custom_call_target="tpu_custom_call" | custom-call | flops 1000 | bytes 1000 | tf_op jit(solution)/shard_map/corner_end/pallas_call | solution.py:163
  73.7 0.9 slice_select_fusion.1.rest_4_
  74.6 0.7 collective-permute-start.15
  75.3 0.1 pad_add_fusion.place_ref
  75.3 2.4 %collective-permute-start.14 = (f32[1024,128]{1,0:T(8,128)}, f32[1024,128]{1,0:T(8,128)}, u32[]{:S(2)}, u32[]{:S(2)}) collective-permute-start(f32[1024,128]{1,0:T(8,128)} %slice_select_fusion.1.rest_4_), channel_id=1, source_target_pairs={{0,4},{1,5},{2,6},{3,7},{4,0},{5,1},{6,2},{7,3},{8,12},{9,8},{10,1... | collective-permute-start | bytes 1572872 | tf_op jit(solution)/shard_map/ppermute | solution.py:422
  77.7 5.5 %row_weights.1 = (bf16[1024,1536]{1,0:T(8,128)(2,1)S(1)}, f32[1024,256]{1,0:T(8,128)S(1)}) custom-call(s32[3]{0:T(128)S(1)} %pad_add_fusion.place_ref, f32[2048,128]{1,0:T(8,128)S(1)} %get-tuple-element.55.rows_mine, f32[2048,128]{1,0:T(8,128)S(1)} %collective-permute-done.9.rows_other, f32[512,512]{1,0:T(8,128)S(1)} %corner_end.1.inverse_ref), custom_call_target="tpu_custom_call" | custom-call | flops 1000 | bytes 1000 | tf_op jit(solution)/shard_map/row_weights/pallas_call | solution.py:315
  83.3 0.0 copy-start.1
  83.3 1.0 copy-done.1
  84.2 0.9 slice_select_fusion.rest_4_
  85.1 1.4 %collective-permute-start.17 = (f32[1024,128]{1,0:T(8,128)}, f32[1024,128]{1,0:T(8,128)}, u32[]{:S(2)}, u32[]{:S(2)}) collective-permute-start(f32[1024,128]{1,0:T(8,128)} %slice_select_fusion.rest_4_), channel_id=1, source_target_pairs={{9,12},{12,9},{17,20},{19,22},{20,17},{22,19},{25,28},{27,30},{28,... | collective-permute-start | bytes 1572872 | tf_op jit(solution)/shard_map/ppermute | solution.py:422
  86.6 0.8 copy-done.3
  87.4 10.0 %collective-permute-start.16 = (f32[1024,128]{1,0:T(8,128)}, f32[1024,128]{1,0:T(8,128)}, u32[]{:S(2)}, u32[]{:S(2)}) collective-permute-start(f32[1024,128]{1,0:T(8,128)} %slice_select_fusion.rest_4_), channel_id=1, source_target_pairs={{0,4},{1,5},{2,6},{3,7},{4,0},{5,1},{6,2},{7,3},{8,12},{9,8},{10,1... | collective-permute-start | bytes 1572872 | tf_op jit(solution)/shard_map/ppermute | solution.py:422
  97.3 0.1 stack.47.place_ref
  97.4 0.0 copy-start
  97.4 3.4 %copy-done = f32[4,1,256,8,1,256]{5,4,3,2,1,0:T(1,128)S(1)} copy-done((f32[4,1,256,8,1,256]{5,4,3,2,1,0:T(1,128)S(1)}, f32[4,1,256,8,1,256]{5,4,3,2,1,0:T(1,128)}, u32[]{:S(2)}) %copy-start) | copy-done | bytes 8388632
  100.8 1.2 %copy-done.2 = f32[1024,256]{1,0:T(8,128)S(1)} copy-done((f32[1024,256]{1,0:T(8,128)S(1)}, f32[1024,256]{1,0:T(8,128)}, u32[]{:S(2)}) %copy-start.2) | copy-done | bytes 1048600
  102.0 1.0 copy-done.4
  103.1 9.5 %trailing_0.1.rest_0_ = f32[1024,2,8,128]{3,2,1,0:T(8,128)} custom-call(s32[7]{0:T(128)S(1)} %stack.47.place_ref, f32[1024,2,8,128]{3,2,1,0:T(8,128)S(1)} %bitcast.16, bf16[1024,1536]{1,0:T(8,128)(2,1)S(1)} %get-tuple-element.48.weights_ref, f32[1024,256]{1,0:T(8,128)S(1)} %copy-done.2, f32[2048,128]{1,0:T(8,128)} %get-tuple-element.50.rest_1_, ...), custom_call_target="tpu_custom_call" | custom-call | flops 1000 | bytes 1000 | tf_op jit(solution)/shard_map/trailing_0/pallas_call | solution.py:397
  112.6 9.4 %trailing_1.1 = f32[1024,2,8,128]{3,2,1,0:T(8,128)} custom-call(s32[7]{0:T(128)S(1)} %stack.47.place_ref, f32[1024,2,8,128]{3,2,1,0:T(8,128)S(1)} %bitcast.17, bf16[1024,1536]{1,0:T(8,128)(2,1)S(1)} %get-tuple-element.48.weights_ref, f32[1024,2,8,128]{3,2,1,0:T(8,128)} %trailing_0.1.rest_0_, ...), custom_call_target="tpu_custom_call", output_to_operand_aliasing={{}: (3, {})} | custom-call | flops 1000 | bytes 1000 | tf_op jit(solution)/shard_map/trailing_1/pallas_call | solution.py:397
  (25 shorter events, 0.1 us)
Async XLA Ops:
  2.1 9.9 %collective-permute-start = (f32[512,128]{1,0:T(8,128)}, f32[512,128]{1,0:T(8,128)S(1)}, u32[]{:S(2)}, u32[]{:S(2)}) collective-permute-start(f32[512,128]{1,0:T(8,128)} %gather_lead.1.lead_ref), channel_id=1, source_target_pairs={{0,2},{1,3},{4,6},{5,7},{8,10},{9,11},{12,14},{13,15},{16,18},{17,... | collective-permute-start | bytes 786440 | tf_op jit(solution)/shard_map/ppermute | solution.py:422
  5.5 6.4 %copy-start.6 = (f32[512,128]{1,0:T(8,128)S(1)}, f32[512,128]{1,0:T(8,128)}, u32[]{:S(2)}) copy-start(f32[512,128]{1,0:T(8,128)} %gather_lead.1.lead_ref) | copy-start | bytes 786436
  12.0 7.8 %collective-permute-start.1 = (f32[256,128]{1,0:T(8,128)S(1)}, f32[256,128]{1,0:T(8,128)S(1)}, u32[]{:S(2)}, u32[]{:S(2)}) collective-permute-start(f32[256,128]{1,0:T(8,128)S(1)} %slice_select_fusion.2), channel_id=1, source_target_pairs={{0,16},{1,17},{2,18},{3,19},{4,20},{5,21},{6,22},{7,23}} | collective-permute-start | bytes 393224 | tf_op jit(solution)/shard_map/ppermute | solution.py:422
  19.8 3.8 %collective-permute-start.2 = (f32[256,128]{1,0:T(8,128)S(1)}, f32[256,128]{1,0:T(8,128)S(1)}, u32[]{:S(2)}, u32[]{:S(2)}) collective-permute-start(f32[256,128]{1,0:T(8,128)S(1)} %broadcast_select_fusion.1), channel_id=1, source_target_pairs={{0,8},{1,9},{2,10},{3,11},{4,12},{5,13},{6,14},{7,15},{16,24},{17,... | collective-permute-start | bytes 393224 | tf_op jit(solution)/shard_map/ppermute | solution.py:422
  23.6 25.5 %collective-permute-start.7 = (f32[2048,128]{1,0:T(8,128)}, f32[2048,128]{1,0:T(8,128)S(1)}, u32[]{:S(2)}, u32[]{:S(2)}) collective-permute-start(f32[2048,128]{1,0:T(8,128)} %get-tuple-element.33), channel_id=1, source_target_pairs={{0,24},{1,25},{2,18},{3,19},{4,28},{5,29},{6,22},{7,23},{16,8},{17... | collective-permute-start | bytes 3145736 | tf_op jit(solution)/shard_map/ppermute | solution.py:422
  26.1 5.9 %collective-permute-start.5 = (f32[256,128]{1,0:T(8,128)S(1)}, f32[256,128]{1,0:T(8,128)S(1)}, u32[]{:S(2)}, u32[]{:S(2)}) collective-permute-start(f32[256,128]{1,0:T(8,128)S(1)} %broadcast_select_fusion.2), channel_id=1, source_target_pairs={{0,6},{1,7},{2,4},{3,5},{4,2},{5,3},{6,0},{7,1},{8,14},{9,15},{10,... | collective-permute-start | bytes 393224 | tf_op jit(solution)/shard_map/ppermute | solution.py:422
  27.8 6.9 %collective-permute-start.3 = (f32[256,128]{1,0:T(8,128)S(1)}, f32[256,128]{1,0:T(8,128)S(1)}, u32[]{:S(2)}, u32[]{:S(2)}) collective-permute-start(f32[256,128]{1,0:T(8,128)S(1)} %broadcast_select_fusion.2), channel_id=1, source_target_pairs={{0,4},{1,5},{2,6},{3,7},{4,0},{5,1},{6,2},{7,3},{8,12},{9,13},{10,... | collective-permute-start | bytes 393224 | tf_op jit(solution)/shard_map/ppermute | solution.py:422
  28.3 6.4 %collective-permute-start.4 = (f32[256,128]{1,0:T(8,128)S(1)}, f32[256,128]{1,0:T(8,128)S(1)}, u32[]{:S(2)}, u32[]{:S(2)}) collective-permute-start(f32[256,128]{1,0:T(8,128)S(1)} %broadcast_select_fusion.2), channel_id=1, source_target_pairs={{0,2},{1,3},{2,0},{3,1},{4,6},{5,7},{6,4},{7,5},{8,10},{9,11},{10,... | collective-permute-start | bytes 393224 | tf_op jit(solution)/shard_map/ppermute | solution.py:422
  32.1 17.1 %collective-permute-start.8 = (f32[1536,128]{1,0:T(8,128)}, f32[1536,128]{1,0:T(8,128)S(1)}, u32[]{:S(2)}, u32[]{:S(2)}) collective-permute-start(f32[1536,128]{1,0:T(8,128)} %get-tuple-element.37), channel_id=1, source_target_pairs={{0,2},{1,3},{4,6},{5,7},{8,10},{9,11},{12,14},{13,15},{16,18},{17,... | collective-permute-start | bytes 2359304 | tf_op jit(solution)/shard_map/ppermute | solution.py:422
  34.7 2.0 %collective-permute-start.6 = (f32[1024,128]{1,0:T(8,128)S(1)}, f32[1024,128]{1,0:T(8,128)S(1)}, u32[]{:S(2)}, u32[]{:S(2)}) collective-permute-start(f32[1024,128]{1,0:T(8,128)S(1)} %constant_dynamic-update-slice_fusion.mine_ref), channel_id=1, source_target_pairs={{0,1},{1,0},{2,3},{3,2},{4,5},{5,4},{6,7},{7,6},{8,9},{9,8},{10,11... | collective-permute-start | bytes 1572872 | tf_op jit(solution)/shard_map/ppermute | solution.py:422
  34.9 38.8 %copy-start.5 = (f32[2048,128]{1,0:T(8,128)S(1)}, f32[2048,128]{1,0:T(8,128)}, u32[]{:S(2)}) copy-start(f32[2048,128]{1,0:T(8,128)} %get-tuple-element.42) | copy-start | bytes 3145732
  51.8 23.5 %collective-permute-start.9 = (f32[2048,128]{1,0:T(8,128)S(1)}, f32[2048,128]{1,0:T(8,128)S(1)}, u32[]{:S(2)}, u32[]{:S(2)}) collective-permute-start(f32[2048,128]{1,0:T(8,128)S(1)} %get-tuple-element.55.rows_mine), channel_id=1, source_target_pairs={{0,1},{1,0},{2,3},{3,2},{4,5},{5,4},{6,7},{7,6},{8,9},{9,8},{10,11... | collective-permute-start | bytes 3145736 | tf_op jit(solution)/shard_map/ppermute | solution.py:422
  51.9 21.8 %collective-permute-start.10 = (f32[1024,128]{1,0:T(8,128)S(1)}, f32[1024,128]{1,0:T(8,128)S(1)}, u32[]{:S(2)}, u32[]{:S(2)}) collective-permute-start(f32[1024,128]{1,0:T(8,128)S(1)} %get-tuple-element.44), channel_id=1, source_target_pairs={{0,8},{1,9},{2,10},{3,11},{4,12},{5,13},{6,14},{7,15},{10,26},{11,... | collective-permute-start | bytes 1572872 | tf_op jit(solution)/shard_map/ppermute | solution.py:422
  57.2 40.2 %collective-permute-start.13 = (f32[2048,128]{1,0:T(8,128)}, f32[2048,128]{1,0:T(8,128)}, u32[]{:S(2)}, u32[]{:S(2)}) collective-permute-start(f32[2048,128]{1,0:T(8,128)} %get-tuple-element.50.rest_1_), channel_id=1, source_target_pairs={{9,12},{11,14},{12,9},{14,11},{17,20},{20,17},{25,28},{27,30},{28,... | collective-permute-start | bytes 3145736 | tf_op jit(solution)/shard_map/ppermute | solution.py:422
  58.9 38.5 %collective-permute-start.12 = (f32[2048,128]{1,0:T(8,128)}, f32[2048,128]{1,0:T(8,128)}, u32[]{:S(2)}, u32[]{:S(2)}) collective-permute-start(f32[2048,128]{1,0:T(8,128)} %get-tuple-element.50.rest_1_), channel_id=1, source_target_pairs={{0,4},{1,5},{2,6},{3,7},{4,0},{5,1},{6,2},{7,3},{8,12},{9,8},{10,1... | collective-permute-start | bytes 3145736 | tf_op jit(solution)/shard_map/ppermute | solution.py:422
  61.0 23.2 %collective-permute-start.11 = (f32[1024,128]{1,0:T(8,128)S(1)}, f32[1024,128]{1,0:T(8,128)S(1)}, u32[]{:S(2)}, u32[]{:S(2)}) collective-permute-start(f32[1024,128]{1,0:T(8,128)S(1)} %get-tuple-element.47), channel_id=1, source_target_pairs={{0,8},{1,9},{2,10},{3,11},{4,12},{5,13},{6,14},{7,15},{10,26},{11,... | collective-permute-start | bytes 1572872 | tf_op jit(solution)/shard_map/ppermute | solution.py:422
  74.6 12.0 %collective-permute-start.15 = (f32[1024,128]{1,0:T(8,128)}, f32[1024,128]{1,0:T(8,128)S(1)}, u32[]{:S(2)}, u32[]{:S(2)}) collective-permute-start(f32[1024,128]{1,0:T(8,128)} %slice_select_fusion.1.rest_4_), channel_id=1, source_target_pairs={{9,12},{12,9},{17,20},{19,22},{20,17},{22,19},{25,28},{27,30},{28,... | collective-permute-start | bytes 1572872 | tf_op jit(solution)/shard_map/ppermute | solution.py:422
  75.3 22.1 %collective-permute-start.14 = (f32[1024,128]{1,0:T(8,128)}, f32[1024,128]{1,0:T(8,128)}, u32[]{:S(2)}, u32[]{:S(2)}) collective-permute-start(f32[1024,128]{1,0:T(8,128)} %slice_select_fusion.1.rest_4_), channel_id=1, source_target_pairs={{0,4},{1,5},{2,6},{3,7},{4,0},{5,1},{6,2},{7,3},{8,12},{9,8},{10,1... | collective-permute-start | bytes 1572872 | tf_op jit(solution)/shard_map/ppermute | solution.py:422
  83.3 1.0 copy-start.1
  85.1 27.5 %collective-permute-start.17 = (f32[1024,128]{1,0:T(8,128)}, f32[1024,128]{1,0:T(8,128)}, u32[]{:S(2)}, u32[]{:S(2)}) collective-permute-start(f32[1024,128]{1,0:T(8,128)} %slice_select_fusion.rest_4_), channel_id=1, source_target_pairs={{9,12},{12,9},{17,20},{19,22},{20,17},{22,19},{25,28},{27,30},{28,... | collective-permute-start | bytes 1572872 | tf_op jit(solution)/shard_map/ppermute | solution.py:422
  86.6 0.8 copy-start.3
  87.4 25.3 %collective-permute-start.16 = (f32[1024,128]{1,0:T(8,128)}, f32[1024,128]{1,0:T(8,128)}, u32[]{:S(2)}, u32[]{:S(2)}) collective-permute-start(f32[1024,128]{1,0:T(8,128)} %slice_select_fusion.rest_4_), channel_id=1, source_target_pairs={{0,4},{1,5},{2,6},{3,7},{4,0},{5,1},{6,2},{7,3},{8,12},{9,8},{10,1... | collective-permute-start | bytes 1572872 | tf_op jit(solution)/shard_map/ppermute | solution.py:422
  97.4 3.4 %copy-start = (f32[4,1,256,8,1,256]{5,4,3,2,1,0:T(1,128)S(1)}, f32[4,1,256,8,1,256]{5,4,3,2,1,0:T(1,128)}, u32[]{:S(2)}) copy-start(f32[4,1,256,8,1,256]{5,4,3,2,1,0:T(1,128)} %param.1) | copy-start | bytes 25165828
  100.8 1.2 %copy-start.2 = (f32[1024,256]{1,0:T(8,128)S(1)}, f32[1024,256]{1,0:T(8,128)}, u32[]{:S(2)}) copy-start(f32[1024,256]{1,0:T(8,128)} %copy-done.1) | copy-start | bytes 3145732
  102.0 1.0 copy-start.4

commit v3 on v2

--- a/solution.py
+++ b/solution.py
@@ -324,7 +324,7 @@
         ],
         out_specs=[pl.BlockSpec((tile, 3 * depth), lambda a: (a, 0)), pl.BlockSpec((tile, tile), lambda a: (a, 0))],
         scratch_shapes=[pltpu.VMEM((depth, 3 * depth), BF16), pltpu.VMEM((3 * depth, depth), BF16)],
-        compiler_params=pltpu.CompilerParams(vmem_limit_bytes=32 * 1024 * 1024),
+        compiler_params=pltpu.CompilerParams(vmem_limit_bytes=18 * 1024 * 1024),
         cost_estimate=COST,
         name="row_weights",
     )(place, rows_mine, rows_other, inverse)
@@ -404,7 +404,7 @@
         out_specs=block_spec,
         scratch_shapes=[pltpu.VMEM((depth, 2 * count * tile), BF16)],
         input_output_aliases={} if group == 0 else {3: 0},
-        compiler_params=pltpu.CompilerParams(vmem_limit_bytes=32 * 1024 * 1024),
+        compiler_params=pltpu.CompilerParams(vmem_limit_bytes=18 * 1024 * 1024),
         cost_estimate=COST,
         name="trailing_%d" % group,
     )(place, view, weights, extra, *pieces[0], *pieces[1])
@@ -468,21 +468,24 @@
     rest, to_far, even, odd = gather_pieces(y.reshape(1), lead, block, row_tiles, col_tiles, tile)
     over_first, rest, to_far = lax.optimization_barrier((over_first, rest, to_far))
     half = jnp.where(y == 0, lead[:middle], over_first[middle:])
-    half = jnp.where(z == 2, send(half, lambda z, x, y, k: (2, x, y, k) if z == 0 else None), half)
-    half = jnp.where(z % 2 == 1, send(half, lambda z, x, y, k: (z + 1, x, y, k) if z % 2 == 0 else None), half)
-    half, to_far = lax.optimization_barrier((half, to_far))
+    down = [send(half, lambda z, x, y, k, to=to: (to, x, y, k) if z == 0 else None) for to in (1, 2, 3)]
+    size = lead.shape[0]
+    first_down, to_far, middle_rest = lax.optimization_barrier((down[0], to_far, rest[:size]))
     far = send(to_far, far_stage)
+    over_middle = send(middle_rest, lambda z, x, y, k: (z, x, 1, k) if y == 0 else None)
+    half = jnp.where(z == 0, half, jnp.where(z == 1, first_down, jnp.where(z == 2, down[1], down[2])))
+    half, over_middle = lax.optimization_barrier((half, over_middle))
     beside = send(half, lambda z, x, y, k: (z, 1 - x, y, k))
     above = send(half, lambda z, x, y, k: (z, x, 1 - y, k))
     corner = send(half, lambda z, x, y, k: (z, 1 - x, 1 - y, k))
-    corner, rest = lax.optimization_barrier((corner, rest))
+    corner, last_rest = lax.optimization_barrier((corner, rest[size:]))
     mine = jnp.concatenate([half, beside, above, corner], axis=0)
-    over_rest = send(rest, lambda z, x, y, k: (z, x, 1, k) if y == 0 else None)
+    over_last = send(last_rest, lambda z, x, y, k: (z, x, 1, k) if y == 0 else None)
     other = send(mine, lambda z, x, y, k: (z, x, y, 1 - k))
     state = corner_start(jnp.stack([core, x, y]).astype(jnp.int32), mine, other)
 
-    state, far, over_rest = lax.optimization_barrier((state, far, over_rest))
-    over = jnp.concatenate([over_first, over_rest], axis=0)
+    state, far, over_middle, over_last = lax.optimization_barrier((state, far, over_middle, over_last))
+    over = jnp.concatenate([over_first, over_middle, over_last], axis=0)
     rows_mine = jnp.where(y == 0, to_far, over)
     first = jnp.where(z == 0, even, jnp.where(y == 0, jnp.where(z == 2, to_far, far), jnp.where(z == 2, far, over)))
     to_near = jnp.where(y == 0, jnp.where(z == 3, far, to_far), jnp.where(z == 0, odd, over))

time: 123 us -> 127 us (1.033)
  the two profiles are of different devices: /device:TPU:16 before, /device:TPU:13 now
where the time goes in v3:
time: 127 us; the launch traced here: 126 us
  Pallas kernels  54.3 us (43%)
  starting transfers between devices  30.9 us (24%)
  waiting for transfers between devices  23.4 us (18%)
  local copies, waits for them, and re-layouts  12.5 us (10%)
  other arithmetic  4.52 us (4%)
    ppermute x20, starting transfers between devices, send(): return lax.ppermute(value, AXES, pairs)  30.9 us
    ppermute x20, waiting for transfers between devices, send(): return lax.ppermute(value, AXES, pairs)  23.4 us
    pallas_call x2, Pallas kernels, trailing(): pl.pallas_call(functools.partial(trailing_kernel, tile, group, count, off...  18.7 us
    pallas_call x1, Pallas kernels, corner_start(): pl.pallas_call(corner_start_kernel, out_shape=jax.ShapeDtypeStruct((width...  11.4 us
    pallas_call x1, Pallas kernels, corner_end(): pl.pallas_call(corner_end_kernel, out_shape=jax.ShapeDtypeStruct(state.sh...  10.3 us
    unnamed x25, local copies, waits for them, and re-layouts  8.45 us
    pallas_call x1, Pallas kernels, gather_pieces(): pl.pallas_call(functools.partial(gather_kernel, tile, col_tiles, row_tile...  6.48 us
    pallas_call x1, Pallas kernels, row_weights(): pl.pallas_call(functools.partial(weights_kernel, tile), grid=(row_tiles,)...  5.37 us
  transfers between devices with their start and end apart: 20, of which 9 were waited for; matrix products, arithmetic and copies ran while one was open for 4% of the time, Pallas kernels for 34%

profile of v3, /device:TPU:13, one launch (start us, length us, event | category | flops | bytes accessed | tf_op | source)
XLA Modules:
  0.0 126.0 jit_solution(4813011295297058747)
XLA Ops:
  0.0 2.1 %gather_lead.1.lead_ref = f32[512,128]{1,0:T(8,128)} custom-call(f32[1024,2,8,128]{3,2,1,0:T(8,128)} %bitcast.13), custom_call_target="tpu_custom_call" | custom-call | flops 1000 | bytes 1000 | tf_op jit(solution)/shard_map/gather_lead/pallas_call | solution.py:227
  2.1 1.3 %collective-permute-start = (f32[512,128]{1,0:T(8,128)}, f32[512,128]{1,0:T(8,128)S(1)}, u32[]{:S(2)}, u32[]{:S(2)}) collective-permute-start(f32[512,128]{1,0:T(8,128)} %gather_lead.1.lead_ref), channel_id=1, source_target_pairs={{0,2},{1,3},{4,6},{5,7},{8,10},{9,11},{12,14},{13,15},{16,18},{17,... | collective-permute-start | bytes 786440 | tf_op jit(solution)/shard_map/ppermute | solution.py:422
  3.4 6.5 %gather_pieces.1 = (f32[1536,128]{1,0:T(8,128)}, f32[2048,128]{1,0:T(8,128)}, f32[2048,128]{1,0:T(8,128)}, f32[2048,128]{1,0:T(8,128)}) custom-call(s32[1]{0:T(128)} %bitcast.9.place_ref, f32[512,128]{1,0:T(8,128)} %gather_lead.1.lead_ref, f32[1024,2,8,128]{3,2,1,0:T(8,128)} %bitcast.14, f32[16384,128]{1,0:T(8,128)} %bitcast.15), custom_call_target="tpu_custom_call" | custom-call | flops 1000 | bytes 1000 | tf_op jit(solution)/shard_map/gather_pieces/pallas_call | solution.py:244
  9.9 1.5 %collective-permute-done = f32[512,128]{1,0:T(8,128)S(1)} collective-permute-done((f32[512,128]{1,0:T(8,128)}, f32[512,128]{1,0:T(8,128)S(1)}, u32[]{:S(2)}, u32[]{:S(2)}) %collective-permute-start) | collective-permute-done | bytes 262176 | tf_op jit(solution)/shard_map/ppermute | solution.py:422
  11.4 1.3 %collective-permute-start.1 = (f32[256,128]{1,0:T(8,128)S(1)}, f32[256,128]{1,0:T(8,128)S(1)}, u32[]{:S(2)}, u32[]{:S(2)}) collective-permute-start(f32[256,128]{1,0:T(8,128)S(1)} %slice_select_fusion.2), channel_id=1, source_target_pairs={{0,8},{1,9},{2,10},{3,11},{4,12},{5,13},{6,14},{7,15}} | collective-permute-start | bytes 393224 | tf_op jit(solution)/shard_map/ppermute | solution.py:422
  12.7 0.7 collective-permute-start.3
  13.3 0.7 collective-permute-start.2
  14.0 1.0 slice.26
  15.0 2.1 %collective-permute-done.1 = f32[256,128]{1,0:T(8,128)S(1)} collective-permute-done((f32[256,128]{1,0:T(8,128)S(1)}, f32[256,128]{1,0:T(8,128)S(1)}, u32[]{:S(2)}, u32[]{:S(2)}) %collective-permute-start.1) | collective-permute-done | bytes 131104 | tf_op jit(solution)/shard_map/ppermute | solution.py:422
  17.1 1.3 %collective-permute-start.4 = (f32[512,128]{1,0:T(8,128)S(1)}, f32[512,128]{1,0:T(8,128)S(1)}, u32[]{:S(2)}, u32[]{:S(2)}) collective-permute-start(f32[512,128]{1,0:T(8,128)S(1)} %slice.26), channel_id=1, source_target_pairs={{0,2},{1,3},{4,6},{5,7},{8,10},{9,11},{12,14},{13,15},{16,18},{17,... | collective-permute-start | bytes 786440 | tf_op jit(solution)/shard_map/ppermute | solution.py:422
  18.4 1.7 %collective-permute-start.9 = (f32[2048,128]{1,0:T(8,128)}, f32[2048,128]{1,0:T(8,128)}, u32[]{:S(2)}, u32[]{:S(2)}) collective-permute-start(f32[2048,128]{1,0:T(8,128)} %get-tuple-element.38), channel_id=1, source_target_pairs={{0,24},{1,25},{2,18},{3,19},{4,28},{5,29},{6,22},{7,23},{16,8},{17... | collective-permute-start | bytes 3145736 | tf_op jit(solution)/shard_map/ppermute | solution.py:422
  20.1 4.1 %collective-permute-done.4 = f32[512,128]{1,0:T(8,128)S(1)} collective-permute-done((f32[512,128]{1,0:T(8,128)S(1)}, f32[512,128]{1,0:T(8,128)S(1)}, u32[]{:S(2)}, u32[]{:S(2)}) %collective-permute-start.4) | collective-permute-done | bytes 262176 | tf_op jit(solution)/shard_map/ppermute | solution.py:422
  24.2 0.5 collective-permute-start.7
  24.7 0.7 collective-permute-start.5
  25.4 1.9 %slice.27 = f32[1024,128]{1,0:T(8,128)} slice(f32[1536,128]{1,0:T(8,128)} %get-tuple-element.37), slice={[512:1536], [0:128]} | slice | bytes 1048576 | tf_op jit(solution)/shard_map/slice | solution.py:481
  27.3 1.4 %collective-permute-start.6 = (f32[256,128]{1,0:T(8,128)S(1)}, f32[256,128]{1,0:T(8,128)S(1)}, u32[]{:S(2)}, u32[]{:S(2)}) collective-permute-start(f32[256,128]{1,0:T(8,128)S(1)} %select_select_fusion.2), channel_id=1, source_target_pairs={{0,2},{1,3},{2,0},{3,1},{4,6},{5,7},{6,4},{7,5},{8,10},{9,11},{10,... | collective-permute-start | bytes 393224 | tf_op jit(solution)/shard_map/ppermute | solution.py:422
  28.7 0.3 collective-permute-done.7
  29.0 0.4 collective-permute-done.5
  29.5 1.6 %collective-permute-done.6 = f32[256,128]{1,0:T(8,128)S(1)} collective-permute-done((f32[256,128]{1,0:T(8,128)S(1)}, f32[256,128]{1,0:T(8,128)S(1)}, u32[]{:S(2)}, u32[]{:S(2)}) %collective-permute-start.6) | collective-permute-done | bytes 131104 | tf_op jit(solution)/shard_map/ppermute | solution.py:422
  31.1 7.5 %collective-permute-start.8 = (f32[1024,128]{1,0:T(8,128)S(1)}, f32[1024,128]{1,0:T(8,128)S(1)}, u32[]{:S(2)}, u32[]{:S(2)}) collective-permute-start(f32[1024,128]{1,0:T(8,128)S(1)} %constant_dynamic-update-slice_fusion.mine_ref), channel_id=1, source_target_pairs={{0,1},{1,0},{2,3},{3,2},{4,5},{5,4},{6,7},{7,6},{8,9},{9,8},{10,11... | collective-permute-start | bytes 1572872 | tf_op jit(solution)/shard_map/ppermute | solution.py:422
  38.6 1.3 %collective-permute-start.10 = (f32[1024,128]{1,0:T(8,128)}, f32[1024,128]{1,0:T(8,128)}, u32[]{:S(2)}, u32[]{:S(2)}) collective-permute-start(f32[1024,128]{1,0:T(8,128)} %slice.27), channel_id=1, source_target_pairs={{0,2},{1,3},{4,6},{5,7},{8,10},{9,11},{12,14},{13,15},{16,18},{17,... | collective-permute-start | bytes 1572872 | tf_op jit(solution)/shard_map/ppermute | solution.py:422
  40.0 0.1 collective-permute-done.8.other_ref
  40.2 11.4 %corner_start.1.state_ref = f32[512,512]{1,0:T(8,128)S(1)} custom-call(s32[3]{0:T(128)S(1)} %pad_add_fusion.1.place_ref, f32[1024,128]{1,0:T(8,128)S(1)} %constant_dynamic-update-slice_fusion.mine_ref, f32[1024,128]{1,0:T(8,128)S(1)} %collective-permute-done.8.other_ref), custom_call_target="tpu_custom_call" | custom-call | flops 1000 | bytes 1000 | tf_op jit(solution)/shard_map/corner_start/pallas_call | solution.py:150
  51.6 2.7 %collective-permute-done.10 = f32[1024,128]{1,0:T(8,128)} collective-permute-done((f32[1024,128]{1,0:T(8,128)}, f32[1024,128]{1,0:T(8,128)}, u32[]{:S(2)}, u32[]{:S(2)}) %collective-permute-start.10) | collective-permute-done | bytes 524320 | tf_op jit(solution)/shard_map/ppermute | solution.py:422
  54.4 1.0 constant_dynamic-update-slice_fusion.5
  55.3 1.1 constant_dynamic-update-slice_fusion.4
  56.5 2.6 %select_select_fusion = (f32[2048,128]{1,0:T(8,128)S(1)}, f32[2048,128]{1,0:T(8,128)}, f32[2048,128]{1,0:T(8,128)S(1)}) fusion(f32[2048,128]{1,0:T(8,128)S(1)} %copy-done.5, f32[2048,128]{1,0:T(8,128)S(1)} %constant_dynamic-update-slice_fusion.4, f32[2048,128]{1,0:T(8,128)} %collective-permute-done.9, f32[2048,128]{1,0:T(8,128)S(1)} %copy-done.8, pred[]{:T(512)S(6)} %eq.29, ...), kind=kLoop, calls=%fused_computation | loop fusion | flops 2097152 | bytes 8388612 | tf_op jit(solution)/shard_map/jit(_where)/select_n | solution.py:491
  59.1 0.9 collective-permute-start.11
  60.0 1.9 %collective-permute-start.12 = (f32[1024,128]{1,0:T(8,128)S(1)}, f32[1024,128]{1,0:T(8,128)S(1)}, u32[]{:S(2)}, u32[]{:S(2)}) collective-permute-start(f32[1024,128]{1,0:T(8,128)S(1)} %get-tuple-element.52), channel_id=1, source_target_pairs={{0,8},{1,9},{2,10},{3,11},{4,12},{5,13},{6,14},{7,15},{10,26},{11,... | collective-permute-start | bytes 1572872 | tf_op jit(solution)/shard_map/ppermute | solution.py:422
  61.9 3.0 %collective-permute-start.15 = (f32[2048,128]{1,0:T(8,128)}, f32[2048,128]{1,0:T(8,128)}, u32[]{:S(2)}, u32[]{:S(2)}) collective-permute-start(f32[2048,128]{1,0:T(8,128)} %get-tuple-element.58.rest_1_), channel_id=1, source_target_pairs={{9,12},{11,14},{12,9},{14,11},{17,20},{20,17},{25,28},{27,30},{28,... | collective-permute-start | bytes 3145736 | tf_op jit(solution)/shard_map/ppermute | solution.py:422
  65.0 2.6 %collective-permute-start.13 = (f32[1024,128]{1,0:T(8,128)S(1)}, f32[1024,128]{1,0:T(8,128)S(1)}, u32[]{:S(2)}, u32[]{:S(2)}) collective-permute-start(f32[1024,128]{1,0:T(8,128)S(1)} %get-tuple-element.55), channel_id=1, source_target_pairs={{0,8},{1,9},{2,10},{3,11},{4,12},{5,13},{6,14},{7,15},{10,26},{11,... | collective-permute-start | bytes 1572872 | tf_op jit(solution)/shard_map/ppermute | solution.py:422
  67.6 10.3 %corner_end.1.inverse_ref = f32[512,512]{1,0:T(8,128)S(1)} custom-call(f32[512,512]{1,0:T(8,128)S(1)} %corner_start.1.state_ref), custom_call_target="tpu_custom_call" | custom-call | flops 1000 | bytes 1000 | tf_op jit(solution)/shard_map/corner_end/pallas_call | solution.py:163
  77.9 0.9 slice_select_fusion.1.rest_4_
  78.8 0.7 collective-permute-start.17
  79.5 1.4 %collective-permute-start.16 = (f32[1024,128]{1,0:T(8,128)}, f32[1024,128]{1,0:T(8,128)}, u32[]{:S(2)}, u32[]{:S(2)}) collective-permute-start(f32[1024,128]{1,0:T(8,128)} %slice_select_fusion.1.rest_4_), channel_id=1, source_target_pairs={{0,4},{1,5},{2,6},{3,7},{4,0},{5,1},{6,2},{7,3},{8,12},{9,8},{10,1... | collective-permute-start | bytes 1572872 | tf_op jit(solution)/shard_map/ppermute | solution.py:422
  81.0 5.4 %row_weights.1 = (bf16[1024,1536]{1,0:T(8,128)(2,1)S(1)}, f32[1024,256]{1,0:T(8,128)S(1)}) custom-call(s32[3]{0:T(128)S(1)} %pad_add_fusion.place_ref, f32[2048,128]{1,0:T(8,128)S(1)} %get-tuple-element.63.rows_mine, f32[2048,128]{1,0:T(8,128)S(1)} %collective-permute-done.11.rows_other, f32[512,512]{1,0:T(8,128)S(1)} %corner_end.1.inverse_ref), custom_call_target="tpu_custom_call" | custom-call | flops 1000 | bytes 1000 | tf_op jit(solution)/shard_map/row_weights/pallas_call | solution.py:315
  86.4 1.0 copy-done.1
  87.3 0.9 slice_select_fusion.rest_4_
  88.2 1.5 %collective-permute-start.19 = (f32[1024,128]{1,0:T(8,128)}, f32[1024,128]{1,0:T(8,128)}, u32[]{:S(2)}, u32[]{:S(2)}) collective-permute-start(f32[1024,128]{1,0:T(8,128)} %slice_select_fusion.rest_4_), channel_id=1, source_target_pairs={{9,12},{12,9},{17,20},{19,22},{20,17},{22,19},{25,28},{27,30},{28,... | collective-permute-start | bytes 1572872 | tf_op jit(solution)/shard_map/ppermute | solution.py:422
  89.6 0.8 copy-done.3
  90.4 0.6 collective-permute-start.18
  91.1 0.1 stack.47.place_ref
  91.1 10.5 %collective-permute-done.16.rest_5_ = f32[1024,128]{1,0:T(8,128)} collective-permute-done((f32[1024,128]{1,0:T(8,128)}, f32[1024,128]{1,0:T(8,128)}, u32[]{:S(2)}, u32[]{:S(2)}) %collective-permute-start.16) | collective-permute-done | bytes 524320 | tf_op jit(solution)/shard_map/ppermute | solution.py:422
  101.7 3.4 %copy-done = f32[4,1,256,8,1,256]{5,4,3,2,1,0:T(1,128)S(1)} copy-done((f32[4,1,256,8,1,256]{5,4,3,2,1,0:T(1,128)S(1)}, f32[4,1,256,8,1,256]{5,4,3,2,1,0:T(1,128)}, u32[]{:S(2)}) %copy-start) | copy-done | bytes 8388632
  105.0 1.2 copy-done.2
  106.3 1.0 copy-done.4
  107.3 9.3 %trailing_0.1.rest_0_ = f32[1024,2,8,128]{3,2,1,0:T(8,128)} custom-call(s32[7]{0:T(128)S(1)} %stack.47.place_ref, f32[1024,2,8,128]{3,2,1,0:T(8,128)S(1)} %bitcast.16, bf16[1024,1536]{1,0:T(8,128)(2,1)S(1)} %get-tuple-element.56.weights_ref, f32[1024,256]{1,0:T(8,128)S(1)} %copy-done.2, f32[2048,128]{1,0:T(8,128)} %get-tuple-element.58.rest_1_, ...), custom_call_target="tpu_custom_call" | custom-call | flops 1000 | bytes 1000 | tf_op jit(solution)/shard_map/trailing_0/pallas_call | solution.py:397
  116.6 9.4 %trailing_1.1 = f32[1024,2,8,128]{3,2,1,0:T(8,128)} custom-call(s32[7]{0:T(128)S(1)} %stack.47.place_ref, f32[1024,2,8,128]{3,2,1,0:T(8,128)S(1)} %bitcast.17, bf16[1024,1536]{1,0:T(8,128)(2,1)S(1)} %get-tuple-element.56.weights_ref, f32[1024,2,8,128]{3,2,1,0:T(8,128)} %trailing_0.1.rest_0_, ...), custom_call_target="tpu_custom_call", output_to_operand_aliasing={{}: (3, {})} | custom-call | flops 1000 | bytes 1000 | tf_op jit(solution)/shard_map/trailing_1/pallas_call | solution.py:397
  (37 shorter events, 0.4 us)
Async XLA Ops:
  2.1 9.3 %collective-permute-start = (f32[512,128]{1,0:T(8,128)}, f32[512,128]{1,0:T(8,128)S(1)}, u32[]{:S(2)}, u32[]{:S(2)}) collective-permute-start(f32[512,128]{1,0:T(8,128)} %gather_lead.1.lead_ref), channel_id=1, source_target_pairs={{0,2},{1,3},{4,6},{5,7},{8,10},{9,11},{12,14},{13,15},{16,18},{17,... | collective-permute-start | bytes 786440 | tf_op jit(solution)/shard_map/ppermute | solution.py:422
  3.4 8.0 %copy-start.7 = (f32[512,128]{1,0:T(8,128)S(1)}, f32[512,128]{1,0:T(8,128)}, u32[]{:S(2)}) copy-start(f32[512,128]{1,0:T(8,128)} %gather_lead.1.lead_ref) | copy-start | bytes 786436
  9.9 46.5 %copy-start.5 = (f32[2048,128]{1,0:T(8,128)S(1)}, f32[2048,128]{1,0:T(8,128)}, u32[]{:S(2)}) copy-start(f32[2048,128]{1,0:T(8,128)} %get-tuple-element.50) | copy-start | bytes 3145732
  9.9 46.6 %copy-start.8 = (f32[2048,128]{1,0:T(8,128)S(1)}, f32[2048,128]{1,0:T(8,128)}, u32[]{:S(2)}) copy-start(f32[2048,128]{1,0:T(8,128)} %get-tuple-element.38) | copy-start | bytes 3145732
  11.4 5.7 %collective-permute-start.1 = (f32[256,128]{1,0:T(8,128)S(1)}, f32[256,128]{1,0:T(8,128)S(1)}, u32[]{:S(2)}, u32[]{:S(2)}) collective-permute-start(f32[256,128]{1,0:T(8,128)S(1)} %slice_select_fusion.2), channel_id=1, source_target_pairs={{0,8},{1,9},{2,10},{3,11},{4,12},{5,13},{6,14},{7,15}} | collective-permute-start | bytes 393224 | tf_op jit(solution)/shard_map/ppermute | solution.py:422
  12.7 7.4 %collective-permute-start.3 = (f32[256,128]{1,0:T(8,128)S(1)}, f32[256,128]{1,0:T(8,128)S(1)}, u32[]{:S(2)}, u32[]{:S(2)}) collective-permute-start(f32[256,128]{1,0:T(8,128)S(1)} %slice_select_fusion.2), channel_id=1, source_target_pairs={{0,24},{1,25},{2,26},{3,27},{4,28},{5,29},{6,30},{7,31}} | collective-permute-start | bytes 393224 | tf_op jit(solution)/shard_map/ppermute | solution.py:422
  13.3 6.7 %collective-permute-start.2 = (f32[256,128]{1,0:T(8,128)S(1)}, f32[256,128]{1,0:T(8,128)S(1)}, u32[]{:S(2)}, u32[]{:S(2)}) collective-permute-start(f32[256,128]{1,0:T(8,128)S(1)} %slice_select_fusion.2), channel_id=1, source_target_pairs={{0,16},{1,17},{2,18},{3,19},{4,20},{5,21},{6,22},{7,23}} | collective-permute-start | bytes 393224 | tf_op jit(solution)/shard_map/ppermute | solution.py:422
  17.1 7.1 %collective-permute-start.4 = (f32[512,128]{1,0:T(8,128)S(1)}, f32[512,128]{1,0:T(8,128)S(1)}, u32[]{:S(2)}, u32[]{:S(2)}) collective-permute-start(f32[512,128]{1,0:T(8,128)S(1)} %slice.26), channel_id=1, source_target_pairs={{0,2},{1,3},{4,6},{5,7},{8,10},{9,11},{12,14},{13,15},{16,18},{17,... | collective-permute-start | bytes 786440 | tf_op jit(solution)/shard_map/ppermute | solution.py:422
  18.4 36.0 %collective-permute-start.9 = (f32[2048,128]{1,0:T(8,128)}, f32[2048,128]{1,0:T(8,128)}, u32[]{:S(2)}, u32[]{:S(2)}) collective-permute-start(f32[2048,128]{1,0:T(8,128)} %get-tuple-element.38), channel_id=1, source_target_pairs={{0,24},{1,25},{2,18},{3,19},{4,28},{5,29},{6,22},{7,23},{16,8},{17... | collective-permute-start | bytes 3145736 | tf_op jit(solution)/shard_map/ppermute | solution.py:422
  24.2 3.1 %copy-start.9 = (f32[512,128]{1,0:T(8,128)}, f32[512,128]{1,0:T(8,128)S(1)}, u32[]{:S(2)}) copy-start(f32[512,128]{1,0:T(8,128)S(1)} %collective-permute-done.4) | copy-start | bytes 786436
  24.2 4.8 %collective-permute-start.7 = (f32[256,128]{1,0:T(8,128)S(1)}, f32[256,128]{1,0:T(8,128)S(1)}, u32[]{:S(2)}, u32[]{:S(2)}) collective-permute-start(f32[256,128]{1,0:T(8,128)S(1)} %select_select_fusion.2), channel_id=1, source_target_pairs={{0,6},{1,7},{2,4},{3,5},{4,2},{5,3},{6,0},{7,1},{8,14},{9,15},{10,... | collective-permute-start | bytes 393224 | tf_op jit(solution)/shard_map/ppermute | solution.py:422
  24.7 4.8 %collective-permute-start.5 = (f32[256,128]{1,0:T(8,128)S(1)}, f32[256,128]{1,0:T(8,128)S(1)}, u32[]{:S(2)}, u32[]{:S(2)}) collective-permute-start(f32[256,128]{1,0:T(8,128)S(1)} %select_select_fusion.2), channel_id=1, source_target_pairs={{0,4},{1,5},{2,6},{3,7},{4,0},{5,1},{6,2},{7,3},{8,12},{9,13},{10,... | collective-permute-start | bytes 393224 | tf_op jit(solution)/shard_map/ppermute | solution.py:422
  27.3 3.8 %collective-permute-start.6 = (f32[256,128]{1,0:T(8,128)S(1)}, f32[256,128]{1,0:T(8,128)S(1)}, u32[]{:S(2)}, u32[]{:S(2)}) collective-permute-start(f32[256,128]{1,0:T(8,128)S(1)} %select_select_fusion.2), channel_id=1, source_target_pairs={{0,2},{1,3},{2,0},{3,1},{4,6},{5,7},{6,4},{7,5},{8,10},{9,11},{10,... | collective-permute-start | bytes 393224 | tf_op jit(solution)/shard_map/ppermute | solution.py:422
  31.1 9.0 %collective-permute-start.8 = (f32[1024,128]{1,0:T(8,128)S(1)}, f32[1024,128]{1,0:T(8,128)S(1)}, u32[]{:S(2)}, u32[]{:S(2)}) collective-permute-start(f32[1024,128]{1,0:T(8,128)S(1)} %constant_dynamic-update-slice_fusion.mine_ref), channel_id=1, source_target_pairs={{0,1},{1,0},{2,3},{3,2},{4,5},{5,4},{6,7},{7,6},{8,9},{9,8},{10,11... | collective-permute-start | bytes 1572872 | tf_op jit(solution)/shard_map/ppermute | solution.py:422
  38.6 15.7 %collective-permute-start.10 = (f32[1024,128]{1,0:T(8,128)}, f32[1024,128]{1,0:T(8,128)}, u32[]{:S(2)}, u32[]{:S(2)}) collective-permute-start(f32[1024,128]{1,0:T(8,128)} %slice.27), channel_id=1, source_target_pairs={{0,2},{1,3},{4,6},{5,7},{8,10},{9,11},{12,14},{13,15},{16,18},{17,... | collective-permute-start | bytes 1572872 | tf_op jit(solution)/shard_map/ppermute | solution.py:422
  56.4 30.9 %copy-start.6 = (f32[2048,128]{1,0:T(8,128)S(1)}, f32[2048,128]{1,0:T(8,128)}, u32[]{:S(2)}) copy-start(f32[2048,128]{1,0:T(8,128)} %get-tuple-element.50) | copy-start | bytes 3145732
  59.1 20.4 %collective-permute-start.11 = (f32[2048,128]{1,0:T(8,128)S(1)}, f32[2048,128]{1,0:T(8,128)S(1)}, u32[]{:S(2)}, u32[]{:S(2)}) collective-permute-start(f32[2048,128]{1,0:T(8,128)S(1)} %get-tuple-element.63.rows_mine), channel_id=1, source_target_pairs={{0,1},{1,0},{2,3},{3,2},{4,5},{5,4},{6,7},{7,6},{8,9},{9,8},{10,11... | collective-permute-start | bytes 3145736 | tf_op jit(solution)/shard_map/ppermute | solution.py:422
  60.0 17.9 %collective-permute-start.12 = (f32[1024,128]{1,0:T(8,128)S(1)}, f32[1024,128]{1,0:T(8,128)S(1)}, u32[]{:S(2)}, u32[]{:S(2)}) collective-permute-start(f32[1024,128]{1,0:T(8,128)S(1)} %get-tuple-element.52), channel_id=1, source_target_pairs={{0,8},{1,9},{2,10},{3,11},{4,12},{5,13},{6,14},{7,15},{10,26},{11,... | collective-permute-start | bytes 1572872 | tf_op jit(solution)/shard_map/ppermute | solution.py:422
  61.9 39.7 %collective-permute-start.15 = (f32[2048,128]{1,0:T(8,128)}, f32[2048,128]{1,0:T(8,128)}, u32[]{:S(2)}, u32[]{:S(2)}) collective-permute-start(f32[2048,128]{1,0:T(8,128)} %get-tuple-element.58.rest_1_), channel_id=1, source_target_pairs={{9,12},{11,14},{12,9},{14,11},{17,20},{20,17},{25,28},{27,30},{28,... | collective-permute-start | bytes 3145736 | tf_op jit(solution)/shard_map/ppermute | solution.py:422
  64.9 36.7 %collective-permute-start.14 = (f32[2048,128]{1,0:T(8,128)}, f32[2048,128]{1,0:T(8,128)}, u32[]{:S(2)}, u32[]{:S(2)}) collective-permute-start(f32[2048,128]{1,0:T(8,128)} %get-tuple-element.58.rest_1_), channel_id=1, source_target_pairs={{0,4},{1,5},{2,6},{3,7},{4,0},{5,1},{6,2},{7,3},{8,12},{9,8},{10,1... | collective-permute-start | bytes 3145736 | tf_op jit(solution)/shard_map/ppermute | solution.py:422
  65.0 22.3 %collective-permute-start.13 = (f32[1024,128]{1,0:T(8,128)S(1)}, f32[1024,128]{1,0:T(8,128)S(1)}, u32[]{:S(2)}, u32[]{:S(2)}) collective-permute-start(f32[1024,128]{1,0:T(8,128)S(1)} %get-tuple-element.55), channel_id=1, source_target_pairs={{0,8},{1,9},{2,10},{3,11},{4,12},{5,13},{6,14},{7,15},{10,26},{11,... | collective-permute-start | bytes 1572872 | tf_op jit(solution)/shard_map/ppermute | solution.py:422
  78.8 10.9 %collective-permute-start.17 = (f32[1024,128]{1,0:T(8,128)}, f32[1024,128]{1,0:T(8,128)S(1)}, u32[]{:S(2)}, u32[]{:S(2)}) collective-permute-start(f32[1024,128]{1,0:T(8,128)} %slice_select_fusion.1.rest_4_), channel_id=1, source_target_pairs={{9,12},{12,9},{17,20},{19,22},{20,17},{22,19},{25,28},{27,30},{28,... | collective-permute-start | bytes 1572872 | tf_op jit(solution)/shard_map/ppermute | solution.py:422
  79.5 22.1 %collective-permute-start.16 = (f32[1024,128]{1,0:T(8,128)}, f32[1024,128]{1,0:T(8,128)}, u32[]{:S(2)}, u32[]{:S(2)}) collective-permute-start(f32[1024,128]{1,0:T(8,128)} %slice_select_fusion.1.rest_4_), channel_id=1, source_target_pairs={{0,4},{1,5},{2,6},{3,7},{4,0},{5,1},{6,2},{7,3},{8,12},{9,8},{10,1... | collective-permute-start | bytes 1572872 | tf_op jit(solution)/shard_map/ppermute | solution.py:422
  86.4 1.0 copy-start.1
  88.2 28.4 %collective-permute-start.19 = (f32[1024,128]{1,0:T(8,128)}, f32[1024,128]{1,0:T(8,128)}, u32[]{:S(2)}, u32[]{:S(2)}) collective-permute-start(f32[1024,128]{1,0:T(8,128)} %slice_select_fusion.rest_4_), channel_id=1, source_target_pairs={{9,12},{12,9},{17,20},{19,22},{20,17},{22,19},{25,28},{27,30},{28,... | collective-permute-start | bytes 1572872 | tf_op jit(solution)/shard_map/ppermute | solution.py:422
  89.6 0.8 copy-start.3
  90.4 26.1 %collective-permute-start.18 = (f32[1024,128]{1,0:T(8,128)}, f32[1024,128]{1,0:T(8,128)}, u32[]{:S(2)}, u32[]{:S(2)}) collective-permute-start(f32[1024,128]{1,0:T(8,128)} %slice_select_fusion.rest_4_), channel_id=1, source_target_pairs={{0,4},{1,5},{2,6},{3,7},{4,0},{5,1},{6,2},{7,3},{8,12},{9,8},{10,1... | collective-permute-start | bytes 1572872 | tf_op jit(solution)/shard_map/ppermute | solution.py:422
  101.7 3.4 %copy-start = (f32[4,1,256,8,1,256]{5,4,3,2,1,0:T(1,128)S(1)}, f32[4,1,256,8,1,256]{5,4,3,2,1,0:T(1,128)}, u32[]{:S(2)}) copy-start(f32[4,1,256,8,1,256]{5,4,3,2,1,0:T(1,128)} %param.1) | copy-start | bytes 25165828
  105.0 1.2 copy-start.2
  106.3 1.0 copy-start.4

commit v4 on v2

--- a/solution.py
+++ b/solution.py
@@ -330,28 +330,53 @@
     )(place, rows_mine, rows_other, inverse)
 
 
-def load_columns(place_ref, pieces, offsets, columns, tile, count):
+def load_columns(choices, pieces, columns, tile, count):
     per = tile // LANES
     depth = 2 * tile
-    for stage in range(2):
-        for panel in range(2):
-            for which, ref in enumerate(pieces[stage]):
-
-                @pl.when(place_ref[3 + 2 * stage + panel] == which)
-                def _(stage=stage, panel=panel, ref=ref):
-                    for i in range(count):
-                        for h in range(per):
-                            start = offsets[stage] + i * tile * per + h
-                            high, low = halves(ref[pl.ds(start, tile, stride=per), :])
-                            at = ((stage * count + i) * per + h) * LANES
-                            for copy, value in enumerate((high, high, low)):
-                                row = copy * depth + panel * tile
-                                columns[row : row + tile, at : at + LANES] = value
-
-
-def trailing_kernel(tile, group, count, offsets, place_ref, block_ref, weights_ref, *rest):
+    for panel in range(2):
+        for which, ref in enumerate(pieces):
+
+            @pl.when(choices[panel] == which)
+            def _(panel=panel, ref=ref):
+                for i in range(count):
+                    for h in range(per):
+                        high, low = halves(ref[pl.ds(i * tile * per + h, tile, stride=per), :])
+                        at = (i * per + h) * LANES
+                        for copy, value in enumerate((high, high, low)):
+                            row = copy * depth + panel * tile
+                            columns[row : row + tile, at : at + LANES] = value
+
+
+def products_kernel(tile, count, place_ref, weights_ref, piece_a, piece_b, piece_c, out_ref, columns):
+    @pl.when(pl.program_id(0) == 0)
+    def _():
+        load_columns((place_ref[3], place_ref[4]), (piece_a, piece_b, piece_c), columns, tile, count)
+
+    for i in range(count):
+        at = i * tile
+        out_ref[:, at : at + tile] = product(weights_ref[...], columns[:, at : at + tile], ((1,), (0,)))
+
+
+def first_products(place, weights, pieces, row_tiles, tile):
+    depth = weights.shape[1]
+    vmem = pl.BlockSpec(memory_space=pltpu.VMEM)
+    count = pieces[0].shape[0] * LANES // tile // tile
+    return pl.pallas_call(
+        functools.partial(products_kernel, tile, count),
+        grid=(row_tiles,),
+        out_shape=jax.ShapeDtypeStruct((row_tiles * tile, count * tile), F32),
+        in_specs=[pl.BlockSpec(memory_space=pltpu.SMEM), pl.BlockSpec((tile, depth), lambda a: (a, 0))] + [vmem] * 3,
+        out_specs=pl.BlockSpec((tile, count * tile), lambda a: (a, 0)),
+        scratch_shapes=[pltpu.VMEM((depth, count * tile), BF16)],
+        compiler_params=pltpu.CompilerParams(vmem_limit_bytes=24 * 1024 * 1024),
+        cost_estimate=COST,
+        name="first_products",
+    )(place, weights, *pieces)
+
+
+def trailing_kernel(tile, group, count, place_ref, block_ref, weights_ref, ready_ref, *rest):
     solved_ref = rest[0] if group == 0 else None
-    pieces = (rest[1:4], rest[4:7])
+    pieces = rest[1:4]
     block_out, columns = rest[-2:]
     step = pl.program_id(0)
     row, col = place_ref[0], place_ref[1]
@@ -362,7 +387,7 @@
 
     @pl.when(step == 0)
     def _():
-        load_columns(place_ref, pieces, offsets, columns, tile, count)
+        load_columns((place_ref[5], place_ref[6]), pieces, columns, tile, count)
 
     @pl.when(top)
     def _():
@@ -373,8 +398,11 @@
         for stage in range(2):
             parity = place_ref[2] if stage == 0 else 1 - place_ref[2]
             for i in range(count):
-                at = (stage * count + i) * tile
-                update = product(weights_ref[...], columns[:, at : at + tile], ((1,), (0,)))
+                at = i * tile
+                if stage == 0:
+                    update = ready_ref[:, at : at + tile]
+                else:
+                    update = product(weights_ref[...], columns[:, at : at + tile], ((1,), (0,)))
                 for h in range(per):
                     where = pl.ds((2 * i + parity) * per + h, tile, stride=GROUP)
                     out[where, :] = block[where, :] - update[:, h * LANES : (h + 1) * LANES]
@@ -387,27 +415,31 @@
                 out[pl.ds(h, tile, stride=GROUP), :] = solved_ref[:, h * LANES : (h + 1) * LANES]
 
 
-def trailing(group, place, block, weights, extra, pieces, offsets, row_tiles, col_tiles, tile):
+def trailing(group, place, block, weights, ready, extra, pieces, row_tiles, col_tiles, tile):
     per = tile // LANES
     depth = weights.shape[1]
     count = GROUP // per // 2
     view = grouped(block, row_tiles, col_tiles, tile)
     block_spec = pl.BlockSpec((tile, None, GROUP, LANES), lambda a: (a, group, 0, 0))
-    weight_spec = pl.BlockSpec((tile, depth), lambda a: (a, 0))
-    return pl.pallas_call(
-        functools.partial(trailing_kernel, tile, group, count, offsets),
+    return pl.pallas_call(
+        functools.partial(trailing_kernel, tile, group, count),
         grid=(row_tiles,),
         out_shape=jax.ShapeDtypeStruct(view.shape, F32),
-        in_specs=[pl.BlockSpec(memory_space=pltpu.SMEM), block_spec, weight_spec]
+        in_specs=[
+            pl.BlockSpec(memory_space=pltpu.SMEM),
+            block_spec,
+            pl.BlockSpec((tile, depth), lambda a: (a, 0)),
+            pl.BlockSpec((tile, count * tile), lambda a: (a, group)),
+        ]
         + [pl.BlockSpec((tile, tile), lambda a: (a, 0)) if group == 0 else pl.BlockSpec(memory_space=pl.ANY)]
-        + [pl.BlockSpec(memory_space=pltpu.VMEM)] * 6,
+        + [pl.BlockSpec(memory_space=pltpu.VMEM)] * 3,
         out_specs=block_spec,
-        scratch_shapes=[pltpu.VMEM((depth, 2 * count * tile), BF16)],
-        input_output_aliases={} if group == 0 else {3: 0},
-        compiler_params=pltpu.CompilerParams(vmem_limit_bytes=32 * 1024 * 1024),
+        scratch_shapes=[pltpu.VMEM((depth, count * tile), BF16)],
+        input_output_aliases={} if group == 0 else {4: 0},
+        compiler_params=pltpu.CompilerParams(vmem_limit_bytes=44 * 1024 * 1024),
         cost_estimate=COST,
         name="trailing_%d" % group,
-    )(place, view, weights, extra, *pieces[0], *pieces[1])
+    )(place, view, weights, ready, extra, *pieces)
 
 
 AXES = ("prow", "pcol")
@@ -461,6 +493,17 @@
     z, x, y, core = row // 2, row % 2, col // 2, col % 2
     per = tile // LANES
     block = kernel_tiles.reshape(row_tiles * tile * col_tiles * per, LANES)
+
+    first_odd = jnp.where(y == 0, (z == 1) | (z == 2), z == 3).astype(jnp.int32)
+    chosen = []
+    for stage in range(2):
+        rowwise = (z == 0) | ((y == 1) & (z == 2 - stage))
+        own = core == x
+        for panel in range(2):
+            by_row = jnp.where(x == panel, 0, 1)
+            by_col = jnp.where(own, jnp.where(core == panel, 0, 1), jnp.where(core == panel, 1, 2))
+            chosen.append(jnp.where(rowwise, by_row, by_col))
+    place = jnp.stack([row, col, jnp.where(z == 0, 0, first_odd)] + chosen).astype(jnp.int32)
 
     lead = gather_lead(block, row_tiles, col_tiles, tile)
     middle = tile * per // 2
@@ -501,25 +544,15 @@
             inverse, held = lax.optimization_barrier((inverse, held))
         last.append([held, send(held, same_core(1)), send(held, cross_core(1))])
         if part == 0:
-            place = jnp.stack([row, col, core]).astype(jnp.int32)
-            weights, solved = row_weights(place, rows_mine, rows_other, inverse, row_tiles, tile)
+            weights, solved = row_weights(
+                jnp.stack([row, col, core]).astype(jnp.int32), rows_mine, rows_other, inverse, row_tiles, tile
+            )
             weights, near[1] = lax.optimization_barrier((weights, near[1]))
 
-    first_odd = jnp.where(y == 0, (z == 1) | (z == 2), z == 3).astype(jnp.int32)
-    chosen = []
-    for stage in range(2):
-        rowwise = (z == 0) | ((y == 1) & (z == 2 - stage))
-        own = core == x
-        for panel in range(2):
-            by_row = jnp.where(x == panel, 0, 1)
-            by_col = jnp.where(own, jnp.where(core == panel, 0, 1), jnp.where(core == panel, 1, 2))
-            chosen.append(jnp.where(rowwise, by_row, by_col))
-    place = jnp.stack([row, col, jnp.where(z == 0, 0, first_odd)] + chosen).astype(jnp.int32)
+    ready = first_products(place, weights, first, row_tiles, tile)
     result = solved
     for part in range(2):
-        result = trailing(
-            part, place, block, weights, result, (first, last[part]), (part * split, 0), row_tiles, col_tiles, tile
-        )
+        result = trailing(part, place, block, weights, ready, result, last[part], row_tiles, col_tiles, tile)
     return result.reshape(kernel_tiles.shape)
 
 
@@ -551,10 +584,10 @@
     place = jnp.stack([row, col, zero, zero, zero + 1, zero, zero + 1]).astype(jnp.int32)
     weights, result = row_weights(place, rows[0], rows[1], inverse, row_tiles, tile)
     split = even.shape[0] // 2
+    ready = first_products(place, weights, pieces[0], row_tiles, tile)
     for part in range(2):
-        result = trailing(
-            part, place, block, weights, result, pieces, (part * split,) * 2, row_tiles, col_tiles, tile
-        )
+        last = [piece[part * split : (part + 1) * split] for piece in pieces[1]]
+        result = trailing(part, place, block, weights, ready, result, last, row_tiles, col_tiles, tile)
     return result.reshape(kernel_tiles.shape)
 
 

time: 123 us -> 118 us (0.959)
  the two profiles are of different devices: /device:TPU:16 before, /device:TPU:5 now
where the time goes in v4:
time: 118 us
  Pallas kernels  54.9 us (47%)
  starting transfers between devices  35.5 us (30%)
  waiting for transfers between devices  18.6 us (16%)
  other arithmetic  5.05 us (4%)
  local copies, waits for them, and re-layouts  3.44 us (3%)
    ppermute x18, starting transfers between devices, send(): return lax.ppermute(value, AXES, pairs)  35.5 us
    ppermute x18, waiting for transfers between devices, send(): return lax.ppermute(value, AXES, pairs)  18.6 us
    pallas_call x2, Pallas kernels, trailing(): pl.pallas_call(functools.partial(trailing_kernel, tile, group, count), gr...  12.9 us
    pallas_call x1, Pallas kernels, corner_start(): pl.pallas_call(corner_start_kernel, out_shape=jax.ShapeDtypeStruct((width...  11.4 us
    pallas_call x1, Pallas kernels, corner_end(): pl.pallas_call(corner_end_kernel, out_shape=jax.ShapeDtypeStruct(state.sh...  10.3 us
    pallas_call x1, Pallas kernels, gather_pieces(): pl.pallas_call(functools.partial(gather_kernel, tile, col_tiles, row_tile...  6.46 us
    pallas_call x1, Pallas kernels, first_products(): pl.pallas_call(functools.partial(products_kernel, tile, count), grid=(row...  6.35 us
    pallas_call x1, Pallas kernels, row_weights(): pl.pallas_call(functools.partial(weights_kernel, tile), grid=(row_tiles,)...  5.37 us
  transfers between devices with their start and end apart: 18, of which 9 were waited for; matrix products, arithmetic and copies ran while one was open for 2% of the time, Pallas kernels for 39%

profile of v4, /device:TPU:5, one launch (start us, length us, event | category | flops | bytes accessed | tf_op | source)
XLA Modules:
  0.0 117.7 jit_solution(16163071142389491291)
XLA Ops:
  0.0 2.1 %gather_lead.1.lead_ref = f32[512,128]{1,0:T(8,128)} custom-call(f32[1024,2,8,128]{3,2,1,0:T(8,128)} %bitcast.13), custom_call_target="tpu_custom_call" | custom-call | flops 1000 | bytes 1000 | tf_op jit(solution)/shard_map/gather_lead/pallas_call | solution.py:227
  2.1 1.3 %collective-permute-start = (f32[512,128]{1,0:T(8,128)}, f32[512,128]{1,0:T(8,128)S(1)}, u32[]{:S(2)}, u32[]{:S(2)}) collective-permute-start(f32[512,128]{1,0:T(8,128)} %gather_lead.1.lead_ref), channel_id=1, source_target_pairs={{0,2},{1,3},{4,6},{5,7},{8,10},{9,11},{12,14},{13,15},{16,18},{17,... | collective-permute-start | bytes 786440 | tf_op jit(solution)/shard_map/ppermute | solution.py:454
  3.4 6.5 %gather_pieces.1 = (f32[1536,128]{1,0:T(8,128)}, f32[2048,128]{1,0:T(8,128)}, f32[2048,128]{1,0:T(8,128)}, f32[2048,128]{1,0:T(8,128)}) custom-call(s32[1]{0:T(128)} %bitcast.9.place_ref, f32[512,128]{1,0:T(8,128)} %gather_lead.1.lead_ref, f32[1024,2,8,128]{3,2,1,0:T(8,128)} %bitcast.14, f32[16384,128]{1,0:T(8,128)} %bitcast.15), custom_call_target="tpu_custom_call" | custom-call | flops 1000 | bytes 1000 | tf_op jit(solution)/shard_map/gather_pieces/pallas_call | solution.py:244
  9.8 1.5 %collective-permute-done = f32[512,128]{1,0:T(8,128)S(1)} collective-permute-done((f32[512,128]{1,0:T(8,128)}, f32[512,128]{1,0:T(8,128)S(1)}, u32[]{:S(2)}, u32[]{:S(2)}) %collective-permute-start) | collective-permute-done | bytes 262176 | tf_op jit(solution)/shard_map/ppermute | solution.py:454
  11.4 4.2 %collective-permute-start.1 = (f32[256,128]{1,0:T(8,128)S(1)}, f32[256,128]{1,0:T(8,128)S(1)}, u32[]{:S(2)}, u32[]{:S(2)}) collective-permute-start(f32[256,128]{1,0:T(8,128)S(1)} %slice_select_fusion.2), channel_id=1, source_target_pairs={{0,16},{1,17},{2,18},{3,19},{4,20},{5,21},{6,22},{7,23}} | collective-permute-start | bytes 393224 | tf_op jit(solution)/shard_map/ppermute | solution.py:454
  15.6 1.9 %collective-permute-done.1 = f32[256,128]{1,0:T(8,128)S(1)} collective-permute-done((f32[256,128]{1,0:T(8,128)S(1)}, f32[256,128]{1,0:T(8,128)S(1)}, u32[]{:S(2)}, u32[]{:S(2)}) %collective-permute-start.1) | collective-permute-done | bytes 131104 | tf_op jit(solution)/shard_map/ppermute | solution.py:454
  17.5 1.3 %collective-permute-start.2 = (f32[256,128]{1,0:T(8,128)S(1)}, f32[256,128]{1,0:T(8,128)S(1)}, u32[]{:S(2)}, u32[]{:S(2)}) collective-permute-start(f32[256,128]{1,0:T(8,128)S(1)} %broadcast_select_fusion.1), channel_id=1, source_target_pairs={{0,8},{1,9},{2,10},{3,11},{4,12},{5,13},{6,14},{7,15},{16,24},{17,... | collective-permute-start | bytes 393224 | tf_op jit(solution)/shard_map/ppermute | solution.py:454
  18.9 2.0 %collective-permute-done.2 = f32[256,128]{1,0:T(8,128)S(1)} collective-permute-done((f32[256,128]{1,0:T(8,128)S(1)}, f32[256,128]{1,0:T(8,128)S(1)}, u32[]{:S(2)}, u32[]{:S(2)}) %collective-permute-start.2) | collective-permute-done | bytes 131104 | tf_op jit(solution)/shard_map/ppermute | solution.py:454
  20.9 4.6 %collective-permute-start.7 = (f32[2048,128]{1,0:T(8,128)}, f32[2048,128]{1,0:T(8,128)S(1)}, u32[]{:S(2)}, u32[]{:S(2)}) collective-permute-start(f32[2048,128]{1,0:T(8,128)} %get-tuple-element.33), channel_id=1, source_target_pairs={{0,24},{1,25},{2,18},{3,19},{4,28},{5,29},{6,22},{7,23},{16,8},{17... | collective-permute-start | bytes 3145736 | tf_op jit(solution)/shard_map/ppermute | solution.py:454
  25.5 3.1 %collective-permute-start.5 = (f32[256,128]{1,0:T(8,128)S(1)}, f32[256,128]{1,0:T(8,128)S(1)}, u32[]{:S(2)}, u32[]{:S(2)}) collective-permute-start(f32[256,128]{1,0:T(8,128)S(1)} %broadcast_select_fusion.2), channel_id=1, source_target_pairs={{0,6},{1,7},{2,4},{3,5},{4,2},{5,3},{6,0},{7,1},{8,14},{9,15},{10,... | collective-permute-start | bytes 393224 | tf_op jit(solution)/shard_map/ppermute | solution.py:454
  28.7 0.3 collective-permute-start.3
  28.9 0.1 collective-permute-start.4
  29.0 2.0 %collective-permute-done.5 = f32[256,128]{1,0:T(8,128)S(1)} collective-permute-done((f32[256,128]{1,0:T(8,128)S(1)}, f32[256,128]{1,0:T(8,128)S(1)}, u32[]{:S(2)}, u32[]{:S(2)}) %collective-permute-start.5) | collective-permute-done | bytes 131104 | tf_op jit(solution)/shard_map/ppermute | solution.py:454
  31.0 1.3 %collective-permute-start.8 = (f32[1536,128]{1,0:T(8,128)}, f32[1536,128]{1,0:T(8,128)S(1)}, u32[]{:S(2)}, u32[]{:S(2)}) collective-permute-start(f32[1536,128]{1,0:T(8,128)} %get-tuple-element.37), channel_id=1, source_target_pairs={{0,2},{1,3},{4,6},{5,7},{8,10},{9,11},{12,14},{13,15},{16,18},{17,... | collective-permute-start | bytes 2359304 | tf_op jit(solution)/shard_map/ppermute | solution.py:454
  32.3 0.4 collective-permute-done.3
  32.7 0.0 collective-permute-done.4
  32.8 6.4 %collective-permute-start.6 = (f32[1024,128]{1,0:T(8,128)S(1)}, f32[1024,128]{1,0:T(8,128)S(1)}, u32[]{:S(2)}, u32[]{:S(2)}) collective-permute-start(f32[1024,128]{1,0:T(8,128)S(1)} %constant_dynamic-update-slice_fusion.mine_ref), channel_id=1, source_target_pairs={{0,1},{1,0},{2,3},{3,2},{4,5},{5,4},{6,7},{7,6},{8,9},{9,8},{10,11... | collective-permute-start | bytes 1572872 | tf_op jit(solution)/shard_map/ppermute | solution.py:454
  39.2 0.1 pad_add_fusion.1.place_ref
  39.3 1.4 %collective-permute-done.6.other_ref = f32[1024,128]{1,0:T(8,128)S(1)} collective-permute-done((f32[1024,128]{1,0:T(8,128)S(1)}, f32[1024,128]{1,0:T(8,128)S(1)}, u32[]{:S(2)}, u32[]{:S(2)}) %collective-permute-start.6) | collective-permute-done | bytes 524320 | tf_op jit(solution)/shard_map/ppermute | solution.py:454
  40.7 11.4 %corner_start.1.state_ref = f32[512,512]{1,0:T(8,128)S(1)} custom-call(s32[3]{0:T(128)S(1)} %pad_add_fusion.1.place_ref, f32[1024,128]{1,0:T(8,128)S(1)} %constant_dynamic-update-slice_fusion.mine_ref, f32[1024,128]{1,0:T(8,128)S(1)} %collective-permute-done.6.other_ref), custom_call_target="tpu_custom_call" | custom-call | flops 1000 | bytes 1000 | tf_op jit(solution)/shard_map/corner_start/pallas_call | solution.py:150
  52.2 0.0 collective-permute-done.7
  52.2 0.1 constant_dynamic-update-slice_fusion.4
  52.3 3.1 %select_select_fusion = (f32[2048,128]{1,0:T(8,128)S(1)}, f32[2048,128]{1,0:T(8,128)}, f32[2048,128]{1,0:T(8,128)S(1)}) fusion(f32[2048,128]{1,0:T(8,128)} %get-tuple-element.42, f32[2048,128]{1,0:T(8,128)S(1)} %constant_dynamic-update-slice_fusion.4, f32[2048,128]{1,0:T(8,128)S(1)} %collective-permute-done.7, f32[2048,128]{1,0:T(8,128)} %get-tuple-element.33, ...), kind=kLoop, calls=%fused_computation | loop fusion | flops 2097152 | bytes 8388612 | tf_op jit(solution)/shard_map/jit(_where)/select_n | solution.py:531
  55.4 2.3 %collective-permute-start.9 = (f32[2048,128]{1,0:T(8,128)S(1)}, f32[2048,128]{1,0:T(8,128)S(1)}, u32[]{:S(2)}, u32[]{:S(2)}) collective-permute-start(f32[2048,128]{1,0:T(8,128)S(1)} %get-tuple-element.55.rows_mine), channel_id=1, source_target_pairs={{0,1},{1,0},{2,3},{3,2},{4,5},{5,4},{6,7},{7,6},{8,9},{9,8},{10,11... | collective-permute-start | bytes 3145736 | tf_op jit(solution)/shard_map/ppermute | solution.py:454
  57.7 0.1 fusion
  57.8 1.3 %collective-permute-start.10 = (f32[1024,128]{1,0:T(8,128)S(1)}, f32[1024,128]{1,0:T(8,128)S(1)}, u32[]{:S(2)}, u32[]{:S(2)}) collective-permute-start(f32[1024,128]{1,0:T(8,128)S(1)} %get-tuple-element.44), channel_id=1, source_target_pairs={{0,8},{1,9},{2,10},{3,11},{4,12},{5,13},{6,14},{7,15},{10,26},{11,... | collective-permute-start | bytes 1572872 | tf_op jit(solution)/shard_map/ppermute | solution.py:454
  59.1 0.7 collective-permute-start.13
  59.8 4.0 %collective-permute-start.11 = (f32[1024,128]{1,0:T(8,128)S(1)}, f32[1024,128]{1,0:T(8,128)S(1)}, u32[]{:S(2)}, u32[]{:S(2)}) collective-permute-start(f32[1024,128]{1,0:T(8,128)S(1)} %get-tuple-element.47), channel_id=1, source_target_pairs={{0,8},{1,9},{2,10},{3,11},{4,12},{5,13},{6,14},{7,15},{10,26},{11,... | collective-permute-start | bytes 1572872 | tf_op jit(solution)/shard_map/ppermute | solution.py:454
  63.8 0.1 pad_add_fusion.place_ref
  63.9 0.2 collective-permute-start.12
  64.1 10.3 %corner_end.1.inverse_ref = f32[512,512]{1,0:T(8,128)S(1)} custom-call(f32[512,512]{1,0:T(8,128)S(1)} %corner_start.1.state_ref), custom_call_target="tpu_custom_call" | custom-call | flops 1000 | bytes 1000 | tf_op jit(solution)/shard_map/corner_end/pallas_call | solution.py:163
  74.4 0.9 slice_select_fusion.1.rest_1_
  75.2 1.5 %collective-permute-start.15 = (f32[1024,128]{1,0:T(8,128)}, f32[1024,128]{1,0:T(8,128)}, u32[]{:S(2)}, u32[]{:S(2)}) collective-permute-start(f32[1024,128]{1,0:T(8,128)} %slice_select_fusion.1.rest_1_), channel_id=1, source_target_pairs={{9,12},{12,9},{17,20},{19,22},{20,17},{22,19},{25,28},{27,30},{28,... | collective-permute-start | bytes 1572872 | tf_op jit(solution)/shard_map/ppermute | solution.py:454
  76.7 1.4 %collective-permute-start.14 = (f32[1024,128]{1,0:T(8,128)}, f32[1024,128]{1,0:T(8,128)}, u32[]{:S(2)}, u32[]{:S(2)}) collective-permute-start(f32[1024,128]{1,0:T(8,128)} %slice_select_fusion.1.rest_1_), channel_id=1, source_target_pairs={{0,4},{1,5},{2,6},{3,7},{4,0},{5,1},{6,2},{7,3},{8,12},{9,8},{10,1... | collective-permute-start | bytes 1572872 | tf_op jit(solution)/shard_map/ppermute | solution.py:454
  78.2 5.4 %row_weights.1 = (bf16[1024,1536]{1,0:T(8,128)(2,1)S(1)}, f32[1024,256]{1,0:T(8,128)S(1)}) custom-call(s32[3]{0:T(128)S(1)} %pad_add_fusion.place_ref, f32[2048,128]{1,0:T(8,128)S(1)} %get-tuple-element.55.rows_mine, f32[2048,128]{1,0:T(8,128)S(1)} %collective-permute-done.9.rows_other, f32[512,512]{1,0:T(8,128)S(1)} %corner_end.1.inverse_ref), custom_call_target="tpu_custom_call" | custom-call | flops 1000 | bytes 1000 | tf_op jit(solution)/shard_map/row_weights/pallas_call | solution.py:315
  83.5 0.9 copy-done
  84.5 0.9 slice_select_fusion.rest_1_
  85.3 1.5 %collective-permute-start.17 = (f32[1024,128]{1,0:T(8,128)}, f32[1024,128]{1,0:T(8,128)}, u32[]{:S(2)}, u32[]{:S(2)}) collective-permute-start(f32[1024,128]{1,0:T(8,128)} %slice_select_fusion.rest_1_), channel_id=1, source_target_pairs={{9,12},{12,9},{17,20},{19,22},{20,17},{22,19},{25,28},{27,30},{28,... | collective-permute-start | bytes 1572872 | tf_op jit(solution)/shard_map/ppermute | solution.py:454
  86.8 1.0 copy-done.2
  87.8 0.0 collective-permute-start.16
  87.8 0.1 stack.47.place_ref
  87.9 1.6 %collective-permute-done.12.piece_b = f32[2048,128]{1,0:T(8,128)} collective-permute-done((f32[2048,128]{1,0:T(8,128)}, f32[2048,128]{1,0:T(8,128)}, u32[]{:S(2)}, u32[]{:S(2)}) %collective-permute-start.12) | collective-permute-done | bytes 1048608 | tf_op jit(solution)/shard_map/ppermute | solution.py:454
  89.5 1.2 %copy-done.3 = f32[2048,128]{1,0:T(8,128)S(1)} copy-done((f32[2048,128]{1,0:T(8,128)S(1)}, f32[2048,128]{1,0:T(8,128)}, u32[]{:S(2)}) %copy-start.3) | copy-done | bytes 1048600
  90.7 6.4 %first_products.1.ready_ref = f32[1024,1024]{1,0:T(8,128)S(1)} custom-call(s32[7]{0:T(128)S(1)} %stack.47.place_ref, bf16[1024,1536]{1,0:T(8,128)(2,1)S(1)} %get-tuple-element.48.weights_ref, f32[2048,128]{1,0:T(8,128)} %get-tuple-element.49.piece_a, f32[2048,128]{1,0:T(8,128)} %collective-permute-done.12.piece_b, f32[2048,128]{1,0:T(8,128)S(1)} %copy-done.3), custom_call_target="tpu_custom_call" | custom-call | flops 1000 | bytes 1000 | tf_op jit(solution)/shard_map/first_products/pallas_call | solution.py:364
  97.1 3.6 %collective-permute-done.14.rest_2_ = f32[1024,128]{1,0:T(8,128)} collective-permute-done((f32[1024,128]{1,0:T(8,128)}, f32[1024,128]{1,0:T(8,128)}, u32[]{:S(2)}, u32[]{:S(2)}) %collective-permute-start.14) | collective-permute-done | bytes 524320 | tf_op jit(solution)/shard_map/ppermute | solution.py:454
  100.8 6.5 %trailing_0.1.rest_0_ = f32[1024,2,8,128]{3,2,1,0:T(8,128)} custom-call(s32[7]{0:T(128)S(1)} %stack.47.place_ref, f32[1024,2,8,128]{3,2,1,0:T(8,128)} %bitcast.16, bf16[1024,1536]{1,0:T(8,128)(2,1)S(1)} %get-tuple-element.48.weights_ref, f32[1024,1024]{1,0:T(8,128)S(1)} %first_products.1.ready_ref, f32[1024,256]{1,0:T(8,128)S(1)} %copy-done.1, ...), custom_call_target="tpu_custom_call" | custom-call | flops 1000 | bytes 1000 | tf_op jit(solution)/shard_map/trailing_0/pallas_call | solution.py:424
  107.2 4.0 %collective-permute-done.16.rest_2_ = f32[1024,128]{1,0:T(8,128)} collective-permute-done((f32[1024,128]{1,0:T(8,128)}, f32[1024,128]{1,0:T(8,128)}, u32[]{:S(2)}, u32[]{:S(2)}) %collective-permute-start.16) | collective-permute-done | bytes 524320 | tf_op jit(solution)/shard_map/ppermute | solution.py:454
  111.2 6.5 %trailing_1.1 = f32[1024,2,8,128]{3,2,1,0:T(8,128)} custom-call(s32[7]{0:T(128)S(1)} %stack.47.place_ref, f32[1024,2,8,128]{3,2,1,0:T(8,128)} %bitcast.17, bf16[1024,1536]{1,0:T(8,128)(2,1)S(1)} %get-tuple-element.48.weights_ref, f32[1024,1024]{1,0:T(8,128)S(1)} %first_products.1.ready_ref, ...), custom_call_target="tpu_custom_call", output_to_operand_aliasing={{}: (4, {})} | custom-call | flops 1000 | bytes 1000 | tf_op jit(solution)/shard_map/trailing_1/pallas_call | solution.py:424
  (24 shorter events, 0.1 us)
Async XLA Ops:
  2.1 9.3 %collective-permute-start = (f32[512,128]{1,0:T(8,128)}, f32[512,128]{1,0:T(8,128)S(1)}, u32[]{:S(2)}, u32[]{:S(2)}) collective-permute-start(f32[512,128]{1,0:T(8,128)} %gather_lead.1.lead_ref), channel_id=1, source_target_pairs={{0,2},{1,3},{4,6},{5,7},{8,10},{9,11},{12,14},{13,15},{16,18},{17,... | collective-permute-start | bytes 786440 | tf_op jit(solution)/shard_map/ppermute | solution.py:454
  3.4 8.0 %copy-start.5 = (f32[512,128]{1,0:T(8,128)S(1)}, f32[512,128]{1,0:T(8,128)}, u32[]{:S(2)}) copy-start(f32[512,128]{1,0:T(8,128)} %gather_lead.1.lead_ref) | copy-start | bytes 786436
  11.4 6.2 %collective-permute-start.1 = (f32[256,128]{1,0:T(8,128)S(1)}, f32[256,128]{1,0:T(8,128)S(1)}, u32[]{:S(2)}, u32[]{:S(2)}) collective-permute-start(f32[256,128]{1,0:T(8,128)S(1)} %slice_select_fusion.2), channel_id=1, source_target_pairs={{0,16},{1,17},{2,18},{3,19},{4,20},{5,21},{6,22},{7,23}} | collective-permute-start | bytes 393224 | tf_op jit(solution)/shard_map/ppermute | solution.py:454
  17.5 3.4 %collective-permute-start.2 = (f32[256,128]{1,0:T(8,128)S(1)}, f32[256,128]{1,0:T(8,128)S(1)}, u32[]{:S(2)}, u32[]{:S(2)}) collective-permute-start(f32[256,128]{1,0:T(8,128)S(1)} %broadcast_select_fusion.1), channel_id=1, source_target_pairs={{0,8},{1,9},{2,10},{3,11},{4,12},{5,13},{6,14},{7,15},{16,24},{17,... | collective-permute-start | bytes 393224 | tf_op jit(solution)/shard_map/ppermute | solution.py:454
  20.9 31.3 %collective-permute-start.7 = (f32[2048,128]{1,0:T(8,128)}, f32[2048,128]{1,0:T(8,128)S(1)}, u32[]{:S(2)}, u32[]{:S(2)}) collective-permute-start(f32[2048,128]{1,0:T(8,128)} %get-tuple-element.33), channel_id=1, source_target_pairs={{0,24},{1,25},{2,18},{3,19},{4,28},{5,29},{6,22},{7,23},{16,8},{17... | collective-permute-start | bytes 3145736 | tf_op jit(solution)/shard_map/ppermute | solution.py:454
  25.5 5.5 %collective-permute-start.5 = (f32[256,128]{1,0:T(8,128)S(1)}, f32[256,128]{1,0:T(8,128)S(1)}, u32[]{:S(2)}, u32[]{:S(2)}) collective-permute-start(f32[256,128]{1,0:T(8,128)S(1)} %broadcast_select_fusion.2), channel_id=1, source_target_pairs={{0,6},{1,7},{2,4},{3,5},{4,2},{5,3},{6,0},{7,1},{8,14},{9,15},{10,... | collective-permute-start | bytes 393224 | tf_op jit(solution)/shard_map/ppermute | solution.py:454
  28.7 4.0 %collective-permute-start.3 = (f32[256,128]{1,0:T(8,128)S(1)}, f32[256,128]{1,0:T(8,128)S(1)}, u32[]{:S(2)}, u32[]{:S(2)}) collective-permute-start(f32[256,128]{1,0:T(8,128)S(1)} %broadcast_select_fusion.2), channel_id=1, source_target_pairs={{0,4},{1,5},{2,6},{3,7},{4,0},{5,1},{6,2},{7,3},{8,12},{9,13},{10,... | collective-permute-start | bytes 393224 | tf_op jit(solution)/shard_map/ppermute | solution.py:454
  28.9 3.8 %collective-permute-start.4 = (f32[256,128]{1,0:T(8,128)S(1)}, f32[256,128]{1,0:T(8,128)S(1)}, u32[]{:S(2)}, u32[]{:S(2)}) collective-permute-start(f32[256,128]{1,0:T(8,128)S(1)} %broadcast_select_fusion.2), channel_id=1, source_target_pairs={{0,2},{1,3},{2,0},{3,1},{4,6},{5,7},{6,4},{7,5},{8,10},{9,11},{10,... | collective-permute-start | bytes 393224 | tf_op jit(solution)/shard_map/ppermute | solution.py:454
  31.0 21.2 %collective-permute-start.8 = (f32[1536,128]{1,0:T(8,128)}, f32[1536,128]{1,0:T(8,128)S(1)}, u32[]{:S(2)}, u32[]{:S(2)}) collective-permute-start(f32[1536,128]{1,0:T(8,128)} %get-tuple-element.37), channel_id=1, source_target_pairs={{0,2},{1,3},{4,6},{5,7},{8,10},{9,11},{12,14},{13,15},{16,18},{17,... | collective-permute-start | bytes 2359304 | tf_op jit(solution)/shard_map/ppermute | solution.py:454
  32.8 8.0 %collective-permute-start.6 = (f32[1024,128]{1,0:T(8,128)S(1)}, f32[1024,128]{1,0:T(8,128)S(1)}, u32[]{:S(2)}, u32[]{:S(2)}) collective-permute-start(f32[1024,128]{1,0:T(8,128)S(1)} %constant_dynamic-update-slice_fusion.mine_ref), channel_id=1, source_target_pairs={{0,1},{1,0},{2,3},{3,2},{4,5},{5,4},{6,7},{7,6},{8,9},{9,8},{10,11... | collective-permute-start | bytes 1572872 | tf_op jit(solution)/shard_map/ppermute | solution.py:454
  39.3 35.1 %copy-start.4 = (f32[2048,128]{1,0:T(8,128)S(1)}, f32[2048,128]{1,0:T(8,128)}, u32[]{:S(2)}) copy-start(f32[2048,128]{1,0:T(8,128)} %get-tuple-element.42) | copy-start | bytes 3145732
  55.4 21.3 %collective-permute-start.9 = (f32[2048,128]{1,0:T(8,128)S(1)}, f32[2048,128]{1,0:T(8,128)S(1)}, u32[]{:S(2)}, u32[]{:S(2)}) collective-permute-start(f32[2048,128]{1,0:T(8,128)S(1)} %get-tuple-element.55.rows_mine), channel_id=1, source_target_pairs={{0,1},{1,0},{2,3},{3,2},{4,5},{5,4},{6,7},{7,6},{8,9},{9,8},{10,11... | collective-permute-start | bytes 3145736 | tf_op jit(solution)/shard_map/ppermute | solution.py:454
  57.8 16.6 %collective-permute-start.10 = (f32[1024,128]{1,0:T(8,128)S(1)}, f32[1024,128]{1,0:T(8,128)S(1)}, u32[]{:S(2)}, u32[]{:S(2)}) collective-permute-start(f32[1024,128]{1,0:T(8,128)S(1)} %get-tuple-element.44), channel_id=1, source_target_pairs={{0,8},{1,9},{2,10},{3,11},{4,12},{5,13},{6,14},{7,15},{10,26},{11,... | collective-permute-start | bytes 1572872 | tf_op jit(solution)/shard_map/ppermute | solution.py:454
  59.1 27.7 %collective-permute-start.13 = (f32[2048,128]{1,0:T(8,128)}, f32[2048,128]{1,0:T(8,128)S(1)}, u32[]{:S(2)}, u32[]{:S(2)}) collective-permute-start(f32[2048,128]{1,0:T(8,128)} %get-tuple-element.49.piece_a), channel_id=1, source_target_pairs={{9,12},{11,14},{12,9},{14,11},{17,20},{20,17},{25,28},{27,30},{28,... | collective-permute-start | bytes 3145736 | tf_op jit(solution)/shard_map/ppermute | solution.py:454
  59.8 24.7 %collective-permute-start.11 = (f32[1024,128]{1,0:T(8,128)S(1)}, f32[1024,128]{1,0:T(8,128)S(1)}, u32[]{:S(2)}, u32[]{:S(2)}) collective-permute-start(f32[1024,128]{1,0:T(8,128)S(1)} %get-tuple-element.47), channel_id=1, source_target_pairs={{0,8},{1,9},{2,10},{3,11},{4,12},{5,13},{6,14},{7,15},{10,26},{11,... | collective-permute-start | bytes 1572872 | tf_op jit(solution)/shard_map/ppermute | solution.py:454
  63.9 25.6 %collective-permute-start.12 = (f32[2048,128]{1,0:T(8,128)}, f32[2048,128]{1,0:T(8,128)}, u32[]{:S(2)}, u32[]{:S(2)}) collective-permute-start(f32[2048,128]{1,0:T(8,128)} %get-tuple-element.49.piece_a), channel_id=1, source_target_pairs={{0,4},{1,5},{2,6},{3,7},{4,0},{5,1},{6,2},{7,3},{8,12},{9,8},{10,1... | collective-permute-start | bytes 3145736 | tf_op jit(solution)/shard_map/ppermute | solution.py:454
  75.2 21.9 %collective-permute-start.15 = (f32[1024,128]{1,0:T(8,128)}, f32[1024,128]{1,0:T(8,128)}, u32[]{:S(2)}, u32[]{:S(2)}) collective-permute-start(f32[1024,128]{1,0:T(8,128)} %slice_select_fusion.1.rest_1_), channel_id=1, source_target_pairs={{9,12},{12,9},{17,20},{19,22},{20,17},{22,19},{25,28},{27,30},{28,... | collective-permute-start | bytes 1572872 | tf_op jit(solution)/shard_map/ppermute | solution.py:454
  76.7 24.0 %collective-permute-start.14 = (f32[1024,128]{1,0:T(8,128)}, f32[1024,128]{1,0:T(8,128)}, u32[]{:S(2)}, u32[]{:S(2)}) collective-permute-start(f32[1024,128]{1,0:T(8,128)} %slice_select_fusion.1.rest_1_), channel_id=1, source_target_pairs={{0,4},{1,5},{2,6},{3,7},{4,0},{5,1},{6,2},{7,3},{8,12},{9,8},{10,1... | collective-permute-start | bytes 1572872 | tf_op jit(solution)/shard_map/ppermute | solution.py:454
  83.5 0.9 copy-start
  85.3 21.9 %collective-permute-start.17 = (f32[1024,128]{1,0:T(8,128)}, f32[1024,128]{1,0:T(8,128)}, u32[]{:S(2)}, u32[]{:S(2)}) collective-permute-start(f32[1024,128]{1,0:T(8,128)} %slice_select_fusion.rest_1_), channel_id=1, source_target_pairs={{9,12},{12,9},{17,20},{19,22},{20,17},{22,19},{25,28},{27,30},{28,... | collective-permute-start | bytes 1572872 | tf_op jit(solution)/shard_map/ppermute | solution.py:454
  86.8 1.0 copy-start.2
  87.8 23.4 %collective-permute-start.16 = (f32[1024,128]{1,0:T(8,128)}, f32[1024,128]{1,0:T(8,128)}, u32[]{:S(2)}, u32[]{:S(2)}) collective-permute-start(f32[1024,128]{1,0:T(8,128)} %slice_select_fusion.rest_1_), channel_id=1, source_target_pairs={{0,4},{1,5},{2,6},{3,7},{4,0},{5,1},{6,2},{7,3},{8,12},{9,8},{10,1... | collective-permute-start | bytes 1572872 | tf_op jit(solution)/shard_map/ppermute | solution.py:454
  87.9 12.9 %copy-start.1 = (f32[1024,256]{1,0:T(8,128)S(1)}, f32[1024,256]{1,0:T(8,128)}, u32[]{:S(2)}) copy-start(f32[1024,256]{1,0:T(8,128)} %copy-done) | copy-start | bytes 3145732
  89.5 1.2 %copy-start.3 = (f32[2048,128]{1,0:T(8,128)S(1)}, f32[2048,128]{1,0:T(8,128)}, u32[]{:S(2)}) copy-start(f32[2048,128]{1,0:T(8,128)} %copy-done.2) | copy-start | bytes 3145732

commit v5 on v4

--- a/solution.py
+++ b/solution.py
@@ -511,31 +511,28 @@
     rest, to_far, even, odd = gather_pieces(y.reshape(1), lead, block, row_tiles, col_tiles, tile)
     over_first, rest, to_far = lax.optimization_barrier((over_first, rest, to_far))
     half = jnp.where(y == 0, lead[:middle], over_first[middle:])
-    half = jnp.where(z == 2, send(half, lambda z, x, y, k: (2, x, y, k) if z == 0 else None), half)
-    half = jnp.where(z % 2 == 1, send(half, lambda z, x, y, k: (z + 1, x, y, k) if z % 2 == 0 else None), half)
-    half, to_far = lax.optimization_barrier((half, to_far))
+    down = [send(half, lambda z, x, y, k, to=to: (to, x, y, k) if z == 0 else None) for to in (1, 2, 3)]
+    down, to_far, rest = lax.optimization_barrier((down, to_far, rest))
     far = send(to_far, far_stage)
+    over_rest = send(rest, lambda z, x, y, k: (z, x, 1, k) if y == 0 else None)
+    half = jnp.where(z == 0, half, jnp.where(z == 1, down[0], jnp.where(z == 2, down[1], down[2])))
     beside = send(half, lambda z, x, y, k: (z, 1 - x, y, k))
     above = send(half, lambda z, x, y, k: (z, x, 1 - y, k))
     corner = send(half, lambda z, x, y, k: (z, 1 - x, 1 - y, k))
-    corner, rest = lax.optimization_barrier((corner, rest))
     mine = jnp.concatenate([half, beside, above, corner], axis=0)
-    over_rest = send(rest, lambda z, x, y, k: (z, x, 1, k) if y == 0 else None)
     other = send(mine, lambda z, x, y, k: (z, x, y, 1 - k))
-    state = corner_start(jnp.stack([core, x, y]).astype(jnp.int32), mine, other)
-
-    state, far, over_rest = lax.optimization_barrier((state, far, over_rest))
+
     over = jnp.concatenate([over_first, over_rest], axis=0)
     rows_mine = jnp.where(y == 0, to_far, over)
     first = jnp.where(z == 0, even, jnp.where(y == 0, jnp.where(z == 2, to_far, far), jnp.where(z == 2, far, over)))
     to_near = jnp.where(y == 0, jnp.where(z == 3, far, to_far), jnp.where(z == 0, odd, over))
     split = to_near.shape[0] // 2
     to_near = [to_near[:split], to_near[split:]]
-    state, first, to_near = lax.optimization_barrier((state, first, to_near))
+    mine, other, first, to_near = lax.optimization_barrier((mine, other, first, to_near))
     near = [send(to_near[0], near_stage), send(to_near[1], near_stage)]
     first = [first, send(first, same_core(0)), send(first, cross_core(0))]
     rows_other = send(rows_mine, lambda z, x, y, k: (z, x, y, 1 - k))
-    inverse = corner_end(state)
+    inverse = corner_end(corner_start(jnp.stack([core, x, y]).astype(jnp.int32), mine, other))
 
     last = []
     for part in range(2):
@@ -544,6 +541,7 @@
             inverse, held = lax.optimization_barrier((inverse, held))
         last.append([held, send(held, same_core(1)), send(held, cross_core(1))])
         if part == 0:
+            inverse, first = lax.optimization_barrier((inverse, first))
             weights, solved = row_weights(
                 jnp.stack([row, col, core]).astype(jnp.int32), rows_mine, rows_other, inverse, row_tiles, tile
             )

time: 118 us -> 130 us (1.10)
  the two profiles are of different devices: /device:TPU:5 before, /device:TPU:16 now
where the time goes in v5:
time: 130 us; the launch traced here: 129 us
  Pallas kernels  57.7 us (44%)
  starting transfers between devices  31.7 us (24%)
  waiting for transfers between devices  27.8 us (21%)
  other arithmetic  6.07 us (5%)
  local copies, waits for them, and re-layouts  5.71 us (4%)
    ppermute x19, starting transfers between devices, send(): return lax.ppermute(value, AXES, pairs)  31.7 us
    ppermute x19, waiting for transfers between devices, send(): return lax.ppermute(value, AXES, pairs)  27.8 us
    pallas_call x2, Pallas kernels, trailing(): pl.pallas_call(functools.partial(trailing_kernel, tile, group, count), gr...  14.7 us
    pallas_call x1, Pallas kernels, corner_start(): pl.pallas_call(corner_start_kernel, out_shape=jax.ShapeDtypeStruct((width...  11.6 us
    pallas_call x1, Pallas kernels, corner_end(): pl.pallas_call(corner_end_kernel, out_shape=jax.ShapeDtypeStruct(state.sh...  10.5 us
    pallas_call x1, Pallas kernels, first_products(): pl.pallas_call(functools.partial(products_kernel, tile, count), grid=(row...  6.44 us
    pallas_call x1, Pallas kernels, gather_pieces(): pl.pallas_call(functools.partial(gather_kernel, tile, col_tiles, row_tile...  6.42 us
    pallas_call x1, Pallas kernels, row_weights(): pl.pallas_call(functools.partial(weights_kernel, tile), grid=(row_tiles,)...  6.02 us
  transfers between devices with their start and end apart: 19, of which 3 were waited for; matrix products, arithmetic and copies ran while one was open for 6% of the time, Pallas kernels for 37%

profile of v5, /device:TPU:16, one launch (start us, length us, event | category | flops | bytes accessed | tf_op | source)
XLA Modules:
  0.0 129.4 jit_solution(8523212461771775747)
XLA Ops:
  0.0 2.1 %gather_lead.1.lead_ref = f32[512,128]{1,0:T(8,128)} custom-call(f32[1024,2,8,128]{3,2,1,0:T(8,128)} %bitcast.13), custom_call_target="tpu_custom_call" | custom-call | flops 1000 | bytes 1000 | tf_op jit(solution)/shard_map/gather_lead/pallas_call | solution.py:227
  2.1 3.4 %collective-permute-start = (f32[512,128]{1,0:T(8,128)}, f32[512,128]{1,0:T(8,128)S(1)}, u32[]{:S(2)}, u32[]{:S(2)}) collective-permute-start(f32[512,128]{1,0:T(8,128)} %gather_lead.1.lead_ref), channel_id=1, source_target_pairs={{0,2},{1,3},{4,6},{5,7},{8,10},{9,11},{12,14},{13,15},{16,18},{17,... | collective-permute-start | bytes 786440 | tf_op jit(solution)/shard_map/ppermute | solution.py:454
  5.5 6.4 %gather_pieces.1 = (f32[1536,128]{1,0:T(8,128)}, f32[2048,128]{1,0:T(8,128)}, f32[2048,128]{1,0:T(8,128)}, f32[2048,128]{1,0:T(8,128)}) custom-call(s32[1]{0:T(128)} %bitcast.9.place_ref, f32[512,128]{1,0:T(8,128)} %gather_lead.1.lead_ref, f32[1024,2,8,128]{3,2,1,0:T(8,128)} %bitcast.14, f32[16384,128]{1,0:T(8,128)} %bitcast.15), custom_call_target="tpu_custom_call" | custom-call | flops 1000 | bytes 1000 | tf_op jit(solution)/shard_map/gather_pieces/pallas_call | solution.py:244
  12.0 0.7 collective-permute-start.3
  12.7 1.3 collective-permute-start.2
  14.0 0.7 collective-permute-start.1
  14.6 0.0 collective-permute-done.3
  14.6 10.3 %collective-permute-done.2 = f32[256,128]{1,0:T(8,128)S(1)} collective-permute-done((f32[256,128]{1,0:T(8,128)S(1)}, f32[256,128]{1,0:T(8,128)S(1)}, u32[]{:S(2)}, u32[]{:S(2)}) %collective-permute-start.2) | collective-permute-done | bytes 131104 | tf_op jit(solution)/shard_map/ppermute | solution.py:454
  25.0 0.0 collective-permute-done.1
  25.0 3.9 %collective-permute-start.10 = (f32[2048,128]{1,0:T(8,128)}, f32[2048,128]{1,0:T(8,128)S(1)}, u32[]{:S(2)}, u32[]{:S(2)}) collective-permute-start(f32[2048,128]{1,0:T(8,128)} %get-tuple-element.37), channel_id=1, source_target_pairs={{0,24},{1,25},{2,18},{3,19},{4,28},{5,29},{6,22},{7,23},{16,8},{17... | collective-permute-start | bytes 3145736 | tf_op jit(solution)/shard_map/ppermute | solution.py:454
  28.9 1.3 %collective-permute-start.4 = (f32[1536,128]{1,0:T(8,128)}, f32[1536,128]{1,0:T(8,128)S(1)}, u32[]{:S(2)}, u32[]{:S(2)}) collective-permute-start(f32[1536,128]{1,0:T(8,128)} %get-tuple-element.38), channel_id=1, source_target_pairs={{0,2},{1,3},{4,6},{5,7},{8,10},{9,11},{12,14},{13,15},{16,18},{17,... | collective-permute-start | bytes 2359304 | tf_op jit(solution)/shard_map/ppermute | solution.py:454
  30.3 0.1 collective-permute-start.8
  30.4 2.9 %collective-permute-start.7 = (f32[256,128]{1,0:T(8,128)S(1)}, f32[256,128]{1,0:T(8,128)S(1)}, u32[]{:S(2)}, u32[]{:S(2)}) collective-permute-start(f32[256,128]{1,0:T(8,128)S(1)} %select_select_fusion.2), channel_id=1, source_target_pairs={{0,2},{1,3},{2,0},{3,1},{4,6},{5,7},{6,4},{7,5},{8,10},{9,11},{10,... | collective-permute-start | bytes 393224 | tf_op jit(solution)/shard_map/ppermute | solution.py:454
  33.3 0.5 collective-permute-start.6
  33.9 2.5 %collective-permute-done.8 = f32[256,128]{1,0:T(8,128)S(1)} collective-permute-done((f32[256,128]{1,0:T(8,128)S(1)}, f32[256,128]{1,0:T(8,128)S(1)}, u32[]{:S(2)}, u32[]{:S(2)}) %collective-permute-start.8) | collective-permute-done | bytes 131104 | tf_op jit(solution)/shard_map/ppermute | solution.py:454
  36.3 15.0 %collective-permute-done.7 = f32[256,128]{1,0:T(8,128)S(1)} collective-permute-done((f32[256,128]{1,0:T(8,128)S(1)}, f32[256,128]{1,0:T(8,128)S(1)}, u32[]{:S(2)}, u32[]{:S(2)}) %collective-permute-start.7) | collective-permute-done | bytes 131104 | tf_op jit(solution)/shard_map/ppermute | solution.py:454
  51.3 0.0 collective-permute-done.6
  51.4 0.1 collective-permute-start.9
  51.4 0.1 constant_dynamic-update-slice_fusion
  51.5 0.0 collective-permute-done.10
  51.5 1.0 copy-done.8
  52.5 1.9 %select_select_fusion = (f32[2048,128]{1,0:T(8,128)S(1)}, f32[2048,128]{1,0:T(8,128)S(1)}, f32[2048,128]{1,0:T(8,128)S(1)}) fusion(f32[2048,128]{1,0:T(8,128)} %get-tuple-element.43, f32[2048,128]{1,0:T(8,128)S(1)} %constant_dynamic-update-slice_fusion, f32[2048,128]{1,0:T(8,128)} %copy-done.8, f32[2048,128]{1,0:T(8,128)} %get-tuple-element.37, pred[]{:T(512)S(6)} %eq.29, ...), kind=kLoop, calls=%fused_computation | loop fusion | flops 2097152 | bytes 8388612 | tf_op jit(solution)/shard_map/jit(_where)/select_n | solution.py:528
  54.3 0.0 copy-start
  54.4 1.2 fusion
  55.5 1.7 %collective-permute-start.13 = (f32[2048,128]{1,0:T(8,128)S(1)}, f32[2048,128]{1,0:T(8,128)}, u32[]{:S(2)}, u32[]{:S(2)}) collective-permute-start(f32[2048,128]{1,0:T(8,128)S(1)} %get-tuple-element.53.piece_a), channel_id=1, source_target_pairs={{9,12},{11,14},{12,9},{14,11},{17,20},{20,17},{25,28},{27,30},{28,... | collective-permute-start | bytes 3145736 | tf_op jit(solution)/shard_map/ppermute | solution.py:454
  57.2 2.4 %collective-permute-start.12 = (f32[2048,128]{1,0:T(8,128)S(1)}, f32[2048,128]{1,0:T(8,128)}, u32[]{:S(2)}, u32[]{:S(2)}) collective-permute-start(f32[2048,128]{1,0:T(8,128)S(1)} %get-tuple-element.53.piece_a), channel_id=1, source_target_pairs={{0,4},{1,5},{2,6},{3,7},{4,0},{5,1},{6,2},{7,3},{8,12},{9,8},{10,1... | collective-permute-start | bytes 3145736 | tf_op jit(solution)/shard_map/ppermute | solution.py:454
  59.6 1.9 %collective-permute-start.11 = (f32[1024,128]{1,0:T(8,128)}, f32[1024,128]{1,0:T(8,128)}, u32[]{:S(2)}, u32[]{:S(2)}) collective-permute-start(f32[1024,128]{1,0:T(8,128)} %get-tuple-element.46), channel_id=1, source_target_pairs={{0,8},{1,9},{2,10},{3,11},{4,12},{5,13},{6,14},{7,15},{10,26},{11,... | collective-permute-start | bytes 1572872 | tf_op jit(solution)/shard_map/ppermute | solution.py:454
  61.5 3.9 %collective-permute-start.14 = (f32[1024,128]{1,0:T(8,128)}, f32[1024,128]{1,0:T(8,128)}, u32[]{:S(2)}, u32[]{:S(2)}) collective-permute-start(f32[1024,128]{1,0:T(8,128)} %get-tuple-element.51), channel_id=1, source_target_pairs={{0,8},{1,9},{2,10},{3,11},{4,12},{5,13},{6,14},{7,15},{10,26},{11,... | collective-permute-start | bytes 1572872 | tf_op jit(solution)/shard_map/ppermute | solution.py:454
  65.5 0.1 pad_add_fusion.1.place_ref
  65.6 11.6 %corner_start.1.state_ref = f32[512,512]{1,0:T(8,128)S(1)} custom-call(s32[3]{0:T(128)S(1)} %pad_add_fusion.1.place_ref, f32[1024,128]{1,0:T(8,128)S(1)} %pad_maximum_fusion.mine_ref, f32[1024,128]{1,0:T(8,128)S(1)} %collective-permute-done.9.other_ref), custom_call_target="tpu_custom_call" | custom-call | flops 1000 | bytes 1000 | tf_op jit(solution)/shard_map/corner_start/pallas_call | solution.py:150
  77.2 0.1 pad_add_fusion.place_ref
  77.3 10.5 %corner_end.1.inverse_ref = f32[512,512]{1,0:T(8,128)S(1)} custom-call(f32[512,512]{1,0:T(8,128)S(1)} %corner_start.1.state_ref), custom_call_target="tpu_custom_call" | custom-call | flops 1000 | bytes 1000 | tf_op jit(solution)/shard_map/corner_end/pallas_call | solution.py:163
  87.8 2.1 %slice_select_fusion.1.rest_1_ = f32[1024,128]{1,0:T(8,128)} fusion(f32[1024,128]{1,0:T(8,128)} %collective-permute-done.11, f32[2048,128]{1,0:T(8,128)} %get-tuple-element.43, pred[]{:T(512)S(6)} %eq.25), kind=kLoop, calls=%fused_computation.4 | loop fusion | flops 131072 | bytes 1572865 | tf_op jit(solution)/shard_map/jit(_where)/select_n | solution.py:539
  89.8 1.5 %collective-permute-start.16 = (f32[1024,128]{1,0:T(8,128)}, f32[1024,128]{1,0:T(8,128)}, u32[]{:S(2)}, u32[]{:S(2)}) collective-permute-start(f32[1024,128]{1,0:T(8,128)} %slice_select_fusion.1.rest_1_), channel_id=1, source_target_pairs={{9,12},{12,9},{17,20},{19,22},{20,17},{22,19},{25,28},{27,30},{28,... | collective-permute-start | bytes 1572872 | tf_op jit(solution)/shard_map/ppermute | solution.py:454
  91.3 2.1 %collective-permute-start.15 = (f32[1024,128]{1,0:T(8,128)}, f32[1024,128]{1,0:T(8,128)}, u32[]{:S(2)}, u32[]{:S(2)}) collective-permute-start(f32[1024,128]{1,0:T(8,128)} %slice_select_fusion.1.rest_1_), channel_id=1, source_target_pairs={{0,4},{1,5},{2,6},{3,7},{4,0},{5,1},{6,2},{7,3},{8,12},{9,8},{10,1... | collective-permute-start | bytes 1572872 | tf_op jit(solution)/shard_map/ppermute | solution.py:454
  93.4 0.0 copy-start.1
  93.4 1.2 copy-done.1
  94.6 6.0 %row_weights.1 = (bf16[1024,1536]{1,0:T(8,128)(2,1)S(1)}, f32[1024,256]{1,0:T(8,128)S(1)}) custom-call(s32[3]{0:T(128)S(1)} %pad_add_fusion.place_ref, f32[2048,128]{1,0:T(8,128)S(1)} %copy-done.1, f32[2048,128]{1,0:T(8,128)} %collective-permute-done.5.rows_other, f32[512,512]{1,0:T(8,128)S(1)} %corner_end.1.inverse_ref), custom_call_target="tpu_custom_call" | custom-call | flops 1000 | bytes 1000 | tf_op jit(solution)/shard_map/row_weights/pallas_call | solution.py:315
  100.7 0.0 copy-start.4
  100.7 1.0 copy-done.4
  101.6 1.9 %slice_select_fusion.rest_1_ = f32[1024,128]{1,0:T(8,128)} fusion(f32[1024,128]{1,0:T(8,128)} %collective-permute-done.14, f32[2048,128]{1,0:T(8,128)S(1)} %copy-done.6, pred[]{:T(512)S(6)} %eq.25), kind=kLoop, calls=%fused_computation.3 | loop fusion | flops 131072 | bytes 1572865 | tf_op jit(solution)/shard_map/jit(_where)/select_n | solution.py:539
  103.5 1.5 %collective-permute-start.18 = (f32[1024,128]{1,0:T(8,128)}, f32[1024,128]{1,0:T(8,128)}, u32[]{:S(2)}, u32[]{:S(2)}) collective-permute-start(f32[1024,128]{1,0:T(8,128)} %slice_select_fusion.rest_1_), channel_id=1, source_target_pairs={{9,12},{12,9},{17,20},{19,22},{20,17},{22,19},{25,28},{27,30},{28,... | collective-permute-start | bytes 1572872 | tf_op jit(solution)/shard_map/ppermute | solution.py:454
  105.0 1.9 %collective-permute-start.17 = (f32[1024,128]{1,0:T(8,128)}, f32[1024,128]{1,0:T(8,128)}, u32[]{:S(2)}, u32[]{:S(2)}) collective-permute-start(f32[1024,128]{1,0:T(8,128)} %slice_select_fusion.rest_1_), channel_id=1, source_target_pairs={{0,4},{1,5},{2,6},{3,7},{4,0},{5,1},{6,2},{7,3},{8,12},{9,8},{10,1... | collective-permute-start | bytes 1572872 | tf_op jit(solution)/shard_map/ppermute | solution.py:454
  106.9 0.1 stack.47.place_ref
  107.0 1.2 copy-done.3
  108.2 6.4 %first_products.1.ready_ref = f32[1024,1024]{1,0:T(8,128)S(1)} custom-call(s32[7]{0:T(128)S(1)} %stack.47.place_ref, bf16[1024,1536]{1,0:T(8,128)(2,1)S(1)} %get-tuple-element.52.weights_ref, f32[2048,128]{1,0:T(8,128)S(1)} %copy-done.3, f32[2048,128]{1,0:T(8,128)} %collective-permute-done.12.piece_b, f32[2048,128]{1,0:T(8,128)} %collective-permute-done.13.piece_c), custom_call_target="tpu_custom_call" | custom-call | flops 1000 | bytes 1000 | tf_op jit(solution)/shard_map/first_products/pallas_call | solution.py:364
  114.7 7.4 %trailing_0.1.rest_0_ = f32[1024,2,8,128]{3,2,1,0:T(8,128)} custom-call(s32[7]{0:T(128)S(1)} %stack.47.place_ref, f32[1024,2,8,128]{3,2,1,0:T(8,128)} %bitcast.16, bf16[1024,1536]{1,0:T(8,128)(2,1)S(1)} %get-tuple-element.52.weights_ref, f32[1024,1024]{1,0:T(8,128)S(1)} %first_products.1.ready_ref, f32[1024,256]{1,0:T(8,128)S(1)} %copy-done.5, ...), custom_call_target="tpu_custom_call" | custom-call | flops 1000 | bytes 1000 | tf_op jit(solution)/shard_map/trailing_0/pallas_call | solution.py:424
  122.1 7.2 %trailing_1.1 = f32[1024,2,8,128]{3,2,1,0:T(8,128)} custom-call(s32[7]{0:T(128)S(1)} %stack.47.place_ref, f32[1024,2,8,128]{3,2,1,0:T(8,128)} %bitcast.17, bf16[1024,1536]{1,0:T(8,128)(2,1)S(1)} %get-tuple-element.52.weights_ref, f32[1024,1024]{1,0:T(8,128)S(1)} %first_products.1.ready_ref, ...), custom_call_target="tpu_custom_call", output_to_operand_aliasing={{}: (4, {})} | custom-call | flops 1000 | bytes 1000 | tf_op jit(solution)/shard_map/trailing_1/pallas_call | solution.py:424
  (28 shorter events, 0.2 us)
Async XLA Ops:
  2.1 9.9 %collective-permute-start = (f32[512,128]{1,0:T(8,128)}, f32[512,128]{1,0:T(8,128)S(1)}, u32[]{:S(2)}, u32[]{:S(2)}) collective-permute-start(f32[512,128]{1,0:T(8,128)} %gather_lead.1.lead_ref), channel_id=1, source_target_pairs={{0,2},{1,3},{4,6},{5,7},{8,10},{9,11},{12,14},{13,15},{16,18},{17,... | collective-permute-start | bytes 786440 | tf_op jit(solution)/shard_map/ppermute | solution.py:454
  5.5 6.4 %copy-start.7 = (f32[512,128]{1,0:T(8,128)S(1)}, f32[512,128]{1,0:T(8,128)}, u32[]{:S(2)}) copy-start(f32[512,128]{1,0:T(8,128)} %gather_lead.1.lead_ref) | copy-start | bytes 786436
  12.0 2.7 %collective-permute-start.3 = (f32[256,128]{1,0:T(8,128)S(1)}, f32[256,128]{1,0:T(8,128)S(1)}, u32[]{:S(2)}, u32[]{:S(2)}) collective-permute-start(f32[256,128]{1,0:T(8,128)S(1)} %slice_select_fusion.2), channel_id=1, source_target_pairs={{0,24},{1,25},{2,26},{3,27},{4,28},{5,29},{6,30},{7,31}} | collective-permute-start | bytes 393224 | tf_op jit(solution)/shard_map/ppermute | solution.py:454
  12.7 12.3 %collective-permute-start.2 = (f32[256,128]{1,0:T(8,128)S(1)}, f32[256,128]{1,0:T(8,128)S(1)}, u32[]{:S(2)}, u32[]{:S(2)}) collective-permute-start(f32[256,128]{1,0:T(8,128)S(1)} %slice_select_fusion.2), channel_id=1, source_target_pairs={{0,16},{1,17},{2,18},{3,19},{4,20},{5,21},{6,22},{7,23}} | collective-permute-start | bytes 393224 | tf_op jit(solution)/shard_map/ppermute | solution.py:454
  14.0 11.0 %collective-permute-start.1 = (f32[256,128]{1,0:T(8,128)S(1)}, f32[256,128]{1,0:T(8,128)S(1)}, u32[]{:S(2)}, u32[]{:S(2)}) collective-permute-start(f32[256,128]{1,0:T(8,128)S(1)} %slice_select_fusion.2), channel_id=1, source_target_pairs={{0,8},{1,9},{2,10},{3,11},{4,12},{5,13},{6,14},{7,15}} | collective-permute-start | bytes 393224 | tf_op jit(solution)/shard_map/ppermute | solution.py:454
  25.0 26.5 %collective-permute-start.10 = (f32[2048,128]{1,0:T(8,128)}, f32[2048,128]{1,0:T(8,128)S(1)}, u32[]{:S(2)}, u32[]{:S(2)}) collective-permute-start(f32[2048,128]{1,0:T(8,128)} %get-tuple-element.37), channel_id=1, source_target_pairs={{0,24},{1,25},{2,18},{3,19},{4,28},{5,29},{6,22},{7,23},{16,8},{17... | collective-permute-start | bytes 3145736 | tf_op jit(solution)/shard_map/ppermute | solution.py:454
  28.9 22.5 %collective-permute-start.4 = (f32[1536,128]{1,0:T(8,128)}, f32[1536,128]{1,0:T(8,128)S(1)}, u32[]{:S(2)}, u32[]{:S(2)}) collective-permute-start(f32[1536,128]{1,0:T(8,128)} %get-tuple-element.38), channel_id=1, source_target_pairs={{0,2},{1,3},{4,6},{5,7},{8,10},{9,11},{12,14},{13,15},{16,18},{17,... | collective-permute-start | bytes 2359304 | tf_op jit(solution)/shard_map/ppermute | solution.py:454
  30.3 6.0 %collective-permute-start.8 = (f32[256,128]{1,0:T(8,128)S(1)}, f32[256,128]{1,0:T(8,128)S(1)}, u32[]{:S(2)}, u32[]{:S(2)}) collective-permute-start(f32[256,128]{1,0:T(8,128)S(1)} %select_select_fusion.2), channel_id=1, source_target_pairs={{0,6},{1,7},{2,4},{3,5},{4,2},{5,3},{6,0},{7,1},{8,14},{9,15},{10,... | collective-permute-start | bytes 393224 | tf_op jit(solution)/shard_map/ppermute | solution.py:454
  30.4 20.9 %collective-permute-start.7 = (f32[256,128]{1,0:T(8,128)S(1)}, f32[256,128]{1,0:T(8,128)S(1)}, u32[]{:S(2)}, u32[]{:S(2)}) collective-permute-start(f32[256,128]{1,0:T(8,128)S(1)} %select_select_fusion.2), channel_id=1, source_target_pairs={{0,2},{1,3},{2,0},{3,1},{4,6},{5,7},{6,4},{7,5},{8,10},{9,11},{10,... | collective-permute-start | bytes 393224 | tf_op jit(solution)/shard_map/ppermute | solution.py:454
  33.3 18.0 %collective-permute-start.6 = (f32[256,128]{1,0:T(8,128)S(1)}, f32[256,128]{1,0:T(8,128)S(1)}, u32[]{:S(2)}, u32[]{:S(2)}) collective-permute-start(f32[256,128]{1,0:T(8,128)S(1)} %select_select_fusion.2), channel_id=1, source_target_pairs={{0,4},{1,5},{2,6},{3,7},{4,0},{5,1},{6,2},{7,3},{8,12},{9,13},{10,... | collective-permute-start | bytes 393224 | tf_op jit(solution)/shard_map/ppermute | solution.py:454
  51.4 4.2 %collective-permute-start.9 = (f32[1024,128]{1,0:T(8,128)S(1)}, f32[1024,128]{1,0:T(8,128)S(1)}, u32[]{:S(2)}, u32[]{:S(2)}) collective-permute-start(f32[1024,128]{1,0:T(8,128)S(1)} %pad_maximum_fusion.mine_ref), channel_id=1, source_target_pairs={{0,1},{1,0},{2,3},{3,2},{4,5},{5,4},{6,7},{7,6},{8,9},{9,8},{10,11... | collective-permute-start | bytes 1572872 | tf_op jit(solution)/shard_map/ppermute | solution.py:454
  51.5 1.0 copy-start.8
  54.3 39.0 %copy-start = (f32[2048,128]{1,0:T(8,128)}, f32[2048,128]{1,0:T(8,128)S(1)}, u32[]{:S(2)}) copy-start(f32[2048,128]{1,0:T(8,128)S(1)} %get-tuple-element.61.rows_mine) | copy-start | bytes 3145732
  54.4 39.0 %copy-start.2 = (f32[2048,128]{1,0:T(8,128)}, f32[2048,128]{1,0:T(8,128)S(1)}, u32[]{:S(2)}) copy-start(f32[2048,128]{1,0:T(8,128)S(1)} %get-tuple-element.53.piece_a) | copy-start | bytes 3145732
  55.5 35.8 %collective-permute-start.13 = (f32[2048,128]{1,0:T(8,128)S(1)}, f32[2048,128]{1,0:T(8,128)}, u32[]{:S(2)}, u32[]{:S(2)}) collective-permute-start(f32[2048,128]{1,0:T(8,128)S(1)} %get-tuple-element.53.piece_a), channel_id=1, source_target_pairs={{9,12},{11,14},{12,9},{14,11},{17,20},{20,17},{25,28},{27,30},{28,... | collective-permute-start | bytes 3145736 | tf_op jit(solution)/shard_map/ppermute | solution.py:454
  57.2 36.2 %collective-permute-start.12 = (f32[2048,128]{1,0:T(8,128)S(1)}, f32[2048,128]{1,0:T(8,128)}, u32[]{:S(2)}, u32[]{:S(2)}) collective-permute-start(f32[2048,128]{1,0:T(8,128)S(1)} %get-tuple-element.53.piece_a), channel_id=1, source_target_pairs={{0,4},{1,5},{2,6},{3,7},{4,0},{5,1},{6,2},{7,3},{8,12},{9,8},{10,1... | collective-permute-start | bytes 3145736 | tf_op jit(solution)/shard_map/ppermute | solution.py:454
  59.6 33.8 %collective-permute-start.5 = (f32[2048,128]{1,0:T(8,128)S(1)}, f32[2048,128]{1,0:T(8,128)}, u32[]{:S(2)}, u32[]{:S(2)}) collective-permute-start(f32[2048,128]{1,0:T(8,128)S(1)} %get-tuple-element.61.rows_mine), channel_id=1, source_target_pairs={{0,1},{1,0},{2,3},{3,2},{4,5},{5,4},{6,7},{7,6},{8,9},{9,8},{10,11... | collective-permute-start | bytes 3145736 | tf_op jit(solution)/shard_map/ppermute | solution.py:454
  59.6 28.1 %collective-permute-start.11 = (f32[1024,128]{1,0:T(8,128)}, f32[1024,128]{1,0:T(8,128)}, u32[]{:S(2)}, u32[]{:S(2)}) collective-permute-start(f32[1024,128]{1,0:T(8,128)} %get-tuple-element.46), channel_id=1, source_target_pairs={{0,8},{1,9},{2,10},{3,11},{4,12},{5,13},{6,14},{7,15},{10,26},{11,... | collective-permute-start | bytes 1572872 | tf_op jit(solution)/shard_map/ppermute | solution.py:454
  61.5 40.1 %collective-permute-start.14 = (f32[1024,128]{1,0:T(8,128)}, f32[1024,128]{1,0:T(8,128)}, u32[]{:S(2)}, u32[]{:S(2)}) collective-permute-start(f32[1024,128]{1,0:T(8,128)} %get-tuple-element.51), channel_id=1, source_target_pairs={{0,8},{1,9},{2,10},{3,11},{4,12},{5,13},{6,14},{7,15},{10,26},{11,... | collective-permute-start | bytes 1572872 | tf_op jit(solution)/shard_map/ppermute | solution.py:454
  65.5 36.2 %copy-start.6 = (f32[2048,128]{1,0:T(8,128)S(1)}, f32[2048,128]{1,0:T(8,128)}, u32[]{:S(2)}) copy-start(f32[2048,128]{1,0:T(8,128)} %get-tuple-element.43) | copy-start | bytes 3145732
  89.8 24.8 %collective-permute-start.16 = (f32[1024,128]{1,0:T(8,128)}, f32[1024,128]{1,0:T(8,128)}, u32[]{:S(2)}, u32[]{:S(2)}) collective-permute-start(f32[1024,128]{1,0:T(8,128)} %slice_select_fusion.1.rest_1_), channel_id=1, source_target_pairs={{9,12},{12,9},{17,20},{19,22},{20,17},{22,19},{25,28},{27,30},{28,... | collective-permute-start | bytes 1572872 | tf_op jit(solution)/shard_map/ppermute | solution.py:454
  91.3 23.3 %collective-permute-start.15 = (f32[1024,128]{1,0:T(8,128)}, f32[1024,128]{1,0:T(8,128)}, u32[]{:S(2)}, u32[]{:S(2)}) collective-permute-start(f32[1024,128]{1,0:T(8,128)} %slice_select_fusion.1.rest_1_), channel_id=1, source_target_pairs={{0,4},{1,5},{2,6},{3,7},{4,0},{5,1},{6,2},{7,3},{8,12},{9,8},{10,1... | collective-permute-start | bytes 1572872 | tf_op jit(solution)/shard_map/ppermute | solution.py:454
  93.4 1.2 copy-start.1
  100.7 1.0 copy-start.4
  103.5 18.6 %collective-permute-start.18 = (f32[1024,128]{1,0:T(8,128)}, f32[1024,128]{1,0:T(8,128)}, u32[]{:S(2)}, u32[]{:S(2)}) collective-permute-start(f32[1024,128]{1,0:T(8,128)} %slice_select_fusion.rest_1_), channel_id=1, source_target_pairs={{9,12},{12,9},{17,20},{19,22},{20,17},{22,19},{25,28},{27,30},{28,... | collective-permute-start | bytes 1572872 | tf_op jit(solution)/shard_map/ppermute | solution.py:454
  105.0 17.1 %collective-permute-start.17 = (f32[1024,128]{1,0:T(8,128)}, f32[1024,128]{1,0:T(8,128)}, u32[]{:S(2)}, u32[]{:S(2)}) collective-permute-start(f32[1024,128]{1,0:T(8,128)} %slice_select_fusion.rest_1_), channel_id=1, source_target_pairs={{0,4},{1,5},{2,6},{3,7},{4,0},{5,1},{6,2},{7,3},{8,12},{9,8},{10,1... | collective-permute-start | bytes 1572872 | tf_op jit(solution)/shard_map/ppermute | solution.py:454
  107.0 1.2 copy-start.3
  108.2 6.5 %copy-start.5 = (f32[1024,256]{1,0:T(8,128)S(1)}, f32[1024,256]{1,0:T(8,128)}, u32[]{:S(2)}) copy-start(f32[1024,256]{1,0:T(8,128)} %copy-done.4) | copy-start | bytes 3145732

commit v6 on v4

--- a/solution.py
+++ b/solution.py
@@ -544,6 +544,7 @@
             inverse, held = lax.optimization_barrier((inverse, held))
         last.append([held, send(held, same_core(1)), send(held, cross_core(1))])
         if part == 0:
+            inverse, first = lax.optimization_barrier((inverse, first))
             weights, solved = row_weights(
                 jnp.stack([row, col, core]).astype(jnp.int32), rows_mine, rows_other, inverse, row_tiles, tile
             )

time: 118 us -> 118 us (level)
  the two profiles are of different devices: /device:TPU:5 before, /device:TPU:27 now
where the time goes in v6:
time: 118 us; the launch traced here: 117 us
  Pallas kernels  55.7 us (47%)
  starting transfers between devices  38.6 us (33%)
  waiting for transfers between devices  12 us (10%)
  local copies, waits for them, and re-layouts  6.9 us (6%)
  other arithmetic  3.48 us (3%)
    ppermute x18, starting transfers between devices, send(): return lax.ppermute(value, AXES, pairs)  38.6 us
    pallas_call x2, Pallas kernels, trailing(): pl.pallas_call(functools.partial(trailing_kernel, tile, group, count), gr...  14.7 us
    ppermute x18, waiting for transfers between devices, send(): return lax.ppermute(value, AXES, pairs)  12 us
    pallas_call x1, Pallas kernels, corner_start(): pl.pallas_call(corner_start_kernel, out_shape=jax.ShapeDtypeStruct((width...  11.4 us
    pallas_call x1, Pallas kernels, corner_end(): pl.pallas_call(corner_end_kernel, out_shape=jax.ShapeDtypeStruct(state.sh...  10.3 us
    unnamed x24, local copies, waits for them, and re-layouts  6.68 us
    pallas_call x1, Pallas kernels, gather_pieces(): pl.pallas_call(functools.partial(gather_kernel, tile, col_tiles, row_tile...  6.42 us
    pallas_call x1, Pallas kernels, row_weights(): pl.pallas_call(functools.partial(weights_kernel, tile), grid=(row_tiles,)...  5.54 us
  transfers between devices with their start and end apart: 18, of which 3 were waited for; matrix products, arithmetic and copies ran while one was open for 2% of the time, Pallas kernels for 40%

profile of v6, /device:TPU:27, one launch (start us, length us, event | category | flops | bytes accessed | tf_op | source)
XLA Modules:
  0.0 117.1 jit_solution(16216443294659956521)
XLA Ops:
  0.0 2.1 %gather_lead.1.lead_ref = f32[512,128]{1,0:T(8,128)} custom-call(f32[1024,2,8,128]{3,2,1,0:T(8,128)} %bitcast.13), custom_call_target="tpu_custom_call" | custom-call | flops 1000 | bytes 1000 | tf_op jit(solution)/shard_map/gather_lead/pallas_call | solution.py:227
  2.1 3.1 %collective-permute-start = (f32[512,128]{1,0:T(8,128)}, f32[512,128]{1,0:T(8,128)S(1)}, u32[]{:S(2)}, u32[]{:S(2)}) collective-permute-start(f32[512,128]{1,0:T(8,128)} %gather_lead.1.lead_ref), channel_id=1, source_target_pairs={{0,2},{1,3},{4,6},{5,7},{8,10},{9,11},{12,14},{13,15},{16,18},{17,... | collective-permute-start | bytes 786440 | tf_op jit(solution)/shard_map/ppermute | solution.py:454
  5.3 6.4 %gather_pieces.1 = (f32[1536,128]{1,0:T(8,128)}, f32[2048,128]{1,0:T(8,128)}, f32[2048,128]{1,0:T(8,128)}, f32[2048,128]{1,0:T(8,128)}) custom-call(s32[1]{0:T(128)} %bitcast.9.place_ref, f32[512,128]{1,0:T(8,128)} %gather_lead.1.lead_ref, f32[1024,2,8,128]{3,2,1,0:T(8,128)} %bitcast.14, f32[16384,128]{1,0:T(8,128)} %bitcast.15), custom_call_target="tpu_custom_call" | custom-call | flops 1000 | bytes 1000 | tf_op jit(solution)/shard_map/gather_pieces/pallas_call | solution.py:244
  11.7 0.7 collective-permute-start.1
  12.4 1.3 %collective-permute-start.2 = (f32[256,128]{1,0:T(8,128)S(1)}, f32[256,128]{1,0:T(8,128)S(1)}, u32[]{:S(2)}, u32[]{:S(2)}) collective-permute-start(f32[256,128]{1,0:T(8,128)S(1)} %broadcast_select_fusion.1), channel_id=1, source_target_pairs={{0,8},{1,9},{2,10},{3,11},{4,12},{5,13},{6,14},{7,15},{16,24},{17,... | collective-permute-start | bytes 393224 | tf_op jit(solution)/shard_map/ppermute | solution.py:454
  13.8 8.4 %collective-permute-done.2 = f32[256,128]{1,0:T(8,128)S(1)} collective-permute-done((f32[256,128]{1,0:T(8,128)S(1)}, f32[256,128]{1,0:T(8,128)S(1)}, u32[]{:S(2)}, u32[]{:S(2)}) %collective-permute-start.2) | collective-permute-done | bytes 131104 | tf_op jit(solution)/shard_map/ppermute | solution.py:454
  22.2 1.3 %collective-permute-start.7 = (f32[2048,128]{1,0:T(8,128)}, f32[2048,128]{1,0:T(8,128)S(1)}, u32[]{:S(2)}, u32[]{:S(2)}) collective-permute-start(f32[2048,128]{1,0:T(8,128)} %get-tuple-element.37), channel_id=1, source_target_pairs={{0,24},{1,25},{2,18},{3,19},{4,28},{5,29},{6,22},{7,23},{16,8},{17... | collective-permute-start | bytes 3145736 | tf_op jit(solution)/shard_map/ppermute | solution.py:454
  23.5 0.4 collective-permute-start.5
  23.8 1.2 %collective-permute-start.3 = (f32[256,128]{1,0:T(8,128)S(1)}, f32[256,128]{1,0:T(8,128)S(1)}, u32[]{:S(2)}, u32[]{:S(2)}) collective-permute-start(f32[256,128]{1,0:T(8,128)S(1)} %broadcast_select_fusion.2), channel_id=1, source_target_pairs={{0,4},{1,5},{2,6},{3,7},{4,0},{5,1},{6,2},{7,3},{8,12},{9,13},{10,... | collective-permute-start | bytes 393224 | tf_op jit(solution)/shard_map/ppermute | solution.py:454
  25.0 1.1 collective-permute-start.4
  26.2 2.1 %collective-permute-done.5 = f32[256,128]{1,0:T(8,128)S(1)} collective-permute-done((f32[256,128]{1,0:T(8,128)S(1)}, f32[256,128]{1,0:T(8,128)S(1)}, u32[]{:S(2)}, u32[]{:S(2)}) %collective-permute-start.5) | collective-permute-done | bytes 131104 | tf_op jit(solution)/shard_map/ppermute | solution.py:454
  28.3 2.2 %collective-permute-start.8 = (f32[1536,128]{1,0:T(8,128)}, f32[1536,128]{1,0:T(8,128)S(1)}, u32[]{:S(2)}, u32[]{:S(2)}) collective-permute-start(f32[1536,128]{1,0:T(8,128)} %get-tuple-element.41), channel_id=1, source_target_pairs={{0,2},{1,3},{4,6},{5,7},{8,10},{9,11},{12,14},{13,15},{16,18},{17,... | collective-permute-start | bytes 2359304 | tf_op jit(solution)/shard_map/ppermute | solution.py:454
  30.6 5.2 %collective-permute-start.6 = (f32[1024,128]{1,0:T(8,128)S(1)}, f32[1024,128]{1,0:T(8,128)S(1)}, u32[]{:S(2)}, u32[]{:S(2)}) collective-permute-start(f32[1024,128]{1,0:T(8,128)S(1)} %constant_dynamic-update-slice_fusion.mine_ref), channel_id=1, source_target_pairs={{0,1},{1,0},{2,3},{3,2},{4,5},{5,4},{6,7},{7,6},{8,9},{9,8},{10,11... | collective-permute-start | bytes 1572872 | tf_op jit(solution)/shard_map/ppermute | solution.py:454
  35.8 0.1 pad_add_fusion.1.place_ref
  35.9 1.4 %collective-permute-done.6.other_ref = f32[1024,128]{1,0:T(8,128)S(1)} collective-permute-done((f32[1024,128]{1,0:T(8,128)S(1)}, f32[1024,128]{1,0:T(8,128)S(1)}, u32[]{:S(2)}, u32[]{:S(2)}) %collective-permute-start.6) | collective-permute-done | bytes 524320 | tf_op jit(solution)/shard_map/ppermute | solution.py:454
  37.3 11.4 %corner_start.1.state_ref = f32[512,512]{1,0:T(8,128)S(1)} custom-call(s32[3]{0:T(128)S(1)} %pad_add_fusion.1.place_ref, f32[1024,128]{1,0:T(8,128)S(1)} %constant_dynamic-update-slice_fusion.mine_ref, f32[1024,128]{1,0:T(8,128)S(1)} %collective-permute-done.6.other_ref), custom_call_target="tpu_custom_call" | custom-call | flops 1000 | bytes 1000 | tf_op jit(solution)/shard_map/corner_start/pallas_call | solution.py:150
  48.8 0.0 collective-permute-done.8
  48.8 0.0 collective-permute-done.7
  48.8 0.1 constant_dynamic-update-slice_fusion.4
  48.8 1.5 %select_select_fusion = (f32[2048,128]{1,0:T(8,128)S(1)}, f32[2048,128]{1,0:T(8,128)S(1)}, f32[2048,128]{1,0:T(8,128)S(1)}) fusion(f32[2048,128]{1,0:T(8,128)} %get-tuple-element.46, f32[2048,128]{1,0:T(8,128)S(1)} %constant_dynamic-update-slice_fusion.4, f32[2048,128]{1,0:T(8,128)S(1)} %collective-permute-done.7, f32[2048,128]{1,0:T(8,128)} %get-tuple-element.37, ...), kind=kLoop, calls=%fused_computation | loop fusion | flops 2097152 | bytes 8388612 | tf_op jit(solution)/shard_map/jit(_where)/select_n | solution.py:531
  50.4 0.0 copy-start
  50.4 0.1 fusion
  50.5 0.7 collective-permute-start.12
  51.2 5.4 %collective-permute-start.11 = (f32[2048,128]{1,0:T(8,128)S(1)}, f32[2048,128]{1,0:T(8,128)S(1)}, u32[]{:S(2)}, u32[]{:S(2)}) collective-permute-start(f32[2048,128]{1,0:T(8,128)S(1)} %get-tuple-element.55.piece_a), channel_id=1, source_target_pairs={{0,4},{1,5},{2,6},{3,7},{4,0},{5,1},{6,2},{7,3},{8,12},{9,8},{10,1... | collective-permute-start | bytes 3145736 | tf_op jit(solution)/shard_map/ppermute | solution.py:454
  56.7 0.0 collective-permute-start.9
  56.7 1.9 %collective-permute-start.10 = (f32[1024,128]{1,0:T(8,128)S(1)}, f32[1024,128]{1,0:T(8,128)S(1)}, u32[]{:S(2)}, u32[]{:S(2)}) collective-permute-start(f32[1024,128]{1,0:T(8,128)S(1)} %get-tuple-element.48), channel_id=1, source_target_pairs={{0,8},{1,9},{2,10},{3,11},{4,12},{5,13},{6,14},{7,15},{10,26},{11,... | collective-permute-start | bytes 1572872 | tf_op jit(solution)/shard_map/ppermute | solution.py:454
  58.6 3.5 %collective-permute-start.13 = (f32[1024,128]{1,0:T(8,128)S(1)}, f32[1024,128]{1,0:T(8,128)S(1)}, u32[]{:S(2)}, u32[]{:S(2)}) collective-permute-start(f32[1024,128]{1,0:T(8,128)S(1)} %get-tuple-element.53), channel_id=1, source_target_pairs={{0,8},{1,9},{2,10},{3,11},{4,12},{5,13},{6,14},{7,15},{10,26},{11,... | collective-permute-start | bytes 1572872 | tf_op jit(solution)/shard_map/ppermute | solution.py:454
  62.1 0.1 pad_add_fusion.place_ref
  62.2 10.3 %corner_end.1.inverse_ref = f32[512,512]{1,0:T(8,128)S(1)} custom-call(f32[512,512]{1,0:T(8,128)S(1)} %corner_start.1.state_ref), custom_call_target="tpu_custom_call" | custom-call | flops 1000 | bytes 1000 | tf_op jit(solution)/shard_map/corner_end/pallas_call | solution.py:163
  72.5 0.9 slice_select_fusion.1.rest_1_
  73.4 1.5 %collective-permute-start.15 = (f32[1024,128]{1,0:T(8,128)}, f32[1024,128]{1,0:T(8,128)}, u32[]{:S(2)}, u32[]{:S(2)}) collective-permute-start(f32[1024,128]{1,0:T(8,128)} %slice_select_fusion.1.rest_1_), channel_id=1, source_target_pairs={{9,12},{12,9},{17,20},{19,22},{20,17},{22,19},{25,28},{27,30},{28,... | collective-permute-start | bytes 1572872 | tf_op jit(solution)/shard_map/ppermute | solution.py:454
  74.8 1.0 copy-done.4
  75.8 4.5 %collective-permute-start.14 = (f32[1024,128]{1,0:T(8,128)}, f32[1024,128]{1,0:T(8,128)}, u32[]{:S(2)}, u32[]{:S(2)}) collective-permute-start(f32[1024,128]{1,0:T(8,128)} %slice_select_fusion.1.rest_1_), channel_id=1, source_target_pairs={{0,4},{1,5},{2,6},{3,7},{4,0},{5,1},{6,2},{7,3},{8,12},{9,8},{10,1... | collective-permute-start | bytes 1572872 | tf_op jit(solution)/shard_map/ppermute | solution.py:454
  80.3 0.0 collective-permute-done.11.piece_b
  80.3 1.0 copy-done.6
  81.3 0.0 collective-permute-done.9.rows_other
  81.3 5.5 %row_weights.1 = (bf16[1024,1536]{1,0:T(8,128)(2,1)S(1)}, f32[1024,256]{1,0:T(8,128)S(1)}) custom-call(s32[3]{0:T(128)S(1)} %pad_add_fusion.place_ref, f32[2048,128]{1,0:T(8,128)S(1)} %get-tuple-element.63.rows_mine, f32[2048,128]{1,0:T(8,128)S(1)} %collective-permute-done.9.rows_other, f32[512,512]{1,0:T(8,128)S(1)} %corner_end.1.inverse_ref), custom_call_target="tpu_custom_call" | custom-call | flops 1000 | bytes 1000 | tf_op jit(solution)/shard_map/row_weights/pallas_call | solution.py:315
  86.8 1.0 copy-done.2
  87.8 0.9 slice_select_fusion.rest_1_
  88.7 1.5 %collective-permute-start.17 = (f32[1024,128]{1,0:T(8,128)}, f32[1024,128]{1,0:T(8,128)}, u32[]{:S(2)}, u32[]{:S(2)}) collective-permute-start(f32[1024,128]{1,0:T(8,128)} %slice_select_fusion.rest_1_), channel_id=1, source_target_pairs={{9,12},{12,9},{17,20},{19,22},{20,17},{22,19},{25,28},{27,30},{28,... | collective-permute-start | bytes 1572872 | tf_op jit(solution)/shard_map/ppermute | solution.py:454
  90.2 3.1 %collective-permute-start.16 = (f32[1024,128]{1,0:T(8,128)}, f32[1024,128]{1,0:T(8,128)}, u32[]{:S(2)}, u32[]{:S(2)}) collective-permute-start(f32[1024,128]{1,0:T(8,128)} %slice_select_fusion.rest_1_), channel_id=1, source_target_pairs={{0,4},{1,5},{2,6},{3,7},{4,0},{5,1},{6,2},{7,3},{8,12},{9,8},{10,1... | collective-permute-start | bytes 1572872 | tf_op jit(solution)/shard_map/ppermute | solution.py:454
  93.2 0.1 stack.47.place_ref
  93.3 1.2 %copy-done.1 = f32[2048,128]{1,0:T(8,128)S(1)} copy-done((f32[2048,128]{1,0:T(8,128)S(1)}, f32[2048,128]{1,0:T(8,128)}, u32[]{:S(2)}) %copy-start.1) | copy-done | bytes 1048600
  94.6 1.2 %copy-done.5 = f32[2048,128]{1,0:T(8,128)S(1)} copy-done((f32[2048,128]{1,0:T(8,128)S(1)}, f32[2048,128]{1,0:T(8,128)}, u32[]{:S(2)}) %copy-start.5) | copy-done | bytes 1048600
  95.8 1.2 %copy-done.7 = f32[2048,128]{1,0:T(8,128)S(1)} copy-done((f32[2048,128]{1,0:T(8,128)S(1)}, f32[2048,128]{1,0:T(8,128)}, u32[]{:S(2)}) %copy-start.7) | copy-done | bytes 1048600
  97.0 5.3 %first_products.1.ready_ref = f32[1024,1024]{1,0:T(8,128)S(1)} custom-call(s32[7]{0:T(128)S(1)} %stack.47.place_ref, bf16[1024,1536]{1,0:T(8,128)(2,1)S(1)} %get-tuple-element.54.weights_ref, f32[2048,128]{1,0:T(8,128)S(1)} %copy-done.1, f32[2048,128]{1,0:T(8,128)S(1)} %copy-done.7, f32[2048,128]{1,0:T(8,128)S(1)} %copy-done.5), custom_call_target="tpu_custom_call" | custom-call | flops 1000 | bytes 1000 | tf_op jit(solution)/shard_map/first_products/pallas_call | solution.py:364
  102.4 7.4 %trailing_0.1.rest_0_ = f32[1024,2,8,128]{3,2,1,0:T(8,128)} custom-call(s32[7]{0:T(128)S(1)} %stack.47.place_ref, f32[1024,2,8,128]{3,2,1,0:T(8,128)} %bitcast.16, bf16[1024,1536]{1,0:T(8,128)(2,1)S(1)} %get-tuple-element.54.weights_ref, f32[1024,1024]{1,0:T(8,128)S(1)} %first_products.1.ready_ref, f32[1024,256]{1,0:T(8,128)S(1)} %copy-done.3, ...), custom_call_target="tpu_custom_call" | custom-call | flops 1000 | bytes 1000 | tf_op jit(solution)/shard_map/trailing_0/pallas_call | solution.py:424
  109.8 7.2 %trailing_1.1 = f32[1024,2,8,128]{3,2,1,0:T(8,128)} custom-call(s32[7]{0:T(128)S(1)} %stack.47.place_ref, f32[1024,2,8,128]{3,2,1,0:T(8,128)} %bitcast.17, bf16[1024,1536]{1,0:T(8,128)(2,1)S(1)} %get-tuple-element.54.weights_ref, f32[1024,1024]{1,0:T(8,128)S(1)} %first_products.1.ready_ref, ...), custom_call_target="tpu_custom_call", output_to_operand_aliasing={{}: (4, {})} | custom-call | flops 1000 | bytes 1000 | tf_op jit(solution)/shard_map/trailing_1/pallas_call | solution.py:424
  (32 shorter events, 0.2 us)
Async XLA Ops:
  2.1 9.6 %collective-permute-start = (f32[512,128]{1,0:T(8,128)}, f32[512,128]{1,0:T(8,128)S(1)}, u32[]{:S(2)}, u32[]{:S(2)}) collective-permute-start(f32[512,128]{1,0:T(8,128)} %gather_lead.1.lead_ref), channel_id=1, source_target_pairs={{0,2},{1,3},{4,6},{5,7},{8,10},{9,11},{12,14},{13,15},{16,18},{17,... | collective-permute-start | bytes 786440 | tf_op jit(solution)/shard_map/ppermute | solution.py:454
  5.2 6.4 %copy-start.9 = (f32[512,128]{1,0:T(8,128)S(1)}, f32[512,128]{1,0:T(8,128)}, u32[]{:S(2)}) copy-start(f32[512,128]{1,0:T(8,128)} %gather_lead.1.lead_ref) | copy-start | bytes 786436
  11.7 0.7 collective-permute-start.1
  12.4 9.7 %collective-permute-start.2 = (f32[256,128]{1,0:T(8,128)S(1)}, f32[256,128]{1,0:T(8,128)S(1)}, u32[]{:S(2)}, u32[]{:S(2)}) collective-permute-start(f32[256,128]{1,0:T(8,128)S(1)} %broadcast_select_fusion.1), channel_id=1, source_target_pairs={{0,8},{1,9},{2,10},{3,11},{4,12},{5,13},{6,14},{7,15},{16,24},{17,... | collective-permute-start | bytes 393224 | tf_op jit(solution)/shard_map/ppermute | solution.py:454
  22.2 26.6 %collective-permute-start.7 = (f32[2048,128]{1,0:T(8,128)}, f32[2048,128]{1,0:T(8,128)S(1)}, u32[]{:S(2)}, u32[]{:S(2)}) collective-permute-start(f32[2048,128]{1,0:T(8,128)} %get-tuple-element.37), channel_id=1, source_target_pairs={{0,24},{1,25},{2,18},{3,19},{4,28},{5,29},{6,22},{7,23},{16,8},{17... | collective-permute-start | bytes 3145736 | tf_op jit(solution)/shard_map/ppermute | solution.py:454
  23.5 4.9 %collective-permute-start.5 = (f32[256,128]{1,0:T(8,128)S(1)}, f32[256,128]{1,0:T(8,128)S(1)}, u32[]{:S(2)}, u32[]{:S(2)}) collective-permute-start(f32[256,128]{1,0:T(8,128)S(1)} %broadcast_select_fusion.2), channel_id=1, source_target_pairs={{0,6},{1,7},{2,4},{3,5},{4,2},{5,3},{6,0},{7,1},{8,14},{9,15},{10,... | collective-permute-start | bytes 393224 | tf_op jit(solution)/shard_map/ppermute | solution.py:454
  23.8 6.7 %collective-permute-start.3 = (f32[256,128]{1,0:T(8,128)S(1)}, f32[256,128]{1,0:T(8,128)S(1)}, u32[]{:S(2)}, u32[]{:S(2)}) collective-permute-start(f32[256,128]{1,0:T(8,128)S(1)} %broadcast_select_fusion.2), channel_id=1, source_target_pairs={{0,4},{1,5},{2,6},{3,7},{4,0},{5,1},{6,2},{7,3},{8,12},{9,13},{10,... | collective-permute-start | bytes 393224 | tf_op jit(solution)/shard_map/ppermute | solution.py:454
  25.0 5.5 %collective-permute-start.4 = (f32[256,128]{1,0:T(8,128)S(1)}, f32[256,128]{1,0:T(8,128)S(1)}, u32[]{:S(2)}, u32[]{:S(2)}) collective-permute-start(f32[256,128]{1,0:T(8,128)S(1)} %broadcast_select_fusion.2), channel_id=1, source_target_pairs={{0,2},{1,3},{2,0},{3,1},{4,6},{5,7},{6,4},{7,5},{8,10},{9,11},{10,... | collective-permute-start | bytes 393224 | tf_op jit(solution)/shard_map/ppermute | solution.py:454
  28.3 20.4 %collective-permute-start.8 = (f32[1536,128]{1,0:T(8,128)}, f32[1536,128]{1,0:T(8,128)S(1)}, u32[]{:S(2)}, u32[]{:S(2)}) collective-permute-start(f32[1536,128]{1,0:T(8,128)} %get-tuple-element.41), channel_id=1, source_target_pairs={{0,2},{1,3},{4,6},{5,7},{8,10},{9,11},{12,14},{13,15},{16,18},{17,... | collective-permute-start | bytes 2359304 | tf_op jit(solution)/shard_map/ppermute | solution.py:454
  30.6 6.7 %collective-permute-start.6 = (f32[1024,128]{1,0:T(8,128)S(1)}, f32[1024,128]{1,0:T(8,128)S(1)}, u32[]{:S(2)}, u32[]{:S(2)}) collective-permute-start(f32[1024,128]{1,0:T(8,128)S(1)} %constant_dynamic-update-slice_fusion.mine_ref), channel_id=1, source_target_pairs={{0,1},{1,0},{2,3},{3,2},{4,5},{5,4},{6,7},{7,6},{8,9},{9,8},{10,11... | collective-permute-start | bytes 1572872 | tf_op jit(solution)/shard_map/ppermute | solution.py:454
  35.9 36.6 %copy-start.8 = (f32[2048,128]{1,0:T(8,128)S(1)}, f32[2048,128]{1,0:T(8,128)}, u32[]{:S(2)}) copy-start(f32[2048,128]{1,0:T(8,128)} %get-tuple-element.46) | copy-start | bytes 3145732
  50.4 29.9 %copy-start = (f32[2048,128]{1,0:T(8,128)}, f32[2048,128]{1,0:T(8,128)S(1)}, u32[]{:S(2)}) copy-start(f32[2048,128]{1,0:T(8,128)S(1)} %get-tuple-element.55.piece_a) | copy-start | bytes 3145732
  50.5 24.3 %collective-permute-start.12 = (f32[2048,128]{1,0:T(8,128)S(1)}, f32[2048,128]{1,0:T(8,128)S(1)}, u32[]{:S(2)}, u32[]{:S(2)}) collective-permute-start(f32[2048,128]{1,0:T(8,128)S(1)} %get-tuple-element.55.piece_a), channel_id=1, source_target_pairs={{9,12},{11,14},{12,9},{14,11},{17,20},{20,17},{25,28},{27,30},{28,... | collective-permute-start | bytes 3145736 | tf_op jit(solution)/shard_map/ppermute | solution.py:454
  51.2 29.1 %collective-permute-start.11 = (f32[2048,128]{1,0:T(8,128)S(1)}, f32[2048,128]{1,0:T(8,128)S(1)}, u32[]{:S(2)}, u32[]{:S(2)}) collective-permute-start(f32[2048,128]{1,0:T(8,128)S(1)} %get-tuple-element.55.piece_a), channel_id=1, source_target_pairs={{0,4},{1,5},{2,6},{3,7},{4,0},{5,1},{6,2},{7,3},{8,12},{9,8},{10,1... | collective-permute-start | bytes 3145736 | tf_op jit(solution)/shard_map/ppermute | solution.py:454
  56.7 24.6 %collective-permute-start.9 = (f32[2048,128]{1,0:T(8,128)S(1)}, f32[2048,128]{1,0:T(8,128)S(1)}, u32[]{:S(2)}, u32[]{:S(2)}) collective-permute-start(f32[2048,128]{1,0:T(8,128)S(1)} %get-tuple-element.63.rows_mine), channel_id=1, source_target_pairs={{0,1},{1,0},{2,3},{3,2},{4,5},{5,4},{6,7},{7,6},{8,9},{9,8},{10,11... | collective-permute-start | bytes 3145736 | tf_op jit(solution)/shard_map/ppermute | solution.py:454
  56.7 15.8 %collective-permute-start.10 = (f32[1024,128]{1,0:T(8,128)S(1)}, f32[1024,128]{1,0:T(8,128)S(1)}, u32[]{:S(2)}, u32[]{:S(2)}) collective-permute-start(f32[1024,128]{1,0:T(8,128)S(1)} %get-tuple-element.48), channel_id=1, source_target_pairs={{0,8},{1,9},{2,10},{3,11},{4,12},{5,13},{6,14},{7,15},{10,26},{11,... | collective-permute-start | bytes 1572872 | tf_op jit(solution)/shard_map/ppermute | solution.py:454
  58.6 29.2 %collective-permute-start.13 = (f32[1024,128]{1,0:T(8,128)S(1)}, f32[1024,128]{1,0:T(8,128)S(1)}, u32[]{:S(2)}, u32[]{:S(2)}) collective-permute-start(f32[1024,128]{1,0:T(8,128)S(1)} %get-tuple-element.53), channel_id=1, source_target_pairs={{0,8},{1,9},{2,10},{3,11},{4,12},{5,13},{6,14},{7,15},{10,26},{11,... | collective-permute-start | bytes 1572872 | tf_op jit(solution)/shard_map/ppermute | solution.py:454
  73.4 29.0 %collective-permute-start.15 = (f32[1024,128]{1,0:T(8,128)}, f32[1024,128]{1,0:T(8,128)}, u32[]{:S(2)}, u32[]{:S(2)}) collective-permute-start(f32[1024,128]{1,0:T(8,128)} %slice_select_fusion.1.rest_1_), channel_id=1, source_target_pairs={{9,12},{12,9},{17,20},{19,22},{20,17},{22,19},{25,28},{27,30},{28,... | collective-permute-start | bytes 1572872 | tf_op jit(solution)/shard_map/ppermute | solution.py:454
  74.8 1.0 copy-start.4
  75.8 26.6 %collective-permute-start.14 = (f32[1024,128]{1,0:T(8,128)}, f32[1024,128]{1,0:T(8,128)}, u32[]{:S(2)}, u32[]{:S(2)}) collective-permute-start(f32[1024,128]{1,0:T(8,128)} %slice_select_fusion.1.rest_1_), channel_id=1, source_target_pairs={{0,4},{1,5},{2,6},{3,7},{4,0},{5,1},{6,2},{7,3},{8,12},{9,8},{10,1... | collective-permute-start | bytes 1572872 | tf_op jit(solution)/shard_map/ppermute | solution.py:454
  80.3 1.0 copy-start.6
  86.8 1.0 copy-start.2
  88.7 21.1 %collective-permute-start.17 = (f32[1024,128]{1,0:T(8,128)}, f32[1024,128]{1,0:T(8,128)}, u32[]{:S(2)}, u32[]{:S(2)}) collective-permute-start(f32[1024,128]{1,0:T(8,128)} %slice_select_fusion.rest_1_), channel_id=1, source_target_pairs={{9,12},{12,9},{17,20},{19,22},{20,17},{22,19},{25,28},{27,30},{28,... | collective-permute-start | bytes 1572872 | tf_op jit(solution)/shard_map/ppermute | solution.py:454
  90.2 19.7 %collective-permute-start.16 = (f32[1024,128]{1,0:T(8,128)}, f32[1024,128]{1,0:T(8,128)}, u32[]{:S(2)}, u32[]{:S(2)}) collective-permute-start(f32[1024,128]{1,0:T(8,128)} %slice_select_fusion.rest_1_), channel_id=1, source_target_pairs={{0,4},{1,5},{2,6},{3,7},{4,0},{5,1},{6,2},{7,3},{8,12},{9,8},{10,1... | collective-permute-start | bytes 1572872 | tf_op jit(solution)/shard_map/ppermute | solution.py:454
  93.3 1.2 %copy-start.1 = (f32[2048,128]{1,0:T(8,128)S(1)}, f32[2048,128]{1,0:T(8,128)}, u32[]{:S(2)}) copy-start(f32[2048,128]{1,0:T(8,128)} %copy-done) | copy-start | bytes 3145732
  94.6 1.2 %copy-start.5 = (f32[2048,128]{1,0:T(8,128)S(1)}, f32[2048,128]{1,0:T(8,128)}, u32[]{:S(2)}) copy-start(f32[2048,128]{1,0:T(8,128)} %copy-done.4) | copy-start | bytes 3145732
  95.8 1.2 %copy-start.7 = (f32[2048,128]{1,0:T(8,128)S(1)}, f32[2048,128]{1,0:T(8,128)}, u32[]{:S(2)}) copy-start(f32[2048,128]{1,0:T(8,128)} %copy-done.6) | copy-start | bytes 3145732
  97.0 5.4 %copy-start.3 = (f32[1024,256]{1,0:T(8,128)S(1)}, f32[1024,256]{1,0:T(8,128)}, u32[]{:S(2)}) copy-start(f32[1024,256]{1,0:T(8,128)} %copy-done.2) | copy-start | bytes 3145732

commit v7 on v4

--- a/solution.py
+++ b/solution.py
@@ -359,13 +359,13 @@
 
 def first_products(place, weights, pieces, row_tiles, tile):
     depth = weights.shape[1]
-    vmem = pl.BlockSpec(memory_space=pltpu.VMEM)
+    piece = pl.BlockSpec(pieces[0].shape, lambda a: (0, 0))
     count = pieces[0].shape[0] * LANES // tile // tile
     return pl.pallas_call(
         functools.partial(products_kernel, tile, count),
         grid=(row_tiles,),
         out_shape=jax.ShapeDtypeStruct((row_tiles * tile, count * tile), F32),
-        in_specs=[pl.BlockSpec(memory_space=pltpu.SMEM), pl.BlockSpec((tile, depth), lambda a: (a, 0))] + [vmem] * 3,
+        in_specs=[pl.BlockSpec(memory_space=pltpu.SMEM), pl.BlockSpec((tile, depth), lambda a: (a, 0))] + [piece] * 3,
         out_specs=pl.BlockSpec((tile, count * tile), lambda a: (a, 0)),
         scratch_shapes=[pltpu.VMEM((depth, count * tile), BF16)],
         compiler_params=pltpu.CompilerParams(vmem_limit_bytes=24 * 1024 * 1024),
@@ -432,7 +432,7 @@
             pl.BlockSpec((tile, count * tile), lambda a: (a, group)),
         ]
         + [pl.BlockSpec((tile, tile), lambda a: (a, 0)) if group == 0 else pl.BlockSpec(memory_space=pl.ANY)]
-        + [pl.BlockSpec(memory_space=pltpu.VMEM)] * 3,
+        + [pl.BlockSpec(pieces[0].shape, lambda a: (0, 0))] * 3,
         out_specs=block_spec,
         scratch_shapes=[pltpu.VMEM((depth, count * tile), BF16)],
         input_output_aliases={} if group == 0 else {4: 0},
@@ -547,7 +547,7 @@
             weights, solved = row_weights(
                 jnp.stack([row, col, core]).astype(jnp.int32), rows_mine, rows_other, inverse, row_tiles, tile
             )
-            weights, near[1] = lax.optimization_barrier((weights, near[1]))
+            weights, near[1], first = lax.optimization_barrier((weights, near[1], first))
 
     ready = first_products(place, weights, first, row_tiles, tile)
     result = solved

time: 118 us -> 115 us (0.975)
  the two profiles are of different devices: /device:TPU:5 before, /device:TPU:16 now
where the time goes in v7:
time: 115 us; the launch traced here: 113 us
  Pallas kernels  55.7 us (48%)
  starting transfers between devices  32 us (28%)
  waiting for transfers between devices  14.5 us (13%)
  local copies, waits for them, and re-layouts  6.89 us (6%)
  other arithmetic  3.48 us (3%)
    ppermute x18, starting transfers between devices, send(): return lax.ppermute(value, AXES, pairs)  32 us
    pallas_call x2, Pallas kernels, trailing(): pl.pallas_call(functools.partial(trailing_kernel, tile, group, count), gr...  14.7 us
    ppermute x18, waiting for transfers between devices, send(): return lax.ppermute(value, AXES, pairs)  14.5 us
    pallas_call x1, Pallas kernels, corner_start(): pl.pallas_call(corner_start_kernel, out_shape=jax.ShapeDtypeStruct((width...  11.4 us
    pallas_call x1, Pallas kernels, corner_end(): pl.pallas_call(corner_end_kernel, out_shape=jax.ShapeDtypeStruct(state.sh...  10.3 us
    unnamed x24, local copies, waits for them, and re-layouts  6.68 us
    pallas_call x1, Pallas kernels, gather_pieces(): pl.pallas_call(functools.partial(gather_kernel, tile, col_tiles, row_tile...  6.42 us
    pallas_call x1, Pallas kernels, row_weights(): pl.pallas_call(functools.partial(weights_kernel, tile), grid=(row_tiles,)...  5.54 us
  transfers between devices with their start and end apart: 18, of which 7 were waited for; matrix products, arithmetic and copies ran while one was open for 2% of the time, Pallas kernels for 41%

profile of v7, /device:TPU:16, one launch (start us, length us, event | category | flops | bytes accessed | tf_op | source)
XLA Modules:
  0.0 113.0 jit_solution(13781301436784544213)
XLA Ops:
  0.0 2.1 %gather_lead.1.lead_ref = f32[512,128]{1,0:T(8,128)} custom-call(f32[1024,2,8,128]{3,2,1,0:T(8,128)} %bitcast.13), custom_call_target="tpu_custom_call" | custom-call | flops 1000 | bytes 1000 | tf_op jit(solution)/shard_map/gather_lead/pallas_call | solution.py:227
  2.1 3.4 %collective-permute-start = (f32[512,128]{1,0:T(8,128)}, f32[512,128]{1,0:T(8,128)S(1)}, u32[]{:S(2)}, u32[]{:S(2)}) collective-permute-start(f32[512,128]{1,0:T(8,128)} %gather_lead.1.lead_ref), channel_id=1, source_target_pairs={{0,2},{1,3},{4,6},{5,7},{8,10},{9,11},{12,14},{13,15},{16,18},{17,... | collective-permute-start | bytes 786440 | tf_op jit(solution)/shard_map/ppermute | solution.py:454
  5.5 6.4 %gather_pieces.1 = (f32[1536,128]{1,0:T(8,128)}, f32[2048,128]{1,0:T(8,128)}, f32[2048,128]{1,0:T(8,128)}, f32[2048,128]{1,0:T(8,128)}) custom-call(s32[1]{0:T(128)} %bitcast.9.place_ref, f32[512,128]{1,0:T(8,128)} %gather_lead.1.lead_ref, f32[1024,2,8,128]{3,2,1,0:T(8,128)} %bitcast.14, f32[16384,128]{1,0:T(8,128)} %bitcast.15), custom_call_target="tpu_custom_call" | custom-call | flops 1000 | bytes 1000 | tf_op jit(solution)/shard_map/gather_pieces/pallas_call | solution.py:244
  12.0 1.3 %collective-permute-start.1 = (f32[256,128]{1,0:T(8,128)S(1)}, f32[256,128]{1,0:T(8,128)S(1)}, u32[]{:S(2)}, u32[]{:S(2)}) collective-permute-start(f32[256,128]{1,0:T(8,128)S(1)} %slice_select_fusion.2), channel_id=1, source_target_pairs={{0,16},{1,17},{2,18},{3,19},{4,20},{5,21},{6,22},{7,23}} | collective-permute-start | bytes 393224 | tf_op jit(solution)/shard_map/ppermute | solution.py:454
  13.3 6.4 %collective-permute-done.1 = f32[256,128]{1,0:T(8,128)S(1)} collective-permute-done((f32[256,128]{1,0:T(8,128)S(1)}, f32[256,128]{1,0:T(8,128)S(1)}, u32[]{:S(2)}, u32[]{:S(2)}) %collective-permute-start.1) | collective-permute-done | bytes 131104 | tf_op jit(solution)/shard_map/ppermute | solution.py:454
  19.8 1.3 %collective-permute-start.2 = (f32[256,128]{1,0:T(8,128)S(1)}, f32[256,128]{1,0:T(8,128)S(1)}, u32[]{:S(2)}, u32[]{:S(2)}) collective-permute-start(f32[256,128]{1,0:T(8,128)S(1)} %broadcast_select_fusion.1), channel_id=1, source_target_pairs={{0,8},{1,9},{2,10},{3,11},{4,12},{5,13},{6,14},{7,15},{16,24},{17,... | collective-permute-start | bytes 393224 | tf_op jit(solution)/shard_map/ppermute | solution.py:454
  21.1 2.5 %collective-permute-done.2 = f32[256,128]{1,0:T(8,128)S(1)} collective-permute-done((f32[256,128]{1,0:T(8,128)S(1)}, f32[256,128]{1,0:T(8,128)S(1)}, u32[]{:S(2)}, u32[]{:S(2)}) %collective-permute-start.2) | collective-permute-done | bytes 131104 | tf_op jit(solution)/shard_map/ppermute | solution.py:454
  23.6 2.5 %collective-permute-start.7 = (f32[2048,128]{1,0:T(8,128)}, f32[2048,128]{1,0:T(8,128)S(1)}, u32[]{:S(2)}, u32[]{:S(2)}) collective-permute-start(f32[2048,128]{1,0:T(8,128)} %get-tuple-element.36), channel_id=1, source_target_pairs={{0,24},{1,25},{2,18},{3,19},{4,28},{5,29},{6,22},{7,23},{16,8},{17... | collective-permute-start | bytes 3145736 | tf_op jit(solution)/shard_map/ppermute | solution.py:454
  26.1 1.6 %collective-permute-start.5 = (f32[256,128]{1,0:T(8,128)S(1)}, f32[256,128]{1,0:T(8,128)S(1)}, u32[]{:S(2)}, u32[]{:S(2)}) collective-permute-start(f32[256,128]{1,0:T(8,128)S(1)} %broadcast_select_fusion.2), channel_id=1, source_target_pairs={{0,6},{1,7},{2,4},{3,5},{4,2},{5,3},{6,0},{7,1},{8,14},{9,15},{10,... | collective-permute-start | bytes 393224 | tf_op jit(solution)/shard_map/ppermute | solution.py:454
  27.8 0.5 collective-permute-start.3
  28.3 1.4 %collective-permute-start.4 = (f32[256,128]{1,0:T(8,128)S(1)}, f32[256,128]{1,0:T(8,128)S(1)}, u32[]{:S(2)}, u32[]{:S(2)}) collective-permute-start(f32[256,128]{1,0:T(8,128)S(1)} %broadcast_select_fusion.2), channel_id=1, source_target_pairs={{0,2},{1,3},{2,0},{3,1},{4,6},{5,7},{6,4},{7,5},{8,10},{9,11},{10,... | collective-permute-start | bytes 393224 | tf_op jit(solution)/shard_map/ppermute | solution.py:454
  29.7 2.4 %collective-permute-done.5 = f32[256,128]{1,0:T(8,128)S(1)} collective-permute-done((f32[256,128]{1,0:T(8,128)S(1)}, f32[256,128]{1,0:T(8,128)S(1)}, u32[]{:S(2)}, u32[]{:S(2)}) %collective-permute-start.5) | collective-permute-done | bytes 131104 | tf_op jit(solution)/shard_map/ppermute | solution.py:454
  32.1 2.6 %collective-permute-start.8 = (f32[1536,128]{1,0:T(8,128)}, f32[1536,128]{1,0:T(8,128)S(1)}, u32[]{:S(2)}, u32[]{:S(2)}) collective-permute-start(f32[1536,128]{1,0:T(8,128)} %get-tuple-element.40), channel_id=1, source_target_pairs={{0,2},{1,3},{4,6},{5,7},{8,10},{9,11},{12,14},{13,15},{16,18},{17,... | collective-permute-start | bytes 2359304 | tf_op jit(solution)/shard_map/ppermute | solution.py:454
  34.7 0.1 collective-permute-start.6
  34.8 0.1 pad_add_fusion.1.place_ref
  34.9 1.8 %collective-permute-done.6.other_ref = f32[1024,128]{1,0:T(8,128)S(1)} collective-permute-done((f32[1024,128]{1,0:T(8,128)S(1)}, f32[1024,128]{1,0:T(8,128)S(1)}, u32[]{:S(2)}, u32[]{:S(2)}) %collective-permute-start.6) | collective-permute-done | bytes 524320 | tf_op jit(solution)/shard_map/ppermute | solution.py:454
  36.7 11.4 %corner_start.1.state_ref = f32[512,512]{1,0:T(8,128)S(1)} custom-call(s32[3]{0:T(128)S(1)} %pad_add_fusion.1.place_ref, f32[1024,128]{1,0:T(8,128)S(1)} %constant_dynamic-update-slice_fusion.mine_ref, f32[1024,128]{1,0:T(8,128)S(1)} %collective-permute-done.6.other_ref), custom_call_target="tpu_custom_call" | custom-call | flops 1000 | bytes 1000 | tf_op jit(solution)/shard_map/corner_start/pallas_call | solution.py:150
  48.2 1.0 collective-permute-done.8
  49.1 0.1 constant_dynamic-update-slice_fusion.4
  49.2 1.5 %select_select_fusion = (f32[2048,128]{1,0:T(8,128)S(1)}, f32[2048,128]{1,0:T(8,128)S(1)}, f32[2048,128]{1,0:T(8,128)S(1)}) fusion(f32[2048,128]{1,0:T(8,128)} %get-tuple-element.45, f32[2048,128]{1,0:T(8,128)S(1)} %constant_dynamic-update-slice_fusion.4, f32[2048,128]{1,0:T(8,128)S(1)} %collective-permute-done.7, f32[2048,128]{1,0:T(8,128)} %get-tuple-element.36, ...), kind=kLoop, calls=%fused_computation | loop fusion | flops 2097152 | bytes 8388612 | tf_op jit(solution)/shard_map/jit(_where)/select_n | solution.py:531
  50.7 0.0 copy-start
  50.8 0.1 fusion
  50.8 0.1 collective-permute-start.9
  50.9 0.7 collective-permute-start.13
  51.6 3.4 %collective-permute-start.12 = (f32[2048,128]{1,0:T(8,128)S(1)}, f32[2048,128]{1,0:T(8,128)S(1)}, u32[]{:S(2)}, u32[]{:S(2)}) collective-permute-start(f32[2048,128]{1,0:T(8,128)S(1)} %get-tuple-element.53.piece_a), channel_id=1, source_target_pairs={{0,4},{1,5},{2,6},{3,7},{4,0},{5,1},{6,2},{7,3},{8,12},{9,8},{10,1... | collective-permute-start | bytes 3145736 | tf_op jit(solution)/shard_map/ppermute | solution.py:454
  55.0 5.3 %collective-permute-start.10 = (f32[1024,128]{1,0:T(8,128)S(1)}, f32[1024,128]{1,0:T(8,128)S(1)}, u32[]{:S(2)}, u32[]{:S(2)}) collective-permute-start(f32[1024,128]{1,0:T(8,128)S(1)} %get-tuple-element.47), channel_id=1, source_target_pairs={{0,8},{1,9},{2,10},{3,11},{4,12},{5,13},{6,14},{7,15},{10,26},{11,... | collective-permute-start | bytes 1572872 | tf_op jit(solution)/shard_map/ppermute | solution.py:454
  60.3 2.1 %collective-permute-start.11 = (f32[1024,128]{1,0:T(8,128)S(1)}, f32[1024,128]{1,0:T(8,128)S(1)}, u32[]{:S(2)}, u32[]{:S(2)}) collective-permute-start(f32[1024,128]{1,0:T(8,128)S(1)} %get-tuple-element.50), channel_id=1, source_target_pairs={{0,8},{1,9},{2,10},{3,11},{4,12},{5,13},{6,14},{7,15},{10,26},{11,... | collective-permute-start | bytes 1572872 | tf_op jit(solution)/shard_map/ppermute | solution.py:454
  62.4 0.1 pad_add_fusion.place_ref
  62.5 10.3 %corner_end.1.inverse_ref = f32[512,512]{1,0:T(8,128)S(1)} custom-call(f32[512,512]{1,0:T(8,128)S(1)} %corner_start.1.state_ref), custom_call_target="tpu_custom_call" | custom-call | flops 1000 | bytes 1000 | tf_op jit(solution)/shard_map/corner_end/pallas_call | solution.py:163
  72.8 0.3 collective-permute-done.10
  73.1 0.9 slice_select_fusion.1.rest_1_
  74.0 1.5 %collective-permute-start.15 = (f32[1024,128]{1,0:T(8,128)}, f32[1024,128]{1,0:T(8,128)}, u32[]{:S(2)}, u32[]{:S(2)}) collective-permute-start(f32[1024,128]{1,0:T(8,128)} %slice_select_fusion.1.rest_1_), channel_id=1, source_target_pairs={{9,12},{12,9},{17,20},{19,22},{20,17},{22,19},{25,28},{27,30},{28,... | collective-permute-start | bytes 1572872 | tf_op jit(solution)/shard_map/ppermute | solution.py:454
  75.4 1.1 collective-permute-start.14
  76.5 5.5 %row_weights.1 = (bf16[1024,1536]{1,0:T(8,128)(2,1)S(1)}, f32[1024,256]{1,0:T(8,128)S(1)}) custom-call(s32[3]{0:T(128)S(1)} %pad_add_fusion.place_ref, f32[2048,128]{1,0:T(8,128)S(1)} %get-tuple-element.61.rows_mine, f32[2048,128]{1,0:T(8,128)S(1)} %collective-permute-done.9.rows_other, f32[512,512]{1,0:T(8,128)S(1)} %corner_end.1.inverse_ref), custom_call_target="tpu_custom_call" | custom-call | flops 1000 | bytes 1000 | tf_op jit(solution)/shard_map/row_weights/pallas_call | solution.py:315
  82.1 1.0 copy-done.2
  83.0 0.1 collective-permute-done.11
  83.1 1.0 copy-done.4
  84.1 1.0 copy-done.6
  85.1 0.9 slice_select_fusion.rest_1_
  86.0 1.5 %collective-permute-start.17 = (f32[1024,128]{1,0:T(8,128)}, f32[1024,128]{1,0:T(8,128)}, u32[]{:S(2)}, u32[]{:S(2)}) collective-permute-start(f32[1024,128]{1,0:T(8,128)} %slice_select_fusion.rest_1_), channel_id=1, source_target_pairs={{9,12},{12,9},{17,20},{19,22},{20,17},{22,19},{25,28},{27,30},{28,... | collective-permute-start | bytes 1572872 | tf_op jit(solution)/shard_map/ppermute | solution.py:454
  87.4 1.7 %collective-permute-start.16 = (f32[1024,128]{1,0:T(8,128)}, f32[1024,128]{1,0:T(8,128)}, u32[]{:S(2)}, u32[]{:S(2)}) collective-permute-start(f32[1024,128]{1,0:T(8,128)} %slice_select_fusion.rest_1_), channel_id=1, source_target_pairs={{0,4},{1,5},{2,6},{3,7},{4,0},{5,1},{6,2},{7,3},{8,12},{9,8},{10,1... | collective-permute-start | bytes 1572872 | tf_op jit(solution)/shard_map/ppermute | solution.py:454
  89.1 0.1 stack.47.place_ref
  89.2 1.2 %copy-done.1 = f32[2048,128]{1,0:T(8,128)S(1)} copy-done((f32[2048,128]{1,0:T(8,128)S(1)}, f32[2048,128]{1,0:T(8,128)}, u32[]{:S(2)}) %copy-start.1) | copy-done | bytes 1048600
  90.5 1.2 %copy-done.5 = f32[2048,128]{1,0:T(8,128)S(1)} copy-done((f32[2048,128]{1,0:T(8,128)S(1)}, f32[2048,128]{1,0:T(8,128)}, u32[]{:S(2)}) %copy-start.5) | copy-done | bytes 1048600
  91.7 1.2 %copy-done.7 = f32[2048,128]{1,0:T(8,128)S(1)} copy-done((f32[2048,128]{1,0:T(8,128)S(1)}, f32[2048,128]{1,0:T(8,128)}, u32[]{:S(2)}) %copy-start.7) | copy-done | bytes 1048600
  92.9 5.3 %first_products.1.ready_ref = f32[1024,1024]{1,0:T(8,128)S(1)} custom-call(s32[7]{0:T(128)S(1)} %stack.47.place_ref, bf16[1024,1536]{1,0:T(8,128)(2,1)S(1)} %get-tuple-element.52.weights_ref, f32[2048,128]{1,0:T(8,128)S(1)} %copy-done.1, f32[2048,128]{1,0:T(8,128)S(1)} %copy-done.7, f32[2048,128]{1,0:T(8,128)S(1)} %copy-done.5), custom_call_target="tpu_custom_call" | custom-call | flops 1000 | bytes 1000 | tf_op jit(solution)/shard_map/first_products/pallas_call | solution.py:364
  98.3 7.4 %trailing_0.1.rest_0_ = f32[1024,2,8,128]{3,2,1,0:T(8,128)} custom-call(s32[7]{0:T(128)S(1)} %stack.47.place_ref, f32[1024,2,8,128]{3,2,1,0:T(8,128)} %bitcast.16, bf16[1024,1536]{1,0:T(8,128)(2,1)S(1)} %get-tuple-element.52.weights_ref, f32[1024,1024]{1,0:T(8,128)S(1)} %first_products.1.ready_ref, f32[1024,256]{1,0:T(8,128)S(1)} %copy-done.3, ...), custom_call_target="tpu_custom_call" | custom-call | flops 1000 | bytes 1000 | tf_op jit(solution)/shard_map/trailing_0/pallas_call | solution.py:424
  105.7 7.2 %trailing_1.1 = f32[1024,2,8,128]{3,2,1,0:T(8,128)} custom-call(s32[7]{0:T(128)S(1)} %stack.47.place_ref, f32[1024,2,8,128]{3,2,1,0:T(8,128)} %bitcast.17, bf16[1024,1536]{1,0:T(8,128)(2,1)S(1)} %get-tuple-element.52.weights_ref, f32[1024,1024]{1,0:T(8,128)S(1)} %first_products.1.ready_ref, ...), custom_call_target="tpu_custom_call", output_to_operand_aliasing={{}: (4, {})} | custom-call | flops 1000 | bytes 1000 | tf_op jit(solution)/shard_map/trailing_1/pallas_call | solution.py:424
  (32 shorter events, 0.2 us)
Async XLA Ops:
  2.1 9.9 %collective-permute-start = (f32[512,128]{1,0:T(8,128)}, f32[512,128]{1,0:T(8,128)S(1)}, u32[]{:S(2)}, u32[]{:S(2)}) collective-permute-start(f32[512,128]{1,0:T(8,128)} %gather_lead.1.lead_ref), channel_id=1, source_target_pairs={{0,2},{1,3},{4,6},{5,7},{8,10},{9,11},{12,14},{13,15},{16,18},{17,... | collective-permute-start | bytes 786440 | tf_op jit(solution)/shard_map/ppermute | solution.py:454
  5.5 6.4 %copy-start.9 = (f32[512,128]{1,0:T(8,128)S(1)}, f32[512,128]{1,0:T(8,128)}, u32[]{:S(2)}) copy-start(f32[512,128]{1,0:T(8,128)} %gather_lead.1.lead_ref) | copy-start | bytes 786436
  12.0 7.8 %collective-permute-start.1 = (f32[256,128]{1,0:T(8,128)S(1)}, f32[256,128]{1,0:T(8,128)S(1)}, u32[]{:S(2)}, u32[]{:S(2)}) collective-permute-start(f32[256,128]{1,0:T(8,128)S(1)} %slice_select_fusion.2), channel_id=1, source_target_pairs={{0,16},{1,17},{2,18},{3,19},{4,20},{5,21},{6,22},{7,23}} | collective-permute-start | bytes 393224 | tf_op jit(solution)/shard_map/ppermute | solution.py:454
  19.8 3.8 %collective-permute-start.2 = (f32[256,128]{1,0:T(8,128)S(1)}, f32[256,128]{1,0:T(8,128)S(1)}, u32[]{:S(2)}, u32[]{:S(2)}) collective-permute-start(f32[256,128]{1,0:T(8,128)S(1)} %broadcast_select_fusion.1), channel_id=1, source_target_pairs={{0,8},{1,9},{2,10},{3,11},{4,12},{5,13},{6,14},{7,15},{16,24},{17,... | collective-permute-start | bytes 393224 | tf_op jit(solution)/shard_map/ppermute | solution.py:454
  23.6 25.5 %collective-permute-start.7 = (f32[2048,128]{1,0:T(8,128)}, f32[2048,128]{1,0:T(8,128)S(1)}, u32[]{:S(2)}, u32[]{:S(2)}) collective-permute-start(f32[2048,128]{1,0:T(8,128)} %get-tuple-element.36), channel_id=1, source_target_pairs={{0,24},{1,25},{2,18},{3,19},{4,28},{5,29},{6,22},{7,23},{16,8},{17... | collective-permute-start | bytes 3145736 | tf_op jit(solution)/shard_map/ppermute | solution.py:454
  26.1 5.9 %collective-permute-start.5 = (f32[256,128]{1,0:T(8,128)S(1)}, f32[256,128]{1,0:T(8,128)S(1)}, u32[]{:S(2)}, u32[]{:S(2)}) collective-permute-start(f32[256,128]{1,0:T(8,128)S(1)} %broadcast_select_fusion.2), channel_id=1, source_target_pairs={{0,6},{1,7},{2,4},{3,5},{4,2},{5,3},{6,0},{7,1},{8,14},{9,15},{10,... | collective-permute-start | bytes 393224 | tf_op jit(solution)/shard_map/ppermute | solution.py:454
  27.8 6.9 %collective-permute-start.3 = (f32[256,128]{1,0:T(8,128)S(1)}, f32[256,128]{1,0:T(8,128)S(1)}, u32[]{:S(2)}, u32[]{:S(2)}) collective-permute-start(f32[256,128]{1,0:T(8,128)S(1)} %broadcast_select_fusion.2), channel_id=1, source_target_pairs={{0,4},{1,5},{2,6},{3,7},{4,0},{5,1},{6,2},{7,3},{8,12},{9,13},{10,... | collective-permute-start | bytes 393224 | tf_op jit(solution)/shard_map/ppermute | solution.py:454
  28.3 6.4 %collective-permute-start.4 = (f32[256,128]{1,0:T(8,128)S(1)}, f32[256,128]{1,0:T(8,128)S(1)}, u32[]{:S(2)}, u32[]{:S(2)}) collective-permute-start(f32[256,128]{1,0:T(8,128)S(1)} %broadcast_select_fusion.2), channel_id=1, source_target_pairs={{0,2},{1,3},{2,0},{3,1},{4,6},{5,7},{6,4},{7,5},{8,10},{9,11},{10,... | collective-permute-start | bytes 393224 | tf_op jit(solution)/shard_map/ppermute | solution.py:454
  32.1 17.1 %collective-permute-start.8 = (f32[1536,128]{1,0:T(8,128)}, f32[1536,128]{1,0:T(8,128)S(1)}, u32[]{:S(2)}, u32[]{:S(2)}) collective-permute-start(f32[1536,128]{1,0:T(8,128)} %get-tuple-element.40), channel_id=1, source_target_pairs={{0,2},{1,3},{4,6},{5,7},{8,10},{9,11},{12,14},{13,15},{16,18},{17,... | collective-permute-start | bytes 2359304 | tf_op jit(solution)/shard_map/ppermute | solution.py:454
  34.7 2.0 %collective-permute-start.6 = (f32[1024,128]{1,0:T(8,128)S(1)}, f32[1024,128]{1,0:T(8,128)S(1)}, u32[]{:S(2)}, u32[]{:S(2)}) collective-permute-start(f32[1024,128]{1,0:T(8,128)S(1)} %constant_dynamic-update-slice_fusion.mine_ref), channel_id=1, source_target_pairs={{0,1},{1,0},{2,3},{3,2},{4,5},{5,4},{6,7},{7,6},{8,9},{9,8},{10,11... | collective-permute-start | bytes 1572872 | tf_op jit(solution)/shard_map/ppermute | solution.py:454
  34.9 38.2 %copy-start.8 = (f32[2048,128]{1,0:T(8,128)S(1)}, f32[2048,128]{1,0:T(8,128)}, u32[]{:S(2)}) copy-start(f32[2048,128]{1,0:T(8,128)} %get-tuple-element.45) | copy-start | bytes 3145732
  50.7 31.3 %copy-start = (f32[2048,128]{1,0:T(8,128)}, f32[2048,128]{1,0:T(8,128)S(1)}, u32[]{:S(2)}) copy-start(f32[2048,128]{1,0:T(8,128)S(1)} %get-tuple-element.53.piece_a) | copy-start | bytes 3145732
  50.8 24.6 %collective-permute-start.9 = (f32[2048,128]{1,0:T(8,128)S(1)}, f32[2048,128]{1,0:T(8,128)S(1)}, u32[]{:S(2)}, u32[]{:S(2)}) collective-permute-start(f32[2048,128]{1,0:T(8,128)S(1)} %get-tuple-element.61.rows_mine), channel_id=1, source_target_pairs={{0,1},{1,0},{2,3},{3,2},{4,5},{5,4},{6,7},{7,6},{8,9},{9,8},{10,11... | collective-permute-start | bytes 3145736 | tf_op jit(solution)/shard_map/ppermute | solution.py:454
  50.9 32.2 %collective-permute-start.13 = (f32[2048,128]{1,0:T(8,128)S(1)}, f32[2048,128]{1,0:T(8,128)S(1)}, u32[]{:S(2)}, u32[]{:S(2)}) collective-permute-start(f32[2048,128]{1,0:T(8,128)S(1)} %get-tuple-element.53.piece_a), channel_id=1, source_target_pairs={{9,12},{11,14},{12,9},{14,11},{17,20},{20,17},{25,28},{27,30},{28,... | collective-permute-start | bytes 3145736 | tf_op jit(solution)/shard_map/ppermute | solution.py:454
  51.6 32.5 %collective-permute-start.12 = (f32[2048,128]{1,0:T(8,128)S(1)}, f32[2048,128]{1,0:T(8,128)S(1)}, u32[]{:S(2)}, u32[]{:S(2)}) collective-permute-start(f32[2048,128]{1,0:T(8,128)S(1)} %get-tuple-element.53.piece_a), channel_id=1, source_target_pairs={{0,4},{1,5},{2,6},{3,7},{4,0},{5,1},{6,2},{7,3},{8,12},{9,8},{10,1... | collective-permute-start | bytes 3145736 | tf_op jit(solution)/shard_map/ppermute | solution.py:454
  55.0 18.1 %collective-permute-start.10 = (f32[1024,128]{1,0:T(8,128)S(1)}, f32[1024,128]{1,0:T(8,128)S(1)}, u32[]{:S(2)}, u32[]{:S(2)}) collective-permute-start(f32[1024,128]{1,0:T(8,128)S(1)} %get-tuple-element.47), channel_id=1, source_target_pairs={{0,8},{1,9},{2,10},{3,11},{4,12},{5,13},{6,14},{7,15},{10,26},{11,... | collective-permute-start | bytes 1572872 | tf_op jit(solution)/shard_map/ppermute | solution.py:454
  60.3 22.8 %collective-permute-start.11 = (f32[1024,128]{1,0:T(8,128)S(1)}, f32[1024,128]{1,0:T(8,128)S(1)}, u32[]{:S(2)}, u32[]{:S(2)}) collective-permute-start(f32[1024,128]{1,0:T(8,128)S(1)} %get-tuple-element.50), channel_id=1, source_target_pairs={{0,8},{1,9},{2,10},{3,11},{4,12},{5,13},{6,14},{7,15},{10,26},{11,... | collective-permute-start | bytes 1572872 | tf_op jit(solution)/shard_map/ppermute | solution.py:454
  74.0 24.3 %collective-permute-start.15 = (f32[1024,128]{1,0:T(8,128)}, f32[1024,128]{1,0:T(8,128)}, u32[]{:S(2)}, u32[]{:S(2)}) collective-permute-start(f32[1024,128]{1,0:T(8,128)} %slice_select_fusion.1.rest_1_), channel_id=1, source_target_pairs={{9,12},{12,9},{17,20},{19,22},{20,17},{22,19},{25,28},{27,30},{28,... | collective-permute-start | bytes 1572872 | tf_op jit(solution)/shard_map/ppermute | solution.py:454
  75.4 22.8 %collective-permute-start.14 = (f32[1024,128]{1,0:T(8,128)}, f32[1024,128]{1,0:T(8,128)}, u32[]{:S(2)}, u32[]{:S(2)}) collective-permute-start(f32[1024,128]{1,0:T(8,128)} %slice_select_fusion.1.rest_1_), channel_id=1, source_target_pairs={{0,4},{1,5},{2,6},{3,7},{4,0},{5,1},{6,2},{7,3},{8,12},{9,8},{10,1... | collective-permute-start | bytes 1572872 | tf_op jit(solution)/shard_map/ppermute | solution.py:454
  82.1 1.0 copy-start.2
  83.1 1.0 copy-start.4
  84.1 1.0 copy-start.6
  86.0 19.8 %collective-permute-start.17 = (f32[1024,128]{1,0:T(8,128)}, f32[1024,128]{1,0:T(8,128)}, u32[]{:S(2)}, u32[]{:S(2)}) collective-permute-start(f32[1024,128]{1,0:T(8,128)} %slice_select_fusion.rest_1_), channel_id=1, source_target_pairs={{9,12},{12,9},{17,20},{19,22},{20,17},{22,19},{25,28},{27,30},{28,... | collective-permute-start | bytes 1572872 | tf_op jit(solution)/shard_map/ppermute | solution.py:454
  87.4 18.3 %collective-permute-start.16 = (f32[1024,128]{1,0:T(8,128)}, f32[1024,128]{1,0:T(8,128)}, u32[]{:S(2)}, u32[]{:S(2)}) collective-permute-start(f32[1024,128]{1,0:T(8,128)} %slice_select_fusion.rest_1_), channel_id=1, source_target_pairs={{0,4},{1,5},{2,6},{3,7},{4,0},{5,1},{6,2},{7,3},{8,12},{9,8},{10,1... | collective-permute-start | bytes 1572872 | tf_op jit(solution)/shard_map/ppermute | solution.py:454
  89.2 1.2 %copy-start.1 = (f32[2048,128]{1,0:T(8,128)S(1)}, f32[2048,128]{1,0:T(8,128)}, u32[]{:S(2)}) copy-start(f32[2048,128]{1,0:T(8,128)} %copy-done) | copy-start | bytes 3145732
  90.5 1.2 %copy-start.5 = (f32[2048,128]{1,0:T(8,128)S(1)}, f32[2048,128]{1,0:T(8,128)}, u32[]{:S(2)}) copy-start(f32[2048,128]{1,0:T(8,128)} %copy-done.4) | copy-start | bytes 3145732
  91.7 1.2 %copy-start.7 = (f32[2048,128]{1,0:T(8,128)S(1)}, f32[2048,128]{1,0:T(8,128)}, u32[]{:S(2)}) copy-start(f32[2048,128]{1,0:T(8,128)} %copy-done.6) | copy-start | bytes 3145732
  92.9 5.4 %copy-start.3 = (f32[1024,256]{1,0:T(8,128)S(1)}, f32[1024,256]{1,0:T(8,128)}, u32[]{:S(2)}) copy-start(f32[1024,256]{1,0:T(8,128)} %copy-done.2) | copy-start | bytes 3145732

commit v8 on v7

--- a/solution.py
+++ b/solution.py
@@ -324,7 +324,7 @@
         ],
         out_specs=[pl.BlockSpec((tile, 3 * depth), lambda a: (a, 0)), pl.BlockSpec((tile, tile), lambda a: (a, 0))],
         scratch_shapes=[pltpu.VMEM((depth, 3 * depth), BF16), pltpu.VMEM((3 * depth, depth), BF16)],
-        compiler_params=pltpu.CompilerParams(vmem_limit_bytes=32 * 1024 * 1024),
+        compiler_params=pltpu.CompilerParams(vmem_limit_bytes=18 * 1024 * 1024),
         cost_estimate=COST,
         name="row_weights",
     )(place, rows_mine, rows_other, inverse)
@@ -368,7 +368,7 @@
         in_specs=[pl.BlockSpec(memory_space=pltpu.SMEM), pl.BlockSpec((tile, depth), lambda a: (a, 0))] + [piece] * 3,
         out_specs=pl.BlockSpec((tile, count * tile), lambda a: (a, 0)),
         scratch_shapes=[pltpu.VMEM((depth, count * tile), BF16)],
-        compiler_params=pltpu.CompilerParams(vmem_limit_bytes=24 * 1024 * 1024),
+        compiler_params=pltpu.CompilerParams(vmem_limit_bytes=20 * 1024 * 1024),
         cost_estimate=COST,
         name="first_products",
     )(place, weights, *pieces)

time: 115 us -> 115 us (level)
  no operation moved by 1% of the time
where the time goes in v8:
time: 115 us; the launch traced here: 113 us
  Pallas kernels  55.7 us (48%)
  starting transfers between devices  32 us (28%)
  waiting for transfers between devices  14.5 us (13%)
  local copies, waits for them, and re-layouts  6.89 us (6%)
  other arithmetic  3.48 us (3%)
    ppermute x18, starting transfers between devices, send(): return lax.ppermute(value, AXES, pairs)  32 us
    pallas_call x2, Pallas kernels, trailing(): pl.pallas_call(functools.partial(trailing_kernel, tile, group, count), gr...  14.7 us
    ppermute x18, waiting for transfers between devices, send(): return lax.ppermute(value, AXES, pairs)  14.5 us
    pallas_call x1, Pallas kernels, corner_start(): pl.pallas_call(corner_start_kernel, out_shape=jax.ShapeDtypeStruct((width...  11.4 us
    pallas_call x1, Pallas kernels, corner_end(): pl.pallas_call(corner_end_kernel, out_shape=jax.ShapeDtypeStruct(state.sh...  10.3 us
    unnamed x24, local copies, waits for them, and re-layouts  6.68 us
    pallas_call x1, Pallas kernels, gather_pieces(): pl.pallas_call(functools.partial(gather_kernel, tile, col_tiles, row_tile...  6.42 us
    pallas_call x1, Pallas kernels, row_weights(): pl.pallas_call(functools.partial(weights_kernel, tile), grid=(row_tiles,)...  5.54 us
  transfers between devices with their start and end apart: 18, of which 7 were waited for; matrix products, arithmetic and copies ran while one was open for 2% of the time, Pallas kernels for 41%

profile of v8, /device:TPU:16, one launch (start us, length us, event | category | flops | bytes accessed | tf_op | source)
XLA Modules:
  0.0 113.0 jit_solution(1576822294430563556)
XLA Ops:
  0.0 2.1 %gather_lead.1.lead_ref = f32[512,128]{1,0:T(8,128)} custom-call(f32[1024,2,8,128]{3,2,1,0:T(8,128)} %bitcast.13), custom_call_target="tpu_custom_call" | custom-call | flops 1000 | bytes 1000 | tf_op jit(solution)/shard_map/gather_lead/pallas_call | solution.py:227
  2.1 3.4 %collective-permute-start = (f32[512,128]{1,0:T(8,128)}, f32[512,128]{1,0:T(8,128)S(1)}, u32[]{:S(2)}, u32[]{:S(2)}) collective-permute-start(f32[512,128]{1,0:T(8,128)} %gather_lead.1.lead_ref), channel_id=1, source_target_pairs={{0,2},{1,3},{4,6},{5,7},{8,10},{9,11},{12,14},{13,15},{16,18},{17,... | collective-permute-start | bytes 786440 | tf_op jit(solution)/shard_map/ppermute | solution.py:454
  5.5 6.4 %gather_pieces.1 = (f32[1536,128]{1,0:T(8,128)}, f32[2048,128]{1,0:T(8,128)}, f32[2048,128]{1,0:T(8,128)}, f32[2048,128]{1,0:T(8,128)}) custom-call(s32[1]{0:T(128)} %bitcast.9.place_ref, f32[512,128]{1,0:T(8,128)} %gather_lead.1.lead_ref, f32[1024,2,8,128]{3,2,1,0:T(8,128)} %bitcast.14, f32[16384,128]{1,0:T(8,128)} %bitcast.15), custom_call_target="tpu_custom_call" | custom-call | flops 1000 | bytes 1000 | tf_op jit(solution)/shard_map/gather_pieces/pallas_call | solution.py:244
  12.0 1.3 %collective-permute-start.1 = (f32[256,128]{1,0:T(8,128)S(1)}, f32[256,128]{1,0:T(8,128)S(1)}, u32[]{:S(2)}, u32[]{:S(2)}) collective-permute-start(f32[256,128]{1,0:T(8,128)S(1)} %slice_select_fusion.2), channel_id=1, source_target_pairs={{0,16},{1,17},{2,18},{3,19},{4,20},{5,21},{6,22},{7,23}} | collective-permute-start | bytes 393224 | tf_op jit(solution)/shard_map/ppermute | solution.py:454
  13.3 6.4 %collective-permute-done.1 = f32[256,128]{1,0:T(8,128)S(1)} collective-permute-done((f32[256,128]{1,0:T(8,128)S(1)}, f32[256,128]{1,0:T(8,128)S(1)}, u32[]{:S(2)}, u32[]{:S(2)}) %collective-permute-start.1) | collective-permute-done | bytes 131104 | tf_op jit(solution)/shard_map/ppermute | solution.py:454
  19.8 1.3 %collective-permute-start.2 = (f32[256,128]{1,0:T(8,128)S(1)}, f32[256,128]{1,0:T(8,128)S(1)}, u32[]{:S(2)}, u32[]{:S(2)}) collective-permute-start(f32[256,128]{1,0:T(8,128)S(1)} %broadcast_select_fusion.1), channel_id=1, source_target_pairs={{0,8},{1,9},{2,10},{3,11},{4,12},{5,13},{6,14},{7,15},{16,24},{17,... | collective-permute-start | bytes 393224 | tf_op jit(solution)/shard_map/ppermute | solution.py:454
  21.1 2.5 %collective-permute-done.2 = f32[256,128]{1,0:T(8,128)S(1)} collective-permute-done((f32[256,128]{1,0:T(8,128)S(1)}, f32[256,128]{1,0:T(8,128)S(1)}, u32[]{:S(2)}, u32[]{:S(2)}) %collective-permute-start.2) | collective-permute-done | bytes 131104 | tf_op jit(solution)/shard_map/ppermute | solution.py:454
  23.6 2.5 %collective-permute-start.7 = (f32[2048,128]{1,0:T(8,128)}, f32[2048,128]{1,0:T(8,128)S(1)}, u32[]{:S(2)}, u32[]{:S(2)}) collective-permute-start(f32[2048,128]{1,0:T(8,128)} %get-tuple-element.36), channel_id=1, source_target_pairs={{0,24},{1,25},{2,18},{3,19},{4,28},{5,29},{6,22},{7,23},{16,8},{17... | collective-permute-start | bytes 3145736 | tf_op jit(solution)/shard_map/ppermute | solution.py:454
  26.1 1.6 %collective-permute-start.5 = (f32[256,128]{1,0:T(8,128)S(1)}, f32[256,128]{1,0:T(8,128)S(1)}, u32[]{:S(2)}, u32[]{:S(2)}) collective-permute-start(f32[256,128]{1,0:T(8,128)S(1)} %broadcast_select_fusion.2), channel_id=1, source_target_pairs={{0,6},{1,7},{2,4},{3,5},{4,2},{5,3},{6,0},{7,1},{8,14},{9,15},{10,... | collective-permute-start | bytes 393224 | tf_op jit(solution)/shard_map/ppermute | solution.py:454
  27.8 0.5 collective-permute-start.3
  28.3 1.4 %collective-permute-start.4 = (f32[256,128]{1,0:T(8,128)S(1)}, f32[256,128]{1,0:T(8,128)S(1)}, u32[]{:S(2)}, u32[]{:S(2)}) collective-permute-start(f32[256,128]{1,0:T(8,128)S(1)} %broadcast_select_fusion.2), channel_id=1, source_target_pairs={{0,2},{1,3},{2,0},{3,1},{4,6},{5,7},{6,4},{7,5},{8,10},{9,11},{10,... | collective-permute-start | bytes 393224 | tf_op jit(solution)/shard_map/ppermute | solution.py:454
  29.7 2.4 %collective-permute-done.5 = f32[256,128]{1,0:T(8,128)S(1)} collective-permute-done((f32[256,128]{1,0:T(8,128)S(1)}, f32[256,128]{1,0:T(8,128)S(1)}, u32[]{:S(2)}, u32[]{:S(2)}) %collective-permute-start.5) | collective-permute-done | bytes 131104 | tf_op jit(solution)/shard_map/ppermute | solution.py:454
  32.1 2.6 %collective-permute-start.8 = (f32[1536,128]{1,0:T(8,128)}, f32[1536,128]{1,0:T(8,128)S(1)}, u32[]{:S(2)}, u32[]{:S(2)}) collective-permute-start(f32[1536,128]{1,0:T(8,128)} %get-tuple-element.40), channel_id=1, source_target_pairs={{0,2},{1,3},{4,6},{5,7},{8,10},{9,11},{12,14},{13,15},{16,18},{17,... | collective-permute-start | bytes 2359304 | tf_op jit(solution)/shard_map/ppermute | solution.py:454
  34.7 0.1 collective-permute-start.6
  34.8 0.1 pad_add_fusion.1.place_ref
  34.9 1.8 %collective-permute-done.6.other_ref = f32[1024,128]{1,0:T(8,128)S(1)} collective-permute-done((f32[1024,128]{1,0:T(8,128)S(1)}, f32[1024,128]{1,0:T(8,128)S(1)}, u32[]{:S(2)}, u32[]{:S(2)}) %collective-permute-start.6) | collective-permute-done | bytes 524320 | tf_op jit(solution)/shard_map/ppermute | solution.py:454
  36.7 11.4 %corner_start.1.state_ref = f32[512,512]{1,0:T(8,128)S(1)} custom-call(s32[3]{0:T(128)S(1)} %pad_add_fusion.1.place_ref, f32[1024,128]{1,0:T(8,128)S(1)} %constant_dynamic-update-slice_fusion.mine_ref, f32[1024,128]{1,0:T(8,128)S(1)} %collective-permute-done.6.other_ref), custom_call_target="tpu_custom_call" | custom-call | flops 1000 | bytes 1000 | tf_op jit(solution)/shard_map/corner_start/pallas_call | solution.py:150
  48.2 1.0 collective-permute-done.8
  49.1 0.1 constant_dynamic-update-slice_fusion.4
  49.2 1.5 %select_select_fusion = (f32[2048,128]{1,0:T(8,128)S(1)}, f32[2048,128]{1,0:T(8,128)S(1)}, f32[2048,128]{1,0:T(8,128)S(1)}) fusion(f32[2048,128]{1,0:T(8,128)} %get-tuple-element.45, f32[2048,128]{1,0:T(8,128)S(1)} %constant_dynamic-update-slice_fusion.4, f32[2048,128]{1,0:T(8,128)S(1)} %collective-permute-done.7, f32[2048,128]{1,0:T(8,128)} %get-tuple-element.36, ...), kind=kLoop, calls=%fused_computation | loop fusion | flops 2097152 | bytes 8388612 | tf_op jit(solution)/shard_map/jit(_where)/select_n | solution.py:531
  50.7 0.0 copy-start
  50.8 0.1 fusion
  50.8 0.1 collective-permute-start.9
  50.9 0.7 collective-permute-start.13
  51.6 3.4 %collective-permute-start.12 = (f32[2048,128]{1,0:T(8,128)S(1)}, f32[2048,128]{1,0:T(8,128)S(1)}, u32[]{:S(2)}, u32[]{:S(2)}) collective-permute-start(f32[2048,128]{1,0:T(8,128)S(1)} %get-tuple-element.53.piece_a), channel_id=1, source_target_pairs={{0,4},{1,5},{2,6},{3,7},{4,0},{5,1},{6,2},{7,3},{8,12},{9,8},{10,1... | collective-permute-start | bytes 3145736 | tf_op jit(solution)/shard_map/ppermute | solution.py:454
  55.0 5.3 %collective-permute-start.10 = (f32[1024,128]{1,0:T(8,128)S(1)}, f32[1024,128]{1,0:T(8,128)S(1)}, u32[]{:S(2)}, u32[]{:S(2)}) collective-permute-start(f32[1024,128]{1,0:T(8,128)S(1)} %get-tuple-element.47), channel_id=1, source_target_pairs={{0,8},{1,9},{2,10},{3,11},{4,12},{5,13},{6,14},{7,15},{10,26},{11,... | collective-permute-start | bytes 1572872 | tf_op jit(solution)/shard_map/ppermute | solution.py:454
  60.3 2.1 %collective-permute-start.11 = (f32[1024,128]{1,0:T(8,128)S(1)}, f32[1024,128]{1,0:T(8,128)S(1)}, u32[]{:S(2)}, u32[]{:S(2)}) collective-permute-start(f32[1024,128]{1,0:T(8,128)S(1)} %get-tuple-element.50), channel_id=1, source_target_pairs={{0,8},{1,9},{2,10},{3,11},{4,12},{5,13},{6,14},{7,15},{10,26},{11,... | collective-permute-start | bytes 1572872 | tf_op jit(solution)/shard_map/ppermute | solution.py:454
  62.4 0.1 pad_add_fusion.place_ref
  62.5 10.3 %corner_end.1.inverse_ref = f32[512,512]{1,0:T(8,128)S(1)} custom-call(f32[512,512]{1,0:T(8,128)S(1)} %corner_start.1.state_ref), custom_call_target="tpu_custom_call" | custom-call | flops 1000 | bytes 1000 | tf_op jit(solution)/shard_map/corner_end/pallas_call | solution.py:163
  72.8 0.3 collective-permute-done.10
  73.1 0.9 slice_select_fusion.1.rest_1_
  74.0 1.5 %collective-permute-start.15 = (f32[1024,128]{1,0:T(8,128)}, f32[1024,128]{1,0:T(8,128)}, u32[]{:S(2)}, u32[]{:S(2)}) collective-permute-start(f32[1024,128]{1,0:T(8,128)} %slice_select_fusion.1.rest_1_), channel_id=1, source_target_pairs={{9,12},{12,9},{17,20},{19,22},{20,17},{22,19},{25,28},{27,30},{28,... | collective-permute-start | bytes 1572872 | tf_op jit(solution)/shard_map/ppermute | solution.py:454
  75.4 1.1 collective-permute-start.14
  76.5 5.5 %row_weights.1 = (bf16[1024,1536]{1,0:T(8,128)(2,1)S(1)}, f32[1024,256]{1,0:T(8,128)S(1)}) custom-call(s32[3]{0:T(128)S(1)} %pad_add_fusion.place_ref, f32[2048,128]{1,0:T(8,128)S(1)} %get-tuple-element.61.rows_mine, f32[2048,128]{1,0:T(8,128)S(1)} %collective-permute-done.9.rows_other, f32[512,512]{1,0:T(8,128)S(1)} %corner_end.1.inverse_ref), custom_call_target="tpu_custom_call" | custom-call | flops 1000 | bytes 1000 | tf_op jit(solution)/shard_map/row_weights/pallas_call | solution.py:315
  82.1 1.0 copy-done.2
  83.0 0.1 collective-permute-done.11
  83.1 1.0 copy-done.4
  84.1 1.0 copy-done.6
  85.1 0.9 slice_select_fusion.rest_1_
  86.0 1.5 %collective-permute-start.17 = (f32[1024,128]{1,0:T(8,128)}, f32[1024,128]{1,0:T(8,128)}, u32[]{:S(2)}, u32[]{:S(2)}) collective-permute-start(f32[1024,128]{1,0:T(8,128)} %slice_select_fusion.rest_1_), channel_id=1, source_target_pairs={{9,12},{12,9},{17,20},{19,22},{20,17},{22,19},{25,28},{27,30},{28,... | collective-permute-start | bytes 1572872 | tf_op jit(solution)/shard_map/ppermute | solution.py:454
  87.4 1.7 %collective-permute-start.16 = (f32[1024,128]{1,0:T(8,128)}, f32[1024,128]{1,0:T(8,128)}, u32[]{:S(2)}, u32[]{:S(2)}) collective-permute-start(f32[1024,128]{1,0:T(8,128)} %slice_select_fusion.rest_1_), channel_id=1, source_target_pairs={{0,4},{1,5},{2,6},{3,7},{4,0},{5,1},{6,2},{7,3},{8,12},{9,8},{10,1... | collective-permute-start | bytes 1572872 | tf_op jit(solution)/shard_map/ppermute | solution.py:454
  89.1 0.1 stack.47.place_ref
  89.2 1.2 %copy-done.1 = f32[2048,128]{1,0:T(8,128)S(1)} copy-done((f32[2048,128]{1,0:T(8,128)S(1)}, f32[2048,128]{1,0:T(8,128)}, u32[]{:S(2)}) %copy-start.1) | copy-done | bytes 1048600
  90.5 1.2 %copy-done.5 = f32[2048,128]{1,0:T(8,128)S(1)} copy-done((f32[2048,128]{1,0:T(8,128)S(1)}, f32[2048,128]{1,0:T(8,128)}, u32[]{:S(2)}) %copy-start.5) | copy-done | bytes 1048600
  91.7 1.2 %copy-done.7 = f32[2048,128]{1,0:T(8,128)S(1)} copy-done((f32[2048,128]{1,0:T(8,128)S(1)}, f32[2048,128]{1,0:T(8,128)}, u32[]{:S(2)}) %copy-start.7) | copy-done | bytes 1048600
  92.9 5.3 %first_products.1.ready_ref = f32[1024,1024]{1,0:T(8,128)S(1)} custom-call(s32[7]{0:T(128)S(1)} %stack.47.place_ref, bf16[1024,1536]{1,0:T(8,128)(2,1)S(1)} %get-tuple-element.52.weights_ref, f32[2048,128]{1,0:T(8,128)S(1)} %copy-done.1, f32[2048,128]{1,0:T(8,128)S(1)} %copy-done.7, f32[2048,128]{1,0:T(8,128)S(1)} %copy-done.5), custom_call_target="tpu_custom_call" | custom-call | flops 1000 | bytes 1000 | tf_op jit(solution)/shard_map/first_products/pallas_call | solution.py:364
  98.3 7.4 %trailing_0.1.rest_0_ = f32[1024,2,8,128]{3,2,1,0:T(8,128)} custom-call(s32[7]{0:T(128)S(1)} %stack.47.place_ref, f32[1024,2,8,128]{3,2,1,0:T(8,128)} %bitcast.16, bf16[1024,1536]{1,0:T(8,128)(2,1)S(1)} %get-tuple-element.52.weights_ref, f32[1024,1024]{1,0:T(8,128)S(1)} %first_products.1.ready_ref, f32[1024,256]{1,0:T(8,128)S(1)} %copy-done.3, ...), custom_call_target="tpu_custom_call" | custom-call | flops 1000 | bytes 1000 | tf_op jit(solution)/shard_map/trailing_0/pallas_call | solution.py:424
  105.7 7.2 %trailing_1.1 = f32[1024,2,8,128]{3,2,1,0:T(8,128)} custom-call(s32[7]{0:T(128)S(1)} %stack.47.place_ref, f32[1024,2,8,128]{3,2,1,0:T(8,128)} %bitcast.17, bf16[1024,1536]{1,0:T(8,128)(2,1)S(1)} %get-tuple-element.52.weights_ref, f32[1024,1024]{1,0:T(8,128)S(1)} %first_products.1.ready_ref, ...), custom_call_target="tpu_custom_call", output_to_operand_aliasing={{}: (4, {})} | custom-call | flops 1000 | bytes 1000 | tf_op jit(solution)/shard_map/trailing_1/pallas_call | solution.py:424
  (32 shorter events, 0.2 us)
Async XLA Ops:
  2.1 9.9 %collective-permute-start = (f32[512,128]{1,0:T(8,128)}, f32[512,128]{1,0:T(8,128)S(1)}, u32[]{:S(2)}, u32[]{:S(2)}) collective-permute-start(f32[512,128]{1,0:T(8,128)} %gather_lead.1.lead_ref), channel_id=1, source_target_pairs={{0,2},{1,3},{4,6},{5,7},{8,10},{9,11},{12,14},{13,15},{16,18},{17,... | collective-permute-start | bytes 786440 | tf_op jit(solution)/shard_map/ppermute | solution.py:454
  5.5 6.4 %copy-start.9 = (f32[512,128]{1,0:T(8,128)S(1)}, f32[512,128]{1,0:T(8,128)}, u32[]{:S(2)}) copy-start(f32[512,128]{1,0:T(8,128)} %gather_lead.1.lead_ref) | copy-start | bytes 786436
  12.0 7.8 %collective-permute-start.1 = (f32[256,128]{1,0:T(8,128)S(1)}, f32[256,128]{1,0:T(8,128)S(1)}, u32[]{:S(2)}, u32[]{:S(2)}) collective-permute-start(f32[256,128]{1,0:T(8,128)S(1)} %slice_select_fusion.2), channel_id=1, source_target_pairs={{0,16},{1,17},{2,18},{3,19},{4,20},{5,21},{6,22},{7,23}} | collective-permute-start | bytes 393224 | tf_op jit(solution)/shard_map/ppermute | solution.py:454
  19.8 3.8 %collective-permute-start.2 = (f32[256,128]{1,0:T(8,128)S(1)}, f32[256,128]{1,0:T(8,128)S(1)}, u32[]{:S(2)}, u32[]{:S(2)}) collective-permute-start(f32[256,128]{1,0:T(8,128)S(1)} %broadcast_select_fusion.1), channel_id=1, source_target_pairs={{0,8},{1,9},{2,10},{3,11},{4,12},{5,13},{6,14},{7,15},{16,24},{17,... | collective-permute-start | bytes 393224 | tf_op jit(solution)/shard_map/ppermute | solution.py:454
  23.6 25.5 %collective-permute-start.7 = (f32[2048,128]{1,0:T(8,128)}, f32[2048,128]{1,0:T(8,128)S(1)}, u32[]{:S(2)}, u32[]{:S(2)}) collective-permute-start(f32[2048,128]{1,0:T(8,128)} %get-tuple-element.36), channel_id=1, source_target_pairs={{0,24},{1,25},{2,18},{3,19},{4,28},{5,29},{6,22},{7,23},{16,8},{17... | collective-permute-start | bytes 3145736 | tf_op jit(solution)/shard_map/ppermute | solution.py:454
  26.1 5.9 %collective-permute-start.5 = (f32[256,128]{1,0:T(8,128)S(1)}, f32[256,128]{1,0:T(8,128)S(1)}, u32[]{:S(2)}, u32[]{:S(2)}) collective-permute-start(f32[256,128]{1,0:T(8,128)S(1)} %broadcast_select_fusion.2), channel_id=1, source_target_pairs={{0,6},{1,7},{2,4},{3,5},{4,2},{5,3},{6,0},{7,1},{8,14},{9,15},{10,... | collective-permute-start | bytes 393224 | tf_op jit(solution)/shard_map/ppermute | solution.py:454
  27.8 6.9 %collective-permute-start.3 = (f32[256,128]{1,0:T(8,128)S(1)}, f32[256,128]{1,0:T(8,128)S(1)}, u32[]{:S(2)}, u32[]{:S(2)}) collective-permute-start(f32[256,128]{1,0:T(8,128)S(1)} %broadcast_select_fusion.2), channel_id=1, source_target_pairs={{0,4},{1,5},{2,6},{3,7},{4,0},{5,1},{6,2},{7,3},{8,12},{9,13},{10,... | collective-permute-start | bytes 393224 | tf_op jit(solution)/shard_map/ppermute | solution.py:454
  28.3 6.4 %collective-permute-start.4 = (f32[256,128]{1,0:T(8,128)S(1)}, f32[256,128]{1,0:T(8,128)S(1)}, u32[]{:S(2)}, u32[]{:S(2)}) collective-permute-start(f32[256,128]{1,0:T(8,128)S(1)} %broadcast_select_fusion.2), channel_id=1, source_target_pairs={{0,2},{1,3},{2,0},{3,1},{4,6},{5,7},{6,4},{7,5},{8,10},{9,11},{10,... | collective-permute-start | bytes 393224 | tf_op jit(solution)/shard_map/ppermute | solution.py:454
  32.1 17.1 %collective-permute-start.8 = (f32[1536,128]{1,0:T(8,128)}, f32[1536,128]{1,0:T(8,128)S(1)}, u32[]{:S(2)}, u32[]{:S(2)}) collective-permute-start(f32[1536,128]{1,0:T(8,128)} %get-tuple-element.40), channel_id=1, source_target_pairs={{0,2},{1,3},{4,6},{5,7},{8,10},{9,11},{12,14},{13,15},{16,18},{17,... | collective-permute-start | bytes 2359304 | tf_op jit(solution)/shard_map/ppermute | solution.py:454
  34.7 2.0 %collective-permute-start.6 = (f32[1024,128]{1,0:T(8,128)S(1)}, f32[1024,128]{1,0:T(8,128)S(1)}, u32[]{:S(2)}, u32[]{:S(2)}) collective-permute-start(f32[1024,128]{1,0:T(8,128)S(1)} %constant_dynamic-update-slice_fusion.mine_ref), channel_id=1, source_target_pairs={{0,1},{1,0},{2,3},{3,2},{4,5},{5,4},{6,7},{7,6},{8,9},{9,8},{10,11... | collective-permute-start | bytes 1572872 | tf_op jit(solution)/shard_map/ppermute | solution.py:454
  34.9 38.2 %copy-start.8 = (f32[2048,128]{1,0:T(8,128)S(1)}, f32[2048,128]{1,0:T(8,128)}, u32[]{:S(2)}) copy-start(f32[2048,128]{1,0:T(8,128)} %get-tuple-element.45) | copy-start | bytes 3145732
  50.7 31.3 %copy-start = (f32[2048,128]{1,0:T(8,128)}, f32[2048,128]{1,0:T(8,128)S(1)}, u32[]{:S(2)}) copy-start(f32[2048,128]{1,0:T(8,128)S(1)} %get-tuple-element.53.piece_a) | copy-start | bytes 3145732
  50.8 24.6 %collective-permute-start.9 = (f32[2048,128]{1,0:T(8,128)S(1)}, f32[2048,128]{1,0:T(8,128)S(1)}, u32[]{:S(2)}, u32[]{:S(2)}) collective-permute-start(f32[2048,128]{1,0:T(8,128)S(1)} %get-tuple-element.61.rows_mine), channel_id=1, source_target_pairs={{0,1},{1,0},{2,3},{3,2},{4,5},{5,4},{6,7},{7,6},{8,9},{9,8},{10,11... | collective-permute-start | bytes 3145736 | tf_op jit(solution)/shard_map/ppermute | solution.py:454
  50.9 32.2 %collective-permute-start.13 = (f32[2048,128]{1,0:T(8,128)S(1)}, f32[2048,128]{1,0:T(8,128)S(1)}, u32[]{:S(2)}, u32[]{:S(2)}) collective-permute-start(f32[2048,128]{1,0:T(8,128)S(1)} %get-tuple-element.53.piece_a), channel_id=1, source_target_pairs={{9,12},{11,14},{12,9},{14,11},{17,20},{20,17},{25,28},{27,30},{28,... | collective-permute-start | bytes 3145736 | tf_op jit(solution)/shard_map/ppermute | solution.py:454
  51.6 32.5 %collective-permute-start.12 = (f32[2048,128]{1,0:T(8,128)S(1)}, f32[2048,128]{1,0:T(8,128)S(1)}, u32[]{:S(2)}, u32[]{:S(2)}) collective-permute-start(f32[2048,128]{1,0:T(8,128)S(1)} %get-tuple-element.53.piece_a), channel_id=1, source_target_pairs={{0,4},{1,5},{2,6},{3,7},{4,0},{5,1},{6,2},{7,3},{8,12},{9,8},{10,1... | collective-permute-start | bytes 3145736 | tf_op jit(solution)/shard_map/ppermute | solution.py:454
  55.0 18.1 %collective-permute-start.10 = (f32[1024,128]{1,0:T(8,128)S(1)}, f32[1024,128]{1,0:T(8,128)S(1)}, u32[]{:S(2)}, u32[]{:S(2)}) collective-permute-start(f32[1024,128]{1,0:T(8,128)S(1)} %get-tuple-element.47), channel_id=1, source_target_pairs={{0,8},{1,9},{2,10},{3,11},{4,12},{5,13},{6,14},{7,15},{10,26},{11,... | collective-permute-start | bytes 1572872 | tf_op jit(solution)/shard_map/ppermute | solution.py:454
  60.3 22.8 %collective-permute-start.11 = (f32[1024,128]{1,0:T(8,128)S(1)}, f32[1024,128]{1,0:T(8,128)S(1)}, u32[]{:S(2)}, u32[]{:S(2)}) collective-permute-start(f32[1024,128]{1,0:T(8,128)S(1)} %get-tuple-element.50), channel_id=1, source_target_pairs={{0,8},{1,9},{2,10},{3,11},{4,12},{5,13},{6,14},{7,15},{10,26},{11,... | collective-permute-start | bytes 1572872 | tf_op jit(solution)/shard_map/ppermute | solution.py:454
  74.0 24.3 %collective-permute-start.15 = (f32[1024,128]{1,0:T(8,128)}, f32[1024,128]{1,0:T(8,128)}, u32[]{:S(2)}, u32[]{:S(2)}) collective-permute-start(f32[1024,128]{1,0:T(8,128)} %slice_select_fusion.1.rest_1_), channel_id=1, source_target_pairs={{9,12},{12,9},{17,20},{19,22},{20,17},{22,19},{25,28},{27,30},{28,... | collective-permute-start | bytes 1572872 | tf_op jit(solution)/shard_map/ppermute | solution.py:454
  75.4 22.8 %collective-permute-start.14 = (f32[1024,128]{1,0:T(8,128)}, f32[1024,128]{1,0:T(8,128)}, u32[]{:S(2)}, u32[]{:S(2)}) collective-permute-start(f32[1024,128]{1,0:T(8,128)} %slice_select_fusion.1.rest_1_), channel_id=1, source_target_pairs={{0,4},{1,5},{2,6},{3,7},{4,0},{5,1},{6,2},{7,3},{8,12},{9,8},{10,1... | collective-permute-start | bytes 1572872 | tf_op jit(solution)/shard_map/ppermute | solution.py:454
  82.1 1.0 copy-start.2
  83.1 1.0 copy-start.4
  84.1 1.0 copy-start.6
  86.0 19.8 %collective-permute-start.17 = (f32[1024,128]{1,0:T(8,128)}, f32[1024,128]{1,0:T(8,128)}, u32[]{:S(2)}, u32[]{:S(2)}) collective-permute-start(f32[1024,128]{1,0:T(8,128)} %slice_select_fusion.rest_1_), channel_id=1, source_target_pairs={{9,12},{12,9},{17,20},{19,22},{20,17},{22,19},{25,28},{27,30},{28,... | collective-permute-start | bytes 1572872 | tf_op jit(solution)/shard_map/ppermute | solution.py:454
  87.4 18.3 %collective-permute-start.16 = (f32[1024,128]{1,0:T(8,128)}, f32[1024,128]{1,0:T(8,128)}, u32[]{:S(2)}, u32[]{:S(2)}) collective-permute-start(f32[1024,128]{1,0:T(8,128)} %slice_select_fusion.rest_1_), channel_id=1, source_target_pairs={{0,4},{1,5},{2,6},{3,7},{4,0},{5,1},{6,2},{7,3},{8,12},{9,8},{10,1... | collective-permute-start | bytes 1572872 | tf_op jit(solution)/shard_map/ppermute | solution.py:454
  89.2 1.2 %copy-start.1 = (f32[2048,128]{1,0:T(8,128)S(1)}, f32[2048,128]{1,0:T(8,128)}, u32[]{:S(2)}) copy-start(f32[2048,128]{1,0:T(8,128)} %copy-done) | copy-start | bytes 3145732
  90.5 1.2 %copy-start.5 = (f32[2048,128]{1,0:T(8,128)S(1)}, f32[2048,128]{1,0:T(8,128)}, u32[]{:S(2)}) copy-start(f32[2048,128]{1,0:T(8,128)} %copy-done.4) | copy-start | bytes 3145732
  91.7 1.2 %copy-start.7 = (f32[2048,128]{1,0:T(8,128)S(1)}, f32[2048,128]{1,0:T(8,128)}, u32[]{:S(2)}) copy-start(f32[2048,128]{1,0:T(8,128)} %copy-done.6) | copy-start | bytes 3145732
  92.9 5.4 %copy-start.3 = (f32[1024,256]{1,0:T(8,128)S(1)}, f32[1024,256]{1,0:T(8,128)}, u32[]{:S(2)}) copy-start(f32[1024,256]{1,0:T(8,128)} %copy-done.2) | copy-start | bytes 3145732
